TPU v7x, 32 devices: a whole 2x2x4 slice. The times are simulated.
32 devices in a mesh: grp: 2 (over y), blk: 4 (over x, core), dep: 4 (over z).
Axes of the slice: x: 2, y: 2, z: 4, core: 2. Of those that a mesh axis runs over, the one named last changes fastest.
Arguments:
- velocity: float32 [3, 1024, 32, 64], P(None, 'blk', 'dep', 'grp'), may hold values from -6 to 6
- scalar: float32 [32, 64, 8192], P('dep', 'grp', 'blk'), may hold values from -6 to 6
- spline_base: int32 [8192], P('blk'), may hold values from -1 to 1023, as said below
- spline_frac: float32 [8192], P('blk'), may hold values from 0 to 1
Outputs:
- segment_velocity: float32 [3, 1024, 32, 64], P(None, 'blk', 'dep', 'grp')
- scalar_segment: float32 [32, 64, 8192], P('dep', 'grp', 'blk')
Inputs may be any that keep to these rules, and one draw needn't show every extreme that they name: spline_base[i] is i // 8 or i // 8 - 1; the spline reads velocity cells spline_base[i] - 1 to spline_base[i] + 2 modulo 1024.
All inputs are finite; a program needn't handle non-finite values.
Results may differ from a plain program's by a relative error of at most 0.00007.
Values sent between devices are 32-bit elements; how exact they have to be, the bound alone decides.
No kernel may reach another device: no remote copies, remote signals or barrier semaphores. Data moves between devices by JAX's collectives and lax.ppermute only.
A program may use at most 64 MiB of HBM per device.

v0:
```python
import math

import jax
import jax.numpy as jnp
from jax import lax
from jax.sharding import PartitionSpec as P

velocity_step = 0.002
viscosity = 0.00125
advect_rate = 0.2
diffuse_rate = 0.05
first_coeffs = (1.0 / 280.0, -4.0 / 105.0, 0.2, -0.8, 0.0, 0.8, -0.2, 4.0 / 105.0, -1.0 / 280.0)
second_coeffs = (
    -1.0 / 560.0,
    8.0 / 315.0,
    -0.2,
    1.6,
    -205.0 / 72.0,
    1.6,
    -0.2,
    8.0 / 315.0,
    -1.0 / 560.0,
)
highest = lax.Precision.HIGHEST


def padded_2(block, sides, width):
    for axis, dim in sides:
        count = lax.axis_size(axis)
        forward = [(i, i + 1) for i in range(count - 1)]
        forward.append((count - 1, 0))
        backward = [(target, source) for source, target in forward]
        low = lax.ppermute(
            lax.slice_in_dim(block, block.shape[dim] - width, None, axis=dim), axis, forward
        )
        high = lax.ppermute(lax.slice_in_dim(block, 0, width, axis=dim), axis, backward)
        block = jnp.concatenate([low, block, high], axis=dim)
    return block


def derivative_rows(first_row, count, length):
    rows = first_row + lax.iota(jnp.int32, count)
    columns = lax.iota(jnp.int32, length)
    offset = (rows[:, None] - columns[None, :]) % length
    signed = jnp.where(offset > length // 2, offset - length, offset)
    angle = signed.astype(jnp.float32) * (math.pi / length)
    parity = 1.0 - 2.0 * (offset % 2).astype(jnp.float32)
    same = offset == 0
    sine = jnp.where(same, 1.0, jnp.sin(angle))
    first = jnp.where(same, 0.0, 0.5 * parity * jnp.cos(angle) / sine)
    second = jnp.where(same, -(length * length) / 12.0 - 1.0 / 6.0, -0.5 * parity / (sine * sine))
    average = jnp.full((count, length), 1.0 / length, jnp.float32)
    return jnp.concatenate([first, second, average], axis=0)


def catmull_weights(fraction):
    square = fraction * fraction
    cube = square * fraction
    return (
        (-cube + 2.0 * square - fraction) * 0.5,
        (3.0 * cube - 5.0 * square + 2.0) * 0.5,
        (-3.0 * cube + 4.0 * square + fraction) * 0.5,
        (cube - square) * 0.5,
    )


def scalar_update(padded, fine):
    extent = (padded.shape[0] - 8, padded.shape[1] - 8, padded.shape[2] - 8)
    centre = lax.slice(padded, (4, 4, 4), (4 + extent[0], 4 + extent[1], 4 + extent[2]))
    gradients = []
    curvature = jnp.zeros(extent, jnp.float32)
    for axis_index in range(3):
        slope = jnp.zeros(extent, jnp.float32)
        for offset in range(9):
            begin = [4, 4, 4]
            begin[axis_index] = offset
            finish = (begin[0] + extent[0], begin[1] + extent[1], begin[2] + extent[2])
            window = lax.slice(padded, tuple(begin), finish)
            if first_coeffs[offset] != 0.0:
                slope = slope + first_coeffs[offset] * window
            curvature = curvature + second_coeffs[offset] * window
        gradients.append(slope)
    advection = fine[2] * gradients[0] + fine[1] * gradients[1] + fine[0] * gradients[2]
    return centre - advect_rate * advection + diffuse_rate * curvature


def per_device(velocity, scalar, spline_base, spline_frac):
    cells = velocity.shape[1]
    length = cells * lax.axis_size("blk")
    block = lax.axis_index("blk")
    table = derivative_rows(block * cells, cells, length)
    both = jnp.einsum(
        "km,cmzy->ckzy",
        table,
        lax.all_gather(velocity, "blk", axis=1, tiled=True),
        precision=highest,
    )
    segment = (
        velocity
        - both[:, 2 * cells :]
        + velocity_step * (viscosity * both[:, cells : 2 * cells] - velocity[0:1] * both[:, :cells])
    )
    widened = padded_2(segment, (("blk", 1),), 2)
    weights = catmull_weights(spline_frac)
    local_base = spline_base - (block * cells - 2)
    slots = lax.iota(jnp.int32, cells + 4)[:, None]
    matrix = jnp.zeros((cells + 4, spline_base.shape[0]), jnp.float32)
    for tap_index in range(4):
        matrix = matrix + jnp.where(
            slots == (local_base + (tap_index - 1))[None, :], weights[tap_index][None, :], 0.0
        )
    fine = jnp.einsum("cxzy,xi->czyi", widened, matrix, precision=highest)
    padded = padded_2(scalar, (("grp", 1), ("blk", 2), ("dep", 0)), 4)
    return (segment, scalar_update(padded, fine))


def solution(mesh):
    in_specs = (P(None, "blk", "dep", "grp"), P("dep", "grp", "blk"), P("blk"), P("blk"))
    out_specs = (P(None, "blk", "dep", "grp"), P("dep", "grp", "blk"))
    return jax.shard_map(
        per_device, mesh=mesh, in_specs=in_specs, out_specs=out_specs, check_vma=False
    )
```

profile of v0, /device:TPU:0, one launch (start us, length us, event | category | flops | bytes accessed | tf_op | source)
XLA Modules:
  0.0 140.2 jit_solution(3180653445395689317)
XLA Ops:
  7.2 0.0 copy-start.3
  7.2 0.0 all-gather.2.cloned.1.call-start
  7.2 0.7 all-gather.2.cloned.1.call-update
  7.9 2.1 %fusion.86 = (f32[8,4,2048]{2,1,0:T(4,128)}, f32[8,4,2048]{2,1,0:T(4,128)}) fusion(f32[8,32,2048]{2,1,0:T(8,128)} %param.5), kind=kLoop, calls=%fused_computation.147 | loop fusion | bytes 1048576 | tf_op jit(solution)/shard_map/slice | solution.py:34
  10.0 3.0 %collective-permute-start.2 = (f32[8,4,2048]{2,1,0:T(4,128)}, f32[8,4,2048]{2,1,0:T(4,128)}, u32[]{:S(2)}, u32[]{:S(2)}) collective-permute-start(f32[8,4,2048]{2,1,0:T(4,128)} %get-tuple-element.10), channel_id=1, source_target_pairs={{0,16},{16,0},{1,17},{17,1},{2,18},{18,2},{3,19},{19,3},{4,20},{20... | collective-permute-start | bytes 786440 | tf_op jit(solution)/shard_map/ppermute | solution.py:33
  13.0 0.0 collective-permute-start.3
  13.0 0.8 broadcast_add_fusion.2
  13.9 0.7 fusion.73
  14.6 0.0 copy-done.3
  14.6 0.7 slice_bitcast_fusion.3
  15.3 6.6 %divide_select_fusion.1 = (f32[256,1024]{1,0:T(8,128)}, f32[256,1024]{1,0:T(8,128)}) fusion(s32[256]{0:T(256)S(1)} %iota_add_fusion), kind=kLoop, calls=%fused_computation.104 | loop fusion | flops 10747904 | bytes 2098176 | tf_op jit(solution)/shard_map/jit(_where)/select_n | solution.py:50
  21.9 0.0 copy-done
  21.9 0.1 constant_dynamic-update-slice_fusion.1
  22.1 0.0 collective-permute-done.2
  22.1 3.1 %collective-permute-done.3 = f32[8,4,2048]{2,1,0:T(4,128)} collective-permute-done((f32[8,4,2048]{2,1,0:T(4,128)}, f32[8,4,2048]{2,1,0:T(4,128)}, u32[]{:S(2)}, u32[]{:S(2)}) %collective-permute-start.3) | collective-permute-done | bytes 262176 | tf_op jit(solution)/shard_map/ppermute | solution.py:36
  25.2 1.5 %pad_maximum_fusion.1 = f32[8,40,2048]{2,1,0:T(8,128)S(1)} fusion(f32[8,4,2048]{2,1,0:T(4,128)} %collective-permute-done.3, f32[8,32,2048]{2,1,0:T(8,128)S(1)} %copy-done, f32[8,4,2048]{2,1,0:T(4,128)} %collective-permute-done.2), kind=kLoop, calls=%fused_computation.26 | loop fusion | flops 1310720 | bytes 5242880 | tf_op jit(solution)/shard_map/concatenate | solution.py:37
  26.8 0.0 copy-start.2
  26.8 0.1 fusion.85
  26.9 0.1 collective-permute-start.4
  26.9 1.7 %collective-permute-start.5 = (f32[8,40,4]{2,1,0:T(8,128)S(1)}, f32[8,40,4]{2,1,0:T(8,128)}, u32[]{:S(2)}, u32[]{:S(2)}) collective-permute-start(f32[8,40,4]{2,1,0:T(8,128)S(1)} %get-tuple-element.9), channel_id=1, source_target_pairs={{4,0},{8,4},{12,8},{0,12},{5,1},{9,5},{13,9},{1,13},{6,2},{10,6},{... | collective-permute-start | bytes 15368 | tf_op jit(solution)/shard_map/ppermute | solution.py:36
  28.7 1.0 constant_dynamic-update-slice_fusion
  29.7 0.0 copy-done.2
  29.7 6.5 %collective-permute-done.4 = f32[8,40,4]{2,1,0:T(8,128)S(1)} collective-permute-done((f32[8,40,4]{2,1,0:T(8,128)S(1)}, f32[8,40,4]{2,1,0:T(8,128)S(1)}, u32[]{:S(2)}, u32[]{:S(2)}) %collective-permute-start.4) | collective-permute-done | bytes 5152 | tf_op jit(solution)/shard_map/ppermute | solution.py:33
  36.2 0.7 copy-done.6
  36.9 0.0 collective-permute-done.5
  36.9 4.7 %concatenate.52 = f32[8,40,2056]{2,1,0:T(8,128)} concatenate(f32[8,40,4]{2,1,0:T(8,128)} %copy-done.6, f32[8,40,2048]{2,1,0:T(8,128)} %copy-done.2, f32[8,40,4]{2,1,0:T(8,128)} %collective-permute-done.5), dimensions={2} | concatenate | bytes 5263360 | tf_op jit(solution)/shard_map/concatenate | solution.py:37
  41.6 3.6 %fusion.84 = (f32[4,40,2056]{2,1,0:T(8,128)}, f32[4,40,2056]{2,1,0:T(8,128)}) fusion(f32[8,40,2056]{2,1,0:T(8,128)} %concatenate.52), kind=kLoop, calls=%fused_computation.145 | loop fusion | bytes 5263360 | tf_op jit(solution)/shard_map/slice | solution.py:34
  45.1 1.8 %collective-permute-start.6 = (f32[4,40,2056]{2,1,0:T(8,128)}, f32[4,40,2056]{2,1,0:T(8,128)}, u32[]{:S(2)}, u32[]{:S(2)}) collective-permute-start(f32[4,40,2056]{2,1,0:T(8,128)} %get-tuple-element.4), channel_id=1, source_target_pairs={{0,1},{1,2},{2,3},{3,0},{4,5},{5,6},{6,7},{7,4},{8,9},{9,10},{10,1... | collective-permute-start | bytes 3947528 | tf_op jit(solution)/shard_map/ppermute | solution.py:33
  47.0 2.0 %collective-permute-start.7 = (f32[4,40,2056]{2,1,0:T(8,128)}, f32[4,40,2056]{2,1,0:T(8,128)}, u32[]{:S(2)}, u32[]{:S(2)}) collective-permute-start(f32[4,40,2056]{2,1,0:T(8,128)} %get-tuple-element.5), channel_id=1, source_target_pairs={{1,0},{2,1},{3,2},{0,3},{5,4},{6,5},{7,6},{4,7},{9,8},{10,9},{11,1... | collective-permute-start | bytes 3947528 | tf_op jit(solution)/shard_map/ppermute | solution.py:36
  49.0 10.4 %fusion = f32[768,768]{0,1:S(1)} fusion(f32[1024,768]{0,1:T(8,128)} %bitcast.41, f32[256,1024]{1,0:T(8,128)} %get-tuple-element.21, f32[256,1024]{1,0:T(8,128)} %get-tuple-element.20, f32[768]{0:T(1024)S(1)} %pad.22.clone), kind=kOutput, calls=%fused_computation.15 | convolution fusion | flops 7249330176 | bytes 7605248
  59.4 0.0 copy-done.5
  59.4 0.0 copy-start.1
  59.4 0.0 copy-start.7
  59.5 0.3 fusion.67
  59.7 0.0 copy-start.4
  59.7 0.2 fusion.87
  59.9 1.1 collective-permute-start
  61.1 0.7 collective-permute-start.1
  61.7 0.0 copy-done.1
  61.7 0.0 copy-done.7
  61.7 2.6 %maximum_maximum_fusion = (f32[8,40,2052]{2,1,0:T(8,128)S(1)}, f32[8,40,2052]{2,1,0:T(8,128)S(1)}) fusion(f32[8,4,2048]{2,1,0:T(4,128)} %collective-permute-done.3, f32[8,32,2048]{2,1,0:T(8,128)S(1)} %copy-done.1, f32[8,4,2048]{2,1,0:T(4,128)} %collective-permute-done.2, f32[8,40,4]{2,1,0:T(8,128)S(1)} %copy-done.7, f32[8,40,4]{2,1,0:T(8,128)} %collective-permute-done.5), kind=kLoop, calls=%fused_computation.24 | loop fusion | flops 3939840 | bytes 7884800 | tf_op jit(solution)/shard_map/concatenate | solution.py:37
  64.4 4.5 %collective-permute-done = f32[3,2,8,32]{1,3,2,0:T(8,128)S(1)} collective-permute-done((f32[3,2,8,32]{1,3,2,0:T(8,128)S(1)}, f32[3,2,8,32]{1,3,2,0:T(8,128)S(1)}, u32[]{:S(2)}, u32[]{:S(2)}) %collective-permute-start) | collective-permute-done | bytes 6176 | tf_op jit(solution)/shard_map/ppermute | solution.py:33
  68.9 2.1 %collective-permute-done.1 = f32[3,2,8,32]{1,3,2,0:T(8,128)S(1)} collective-permute-done((f32[3,2,8,32]{1,3,2,0:T(8,128)S(1)}, f32[3,2,8,32]{1,3,2,0:T(8,128)S(1)}, u32[]{:S(2)}, u32[]{:S(2)}) %collective-permute-start.1) | collective-permute-done | bytes 6176 | tf_op jit(solution)/shard_map/ppermute | solution.py:36
  71.0 0.0 copy-done.4
  71.0 13.0 %fusion.5 = f32[3,8,32,2048]{3,2,1,0:T(8,128)} fusion(f32[3,2,8,32]{1,3,2,0:T(8,128)S(1)} %collective-permute-done.1, f32[3,256,8,32]{1,3,2,0:T(8,128)S(1)} %fusion.67, f32[3,2,8,32]{1,3,2,0:T(8,128)S(1)} %collective-permute-done, f32[2048]{0:T(1024)S(1)} %get-tuple-element.16, s32[2048]{0:T(1024)S(1)} %get-tuple-element.19, ...), kind=kOutput, calls=%fused_computation.27 | convolution fusion | flops 4913592320 | bytes 7155712 | tf_op jit(solution)/shard_map/cxzy,xi->czyi/dot_general | solution.py:112
  84.1 0.0 collective-permute-done.6
  84.1 26.4 %collective-permute-done.7 = f32[4,40,2056]{2,1,0:T(8,128)} collective-permute-done((f32[4,40,2056]{2,1,0:T(8,128)}, f32[4,40,2056]{2,1,0:T(8,128)}, u32[]{:S(2)}, u32[]{:S(2)}) %collective-permute-start.7) | collective-permute-done | bytes 1315872 | tf_op jit(solution)/shard_map/ppermute | solution.py:36
  110.4 22.9 %fusion.28 = f32[8,32,2048]{2,1,0:T(8,128)} fusion(f32[8,32,2048]{2,1,0:T(8,128)} %param.5, f32[3,8,32,2048]{3,2,1,0:T(8,128)} %fusion.5, f32[8,40,2052]{2,1,0:T(8,128)S(1)} %get-tuple-element.7, f32[8,40,2052]{2,1,0:T(8,128)S(1)} %get-tuple-element.6, f32[8,36,2048]{2,1,0:T(8,128)S(1)} %constant_dynamic-update-slice_fusion, ...), kind=kLoop, calls=%fused_computation.56 | loop fusion | flops 59768832 | bytes 41177088 | tf_op jit(solution)/shard_map/add | solution.py:84
  (8 shorter events, 0.0 us)
Async XLA Ops:
  7.2 7.4 %copy-start.3 = (f32[3,256,8,32]{1,3,2,0:T(8,128)S(1)}, f32[3,256,8,32]{1,3,2,0:T(8,128)}, u32[]{:S(2)}) copy-start(f32[3,256,8,32]{1,3,2,0:T(8,128)} %param.4) | copy-start | bytes 2359300
  7.2 41.8 %all-gather.2.cloned.1.call-start = ((), (), s32[]{:S(2)}) async-start(), calls=%async_computation | async-start | bytes 3932160 | tf_op jit(solution)/shard_map/all_gather | solution.py:95
  10.0 12.1 %collective-permute-start.2 = (f32[8,4,2048]{2,1,0:T(4,128)}, f32[8,4,2048]{2,1,0:T(4,128)}, u32[]{:S(2)}, u32[]{:S(2)}) collective-permute-start(f32[8,4,2048]{2,1,0:T(4,128)} %get-tuple-element.10), channel_id=1, source_target_pairs={{0,16},{16,0},{1,17},{17,1},{2,18},{18,2},{3,19},{19,3},{4,20},{20... | collective-permute-start | bytes 786440 | tf_op jit(solution)/shard_map/ppermute | solution.py:33
  13.0 12.2 %collective-permute-start.3 = (f32[8,4,2048]{2,1,0:T(4,128)}, f32[8,4,2048]{2,1,0:T(4,128)}, u32[]{:S(2)}, u32[]{:S(2)}) collective-permute-start(f32[8,4,2048]{2,1,0:T(4,128)} %get-tuple-element.11), channel_id=1, source_target_pairs={{16,0},{0,16},{17,1},{1,17},{18,2},{2,18},{19,3},{3,19},{20,4},{4,... | collective-permute-start | bytes 786440 | tf_op jit(solution)/shard_map/ppermute | solution.py:36
  13.0 8.9 %copy-start = (f32[8,32,2048]{2,1,0:T(8,128)S(1)}, f32[8,32,2048]{2,1,0:T(8,128)}, u32[]{:S(2)}) copy-start(f32[8,32,2048]{2,1,0:T(8,128)} %param.5) | copy-start | bytes 6291460
  26.8 2.9 %copy-start.2 = (f32[8,40,2048]{2,1,0:T(8,128)}, f32[8,40,2048]{2,1,0:T(8,128)S(1)}, u32[]{:S(2)}) copy-start(f32[8,40,2048]{2,1,0:T(8,128)S(1)} %pad_maximum_fusion.1) | copy-start | bytes 7864324
  26.9 9.4 %collective-permute-start.4 = (f32[8,40,4]{2,1,0:T(8,128)S(1)}, f32[8,40,4]{2,1,0:T(8,128)S(1)}, u32[]{:S(2)}, u32[]{:S(2)}) collective-permute-start(f32[8,40,4]{2,1,0:T(8,128)S(1)} %get-tuple-element.8), channel_id=1, source_target_pairs={{0,4},{4,8},{8,12},{12,0},{1,5},{5,9},{9,13},{13,1},{2,6},{6,10},{... | collective-permute-start | bytes 15368 | tf_op jit(solution)/shard_map/ppermute | solution.py:33
  26.9 10.0 %collective-permute-start.5 = (f32[8,40,4]{2,1,0:T(8,128)S(1)}, f32[8,40,4]{2,1,0:T(8,128)}, u32[]{:S(2)}, u32[]{:S(2)}) collective-permute-start(f32[8,40,4]{2,1,0:T(8,128)S(1)} %get-tuple-element.9), channel_id=1, source_target_pairs={{4,0},{8,4},{12,8},{0,12},{5,1},{9,5},{13,9},{1,13},{6,2},{10,6},{... | collective-permute-start | bytes 15368 | tf_op jit(solution)/shard_map/ppermute | solution.py:36
  36.2 0.7 copy-start.6
  45.1 39.0 %collective-permute-start.6 = (f32[4,40,2056]{2,1,0:T(8,128)}, f32[4,40,2056]{2,1,0:T(8,128)}, u32[]{:S(2)}, u32[]{:S(2)}) collective-permute-start(f32[4,40,2056]{2,1,0:T(8,128)} %get-tuple-element.4), channel_id=1, source_target_pairs={{0,1},{1,2},{2,3},{3,0},{4,5},{5,6},{6,7},{7,4},{8,9},{9,10},{10,1... | collective-permute-start | bytes 3947528 | tf_op jit(solution)/shard_map/ppermute | solution.py:33
  47.0 63.5 %collective-permute-start.7 = (f32[4,40,2056]{2,1,0:T(8,128)}, f32[4,40,2056]{2,1,0:T(8,128)}, u32[]{:S(2)}, u32[]{:S(2)}) collective-permute-start(f32[4,40,2056]{2,1,0:T(8,128)} %get-tuple-element.5), channel_id=1, source_target_pairs={{1,0},{2,1},{3,2},{0,3},{5,4},{6,5},{7,6},{4,7},{9,8},{10,9},{11,1... | collective-permute-start | bytes 3947528 | tf_op jit(solution)/shard_map/ppermute | solution.py:36
  49.0 10.4 %copy-start.5 = (f32[256,8,32]{0,2,1:T(8,128)S(1)}, f32[256,8,32]{0,2,1:T(8,128)}, u32[]{:S(2)}) copy-start(f32[256,8,32]{0,2,1:T(8,128)} %slice_bitcast_fusion.3) | copy-start | bytes 786436
  59.4 2.3 %copy-start.1 = (f32[8,32,2048]{2,1,0:T(8,128)S(1)}, f32[8,32,2048]{2,1,0:T(8,128)}, u32[]{:S(2)}) copy-start(f32[8,32,2048]{2,1,0:T(8,128)} %param.5) | copy-start | bytes 6291460
  59.4 2.3 %copy-start.7 = (f32[8,40,4]{2,1,0:T(8,128)S(1)}, f32[8,40,4]{2,1,0:T(8,128)}, u32[]{:S(2)}) copy-start(f32[8,40,4]{2,1,0:T(8,128)} %copy-done.6) | copy-start | bytes 15364
  59.7 11.3 %copy-start.4 = (f32[3,256,8,32]{1,3,2,0:T(8,128)}, f32[3,256,8,32]{1,3,2,0:T(8,128)S(1)}, u32[]{:S(2)}) copy-start(f32[3,256,8,32]{1,3,2,0:T(8,128)S(1)} %fusion.67) | copy-start | bytes 2359300
  59.9 9.0 %collective-permute-start = (f32[3,2,8,32]{1,3,2,0:T(8,128)S(1)}, f32[3,2,8,32]{1,3,2,0:T(8,128)S(1)}, u32[]{:S(2)}, u32[]{:S(2)}) collective-permute-start(f32[3,2,8,32]{1,3,2,0:T(8,128)S(1)} %get-tuple-element.12), channel_id=1, source_target_pairs={{0,4},{4,8},{8,12},{12,0},{1,5},{5,9},{9,13},{13,1},{2,6},{6,10},{... | collective-permute-start | bytes 18440 | tf_op jit(solution)/shard_map/ppermute | solution.py:33
  61.1 10.0 %collective-permute-start.1 = (f32[3,2,8,32]{1,3,2,0:T(8,128)S(1)}, f32[3,2,8,32]{1,3,2,0:T(8,128)S(1)}, u32[]{:S(2)}, u32[]{:S(2)}) collective-permute-start(f32[3,2,8,32]{1,3,2,0:T(8,128)S(1)} %get-tuple-element.13), channel_id=1, source_target_pairs={{4,0},{8,4},{12,8},{0,12},{5,1},{9,5},{13,9},{1,13},{6,2},{10,6},{... | collective-permute-start | bytes 18440 | tf_op jit(solution)/shard_map/ppermute | solution.py:36
Sparse Core Ops, SparseCore 0:
  9.6 34.7 all-gather.1
where the time goes:
time: 141 us; the launch traced here: 140 us
  waiting for transfers between devices  43.4 us (31%)
  other arithmetic  35.5 us (25%)
  matrix products  23.5 us (17%)
  between operations  14.2 us (10%)
  local copies, waits for them, and re-layouts  13.2 us (9%)
  starting transfers between devices  10.5 us (7%)
    ppermute x4, waiting for transfers between devices, padded_2(): lax.ppermute(lax.slice_in_dim(block, 0, width, axis=dim), axis, backward)  31.6 us
    add x1, other arithmetic, scalar_update(): return centre - advect_rate * advection + diffuse_rate * curvature  22.9 us
    dot_general x1, matrix products, per_device(): fine = jnp.einsum('cxzy,xi->czyi', widened, matrix, precision=highest)  13 us
    ppermute x4, waiting for transfers between devices, padded_2(): lax.ppermute(lax.slice_in_dim(block, block.shape[dim] - width, None, axis...  11.1 us
    unnamed x1, matrix products  10.4 us
    select_n x1, other arithmetic, derivative_rows(): first = jnp.where(same, 0.0, 0.5 * parity * jnp.cos(angle) / sine)  6.59 us
    ppermute x4, starting transfers between devices, padded_2(): lax.ppermute(lax.slice_in_dim(block, block.shape[dim] - width, None, axis...  6.01 us
    slice x4, local copies, waits for them, and re-layouts, padded_2(): lax.slice_in_dim(block, block.shape[dim] - width, None, axis=dim)  5.93 us
  transfers between devices with their start and end apart: 9, of which 5 were waited for; matrix products, arithmetic and copies ran while one was open for 35% of the time, Pallas kernels for 0%

commit v1 on v0

v1 whole, which is shorter than its diff:
```python
import functools

import jax
import jax.numpy as jnp
import ml_dtypes
import numpy as np
from jax import lax
from jax.experimental import pallas as pl
from jax.experimental.pallas import tpu as pltpu
from jax.sharding import PartitionSpec as P

velocity_step = 0.002
viscosity = 0.00125
advect_rate = 0.2
diffuse_rate = 0.05
first_side = (0.8, -0.2, 4.0 / 105.0, -1.0 / 280.0)
second_side = (1.6, -0.2, 8.0 / 315.0, -1.0 / 560.0)
second_centre = -205.0 / 72.0
slope = tuple(-advect_rate * a for a in first_side)
bend = tuple(diffuse_rate * b for b in second_side)
centre_weight = 1.0 + 3.0 * diffuse_rate * second_centre
reach = 4
lanes = 128
vmem_bytes = 48 * 1024 * 1024


def ring(axis, step):
    count = lax.axis_size(axis)
    return [(i, (i + step) % count) for i in range(count)]


def exclusive(axis, mask):
    return [(i, i ^ mask) for i in range(lax.axis_size(axis))]


def split_table(values):
    high = values.astype(np.float32).astype(ml_dtypes.bfloat16)
    low = (values - high.astype(np.float64)).astype(np.float32).astype(ml_dtypes.bfloat16)
    return high, low


def circulant_tables(length, cells):
    s = np.arange(length)
    signed = np.where(s > length // 2, s - length, s)
    angle = signed * (np.pi / length)
    sine = np.where(s == 0, 1.0, np.sin(angle))
    parity = 1.0 - 2.0 * (s % 2)
    first = np.where(s == 0, 0.0, 0.5 * parity * np.cos(angle) / sine) * velocity_step
    second = np.where(s == 0, -(length * length) / 12.0 - 1.0 / 6.0, -0.5 * parity / (sine * sine))
    second = second * (velocity_step * viscosity)
    own = np.arange(cells)
    outer = np.zeros(lanes, np.int64)
    used = np.zeros(lanes)
    for lane, cell in ((0, cells), (1, cells + 1), (lanes - 2, -2), (lanes - 1, -1)):
        outer[lane] = cell
        used[lane] = 1.0
    blocks = []
    for distance in range(length // cells):
        main = (distance * cells + own[None, :] - own[:, None]) % length
        side = (distance * cells + outer[None, :] - own[:, None]) % length
        blocks.append(
            np.concatenate([first[main], second[main], first[side] * used, second[side] * used], axis=1)
        )
    return split_table(np.stack(blocks))


def dot(a, b):
    return jnp.dot(a, b, preferred_element_type=jnp.float32)


def split(value):
    high = value.astype(jnp.bfloat16)
    return high, (value - high.astype(jnp.float32)).astype(jnp.bfloat16)


def segment_kernel(length, info, *refs):
    v_refs, high_refs, low_refs = refs[:4], refs[4:8], refs[8:12]
    main_ref, outer_ref = refs[12:]
    kinds, rows, cells = v_refs[0].shape
    blocks = [ref[...].reshape(kinds * rows, cells) for ref in v_refs]
    total = jnp.zeros((kinds * rows, 2 * cells + 2 * lanes), jnp.float32)
    sums = jnp.zeros((kinds * rows, 1), jnp.float32)
    for block, high_ref, low_ref in zip(blocks, high_refs, low_refs):
        high, low = split(block)
        total += dot(high, high_ref[0]) + (dot(low, high_ref[0]) + dot(high, low_ref[0]))
        sums += jnp.sum(block, axis=1, keepdims=True)
    mean = sums * (1.0 / length)
    even = info[4] == 0
    after = jnp.where(even, blocks[1][:, :lanes], blocks[3][:, :lanes])
    before = jnp.where(even, blocks[3][:, cells - lanes :], blocks[1][:, cells - lanes :])
    place = lax.broadcasted_iota(jnp.int32, after.shape, 1)
    outer = jnp.where(place < lanes // 2, after, before)

    def advance(own, first, second):
        lead = jnp.concatenate([own[:rows]] * kinds, axis=0)
        return own - mean + (second - lead * first)

    main = advance(blocks[0], total[:, :cells], total[:, cells : 2 * cells])
    side = advance(outer, total[:, 2 * cells : 2 * cells + lanes], total[:, 2 * cells + lanes :])
    main_ref[...] = main.reshape(kinds, rows, cells)
    outer_ref[...] = side.reshape(kinds, rows, lanes)


def segment_call(blocks, info, length):
    kinds, rows, cells = blocks[0].shape
    steps = 2
    part = rows // steps
    high, low = circulant_tables(length, cells)
    width = high.shape[2]
    whole = pl.BlockSpec((kinds, part, cells), lambda g, info: (0, g, 0))
    tables = [
        pl.BlockSpec((1, cells, width), functools.partial(lambda j, g, info: (info[j], 0, 0), j))
        for j in range(4)
    ]
    return pl.pallas_call(
        functools.partial(segment_kernel, length),
        grid_spec=pltpu.PrefetchScalarGridSpec(
            num_scalar_prefetch=1,
            grid=(steps,),
            in_specs=[whole] * 4 + tables + tables,
            out_specs=[whole, pl.BlockSpec((kinds, part, lanes), lambda g, info: (0, g, 0))],
        ),
        out_shape=[
            jax.ShapeDtypeStruct((kinds, rows, cells), jnp.float32),
            jax.ShapeDtypeStruct((kinds, rows, lanes), jnp.float32),
        ],
        compiler_params=pltpu.CompilerParams(vmem_limit_bytes=vmem_bytes),
        cost_estimate=pl.CostEstimate(
            flops=6 * kinds * rows * length * width, bytes_accessed=8 * 2**20, transcendentals=0
        ),
        name="segment",
    )(info, *blocks, *([jnp.asarray(high)] * 4), *([jnp.asarray(low)] * 4))


def catmull_weights(fraction):
    square = fraction * fraction
    cube = square * fraction
    return (
        (-cube + 2.0 * square - fraction) * 0.5,
        (3.0 * cube - 5.0 * square + 2.0) * 0.5,
        (-3.0 * cube + 4.0 * square + fraction) * 0.5,
        (cube - square) * 0.5,
    )


def spline_matrix(local_base, fraction, cells, refine):
    tiles = cells // lanes
    row = lax.iota(jnp.int32, 2 * lanes)[:, None]
    half = (lax.iota(jnp.int32, local_base.shape[0]) // (refine * (lanes // 2)))[None, :]
    own = half // 2
    other = (own + jnp.where(half % 2 == 1, 1, tiles)) % (tiles + 1)
    lane = jnp.where(row < lanes, own * lanes + row, other * lanes + row - lanes)
    cell = jnp.where(lane < cells + lanes // 2, lane, lane - cells - lanes)
    gap = cell - local_base[None, :]
    matrix = jnp.zeros(gap.shape, jnp.float32)
    for tap, weight in enumerate(catmull_weights(fraction)):
        matrix = jnp.where(gap == tap - 1, weight[None, :], matrix)
    return matrix


def combine_kernel(tiles, main_ref, outer_ref, matrix_ref, gx_ref, gy_ref, gz_ref, base_ref,
                   out_ref, fine_ref, seg_high, seg_low):
    step = pl.program_id(0)
    kinds, rows, cells = main_ref.shape

    @pl.when(step == 0)
    def _():
        for ref, begin, width in ((main_ref, 0, cells), (outer_ref, cells, lanes)):
            high, low = split(ref[...].reshape(kinds * rows, width))
            seg_high[:, begin : begin + width] = high
            seg_low[:, begin : begin + width] = low

    own = step // 2
    other = lax.rem(own + jnp.where(lax.rem(step, 2) == 1, 1, tiles), tiles + 1)

    def pair(ref):
        return jnp.concatenate(
            [ref[:, pl.ds(pl.multiple_of(at * lanes, lanes), lanes)] for at in (own, other)], axis=1
        )

    high, low = pair(seg_high), pair(seg_low)
    weights, rest = split(matrix_ref[...])
    fine = dot(high, weights) + (dot(low, weights) + dot(high, rest))
    vertical = fine[2 * rows :]
    out_ref[...] = base_ref[...] + (
        fine[:rows] * gx_ref[...] + fine[rows : 2 * rows] * gy_ref[...] + vertical * gz_ref[...]
    )
    fine_ref[...] = vertical


def combine_call(main, outer, matrix, gx, gy, gz, base):
    kinds, rows, cells = main.shape
    points = matrix.shape[1]
    steps = 2 * (cells // lanes)
    width = points // steps
    tile = pl.BlockSpec((rows, width), lambda t: (0, t))
    weight = pl.BlockSpec((2 * lanes, width), lambda t: (0, t))
    flat = jax.ShapeDtypeStruct((rows, points), jnp.float32)
    return pl.pallas_call(
        functools.partial(combine_kernel, cells // lanes),
        grid=(steps,),
        in_specs=[
            pl.BlockSpec((kinds, rows, cells), lambda t: (0, 0, 0)),
            pl.BlockSpec((kinds, rows, lanes), lambda t: (0, 0, 0)),
            weight,
            tile,
            tile,
            tile,
            tile,
        ],
        out_specs=[tile, tile],
        out_shape=[flat, flat],
        scratch_shapes=[
            pltpu.VMEM((kinds * rows, cells + lanes), jnp.bfloat16),
            pltpu.VMEM((kinds * rows, cells + lanes), jnp.bfloat16),
        ],
        compiler_params=pltpu.CompilerParams(vmem_limit_bytes=vmem_bytes),
        cost_estimate=pl.CostEstimate(
            flops=12 * kinds * rows * lanes * points, bytes_accessed=16 * 2**20, transcendentals=0
        ),
        name="combine",
    )(main, outer, matrix, gx, gy, gz, base)


def inner_kernel(steps, mid_ref, left_ref, right_ref, before_ref, after_ref, rows_ref,
                 gx_ref, gy_ref, gz_ref, base_ref):
    step = pl.program_id(0)
    depth, rows, width = mid_ref.shape
    at_first, at_last = step == 0, step == steps - 1
    place = lax.broadcasted_iota(jnp.int32, (rows, lanes), 1)
    for z in range(depth):
        mid = mid_ref[z]
        left = jnp.where(at_first, before_ref[z], left_ref[z])
        right = jnp.where(at_last, after_ref[z], right_ref[z])
        curve = centre_weight * mid

        ringed = jnp.concatenate([mid, jnp.where(place < lanes // 2, right, left)], axis=1)
        grade = None
        for m in range(1, reach + 1):
            ahead = pltpu.roll(ringed, width + lanes - m, 1)[:, :width]
            behind = pltpu.roll(ringed, m, 1)[:, :width]
            term = slope[m - 1] * (ahead - behind)
            grade = term if grade is None else grade + term
            curve += bend[m - 1] * (ahead + behind)
        gx_ref[z] = grade

        ringed = jnp.concatenate([mid, rows_ref[z]], axis=0)
        grade = None
        for m in range(1, reach + 1):
            ahead = pltpu.roll(ringed, rows + 2 * reach - m, 0)[:rows]
            behind = pltpu.roll(ringed, m, 0)[:rows]
            term = slope[m - 1] * (ahead - behind)
            grade = term if grade is None else grade + term
            curve += bend[m - 1] * (ahead + behind)
        gy_ref[z] = grade

        grade = None
        for m in range(1, reach + 1):
            for sign in (1, -1):
                if 0 <= z + sign * m < depth:
                    near = mid_ref[z + sign * m]
                    term = (sign * slope[m - 1]) * near
                    grade = term if grade is None else grade + term
                    curve += bend[m - 1] * near
        gz_ref[z] = grade
        base_ref[z] = curve


def inner_call(scalar, before, after, outer_rows):
    depth, rows, points = scalar.shape
    width = min(512, points)
    steps = points // width
    tiles = width // lanes
    last = points // lanes - 1
    tile = pl.BlockSpec((depth, rows, width), lambda t: (0, 0, t))
    edge = (depth, rows, lanes)
    shape = jax.ShapeDtypeStruct(scalar.shape, jnp.float32)
    return pl.pallas_call(
        functools.partial(inner_kernel, steps),
        grid=(steps,),
        in_specs=[
            tile,
            pl.BlockSpec(edge, lambda t: (0, 0, jnp.maximum(t * tiles - 1, 0))),
            pl.BlockSpec(edge, lambda t: (0, 0, jnp.minimum((t + 1) * tiles, last))),
            pl.BlockSpec(edge, lambda t: (0, 0, 0)),
            pl.BlockSpec(edge, lambda t: (0, 0, 0)),
            pl.BlockSpec((depth, 2 * reach, width), lambda t: (0, 0, t)),
        ],
        out_specs=[tile] * 4,
        out_shape=[shape] * 4,
        compiler_params=pltpu.CompilerParams(vmem_limit_bytes=vmem_bytes),
        cost_estimate=pl.CostEstimate(
            flops=100 * scalar.size, bytes_accessed=24 * scalar.size, transcendentals=0
        ),
        name="inner",
    )(scalar, scalar, scalar, before, after, outer_rows)


def outer_kernel(above, part_ref, fine_ref, halo_ref, out_ref):
    for p in range(reach):
        grade = curve = None
        for h in range(reach):
            m = reach + h - p if above else h - reach - p
            if 1 <= abs(m) <= reach:
                near = halo_ref[h]
                first = (slope[m - 1] if m > 0 else -slope[-m - 1]) * near
                second = bend[abs(m) - 1] * near
                grade = first if grade is None else grade + first
                curve = second if curve is None else curve + second
        out_ref[p] = part_ref[p] + (fine_ref[p] * grade + curve)


def outer_call(above, part, fine, halo):
    depth, rows, points = part.shape
    half = depth // reach - 1 if above else 0
    steps = 4
    width = points // steps if points % (steps * lanes) == 0 else points
    block = pl.BlockSpec((reach, rows, width), lambda t: (half, 0, t))
    return pl.pallas_call(
        functools.partial(outer_kernel, above),
        grid=(points // width,),
        in_specs=[block, block, pl.BlockSpec((reach, rows, width), lambda t: (0, 0, t))],
        out_specs=block,
        out_shape=jax.ShapeDtypeStruct(part.shape, jnp.float32),
        input_output_aliases={0: 0},
        compiler_params=pltpu.CompilerParams(vmem_limit_bytes=vmem_bytes),
        cost_estimate=pl.CostEstimate(
            flops=50 * halo.size, bytes_accessed=16 * halo.size, transcendentals=0
        ),
        name="outer",
    )(part, fine, halo)


def general_segment(rows_of_x, block, length):
    cells = rows_of_x.shape[2]
    high, low = circulant_tables(length, cells)
    table = jnp.asarray(high.astype(np.float32)) + jnp.asarray(low.astype(np.float32))
    everyone = lax.all_gather(rows_of_x, "blk", axis=0)
    count = everyone.shape[0]
    order = (block - lax.iota(jnp.int32, count)) % count
    total = jnp.einsum(
        "bcrx,bxk->crk", everyone, jnp.take(table, order, axis=0), precision=lax.Precision.HIGHEST
    )
    mean = jnp.sum(everyone, axis=(0, 3))[..., None] / length
    before = jnp.take(everyone, (block - 1) % count, axis=0)[..., -2:]
    after = jnp.take(everyone, (block + 1) % count, axis=0)[..., :2]

    def sides(start):
        return (total[..., start + lanes - 2 : start + lanes], total[..., start : start + 2])

    low_first, high_first = sides(2 * cells)
    low_second, high_second = sides(2 * cells + lanes)
    first = jnp.concatenate([low_first, total[..., :cells], high_first], axis=2)
    second = jnp.concatenate([low_second, total[..., cells : 2 * cells], high_second], axis=2)
    own = jnp.concatenate([before, rows_of_x, after], axis=2)
    return own - mean + (second - own[0:1] * first)


def general_fine(wide, local_base, fraction):
    slots = lax.iota(jnp.int32, wide.shape[2])[:, None]
    matrix = jnp.zeros((wide.shape[2], local_base.shape[0]), jnp.float32)
    for tap, weight in enumerate(catmull_weights(fraction)):
        matrix = matrix + jnp.where(slots == (local_base + (tap + 1))[None, :], weight[None, :], 0.0)
    return jnp.einsum("crx,xi->cri", wide, matrix, precision=lax.Precision.HIGHEST)


def per_device(velocity, scalar, spline_base, spline_frac):
    kinds, cells, depth, height = velocity.shape
    points = scalar.shape[2]
    rows = depth * height
    count = lax.axis_size("blk")
    length = cells * count
    block = lax.axis_index("blk")

    lower = lax.ppermute(scalar[-reach:], "dep", ring("dep", 1))
    upper = lax.ppermute(scalar[:reach], "dep", ring("dep", -1))
    rows_of_x = jnp.transpose(velocity, (0, 2, 3, 1)).reshape(kinds, rows, cells)

    fast = count == 4 and cells % lanes == 0
    if fast:
        chip = lax.ppermute(rows_of_x, "blk", exclusive("blk", 2))
        core = lax.ppermute(rows_of_x, "blk", exclusive("blk", 1))
    if lax.axis_size("grp") == 2:
        edges = jnp.concatenate([scalar[:, :reach], scalar[:, -reach:]], axis=1)
        outer_rows = lax.ppermute(edges, "grp", ring("grp", 1))
    else:
        outer_rows = jnp.concatenate(
            [
                lax.ppermute(scalar[:, :reach], "grp", ring("grp", -1)),
                lax.ppermute(scalar[:, -reach:], "grp", ring("grp", 1)),
            ],
            axis=1,
        )
    before = lax.ppermute(scalar[:, :, -lanes:], "blk", ring("blk", 1))
    after = lax.ppermute(scalar[:, :, :lanes], "blk", ring("blk", -1))

    gx, gy, gz, base = inner_call(scalar, before, after, outer_rows)
    local_base = spline_base - block * cells
    flat = (rows, points)
    if fast:
        matrix = spline_matrix(local_base, spline_frac, cells, points // cells)
        diagonal = lax.ppermute(chip, "blk", exclusive("blk", 1))
        info = jnp.stack([(block - (block ^ j)) % count for j in range(4)] + [block % 2])
        main, outer = segment_call([rows_of_x, core, chip, diagonal], info.astype(jnp.int32), length)
        part, vertical = combine_call(
            main, outer, matrix, gx.reshape(flat), gy.reshape(flat), gz.reshape(flat), base.reshape(flat)
        )
    else:
        wide = general_segment(rows_of_x, block, length)
        main = wide[..., 2:-2]
        fine = general_fine(wide, local_base, spline_frac)
        vertical = fine[2]
        part = base.reshape(flat) + (
            fine[0] * gx.reshape(flat) + fine[1] * gy.reshape(flat) + vertical * gz.reshape(flat)
        )
    part, vertical = part.reshape(scalar.shape), vertical.reshape(scalar.shape)
    part = outer_call(False, part, vertical, lower)
    result = outer_call(True, part, vertical, upper)
    segment = jnp.transpose(main.reshape(kinds, depth, height, cells), (0, 3, 1, 2))
    return segment, result


def solution(mesh):
    in_specs = (P(None, "blk", "dep", "grp"), P("dep", "grp", "blk"), P("blk"), P("blk"))
    out_specs = (P(None, "blk", "dep", "grp"), P("dep", "grp", "blk"))
    return jax.shard_map(
        per_device, mesh=mesh, in_specs=in_specs, out_specs=out_specs, check_vma=False
    )
```

time: 141 us -> 77.3 us (0.55)
  other arithmetic: 35.5 us -> 2.26 us
  Pallas kernels: 0 us -> 31.3 us
  matrix products: 23.5 us -> 0 us
  waiting for transfers between devices: 43.4 us -> 22.1 us
  between operations: 14.2 us -> 0.79 us
  local copies, waits for them, and re-layouts: 13.2 us -> 9.4 us
    pallas_call x0 -> x5, Pallas kernels: none -> 31.3 us  [the longest x1 10.3 us: inner_call(): pl.pallas_call(functools.partial(inner_kernel, steps), grid=(steps,), in_...]
    add x5 -> x0, other arithmetic: 24.1 us -> none  [the longest x1 22.9 us: scalar_update(): return centre - advect_rate * advection + diffuse_rate * curvature]
    ppermute x8, waiting for transfers between devices: 42.7 us -> 22.1 us  [the longest x1 12.3 us: per_device(): upper = lax.ppermute(scalar[:reach], 'dep', ring('dep', -1))]
    dot_general x1 -> x0, matrix products: 13 us -> none  [per_device(): fine = jnp.einsum('cxzy,xi->czyi', widened, matrix, precision=highest)]
    unnamed x1 -> x0, matrix products: 10.4 us -> none
    concatenate x3 -> x0, local copies, waits for them, and re-layouts: 5.68 us -> none  [the longest x2 5.68 us: padded_2(): block = jnp.concatenate([low, block, high], axis=dim)]
    select_n x1, other arithmetic: 6.59 us -> 1.31 us  [spline_matrix(): matrix = jnp.where(gap == tap - 1, weight[None, :], matrix)]
    concatenate x2 -> x1, other arithmetic: 4.18 us -> 0.9 us  [per_device(): edges = jnp.concatenate([scalar[:, :reach], scalar[:, -reach:]], axis=1)]
  transfers between devices with their start and end apart: 9 -> 8, of which waited for: 5 -> 3; matrix products, arithmetic and copies ran while one was open for 35% -> 10% of each run, Pallas kernels for 0% -> 37%
where the time goes in v1:
time: 77.3 us; the launch traced here: 76.1 us
  Pallas kernels  31.3 us (40%)
  waiting for transfers between devices  22.1 us (29%)
  starting transfers between devices  10.1 us (13%)
  local copies, waits for them, and re-layouts  9.4 us (12%)
  other arithmetic  2.26 us (3%)
  between operations  0.79 us (1%)
    ppermute x1, waiting for transfers between devices, per_device(): upper = lax.ppermute(scalar[:reach], 'dep', ring('dep', -1))  12.3 us
    pallas_call x1, Pallas kernels, inner_call(): pl.pallas_call(functools.partial(inner_kernel, steps), grid=(steps,), in_...  10.3 us
    ppermute x1, waiting for transfers between devices, per_device(): chip = lax.ppermute(rows_of_x, 'blk', exclusive('blk', 2))  8.87 us
    pallas_call x2, Pallas kernels, outer_call(): pl.pallas_call(functools.partial(outer_kernel, above), grid=(points // wi...  7.05 us
    pallas_call x1, Pallas kernels, combine_call(): pl.pallas_call(functools.partial(combine_kernel, cells // lanes), grid=(s...  7.02 us
    pallas_call x1, Pallas kernels, segment_call(): pl.pallas_call(functools.partial(segment_kernel, length), grid_spec=pltpu...  6.96 us
    unnamed x14, local copies, waits for them, and re-layouts  3.86 us
    slice x1, local copies, waits for them, and re-layouts, per_device(): upper = lax.ppermute(scalar[:reach], 'dep', ring('dep', -1))  3.17 us
  transfers between devices with their start and end apart: 8, of which 3 were waited for; matrix products, arithmetic and copies ran while one was open for 10% of the time, Pallas kernels for 37%

profile of v1, /device:TPU:0, one launch (start us, length us, event | category | flops | bytes accessed | tf_op | source)
XLA Modules:
  0.0 76.1 jit_solution(4463207344309562325)
XLA Ops:
  0.6 0.0 copy-start.5
  0.6 3.0 %collective-permute-start.1 = (f32[3,256,256]{2,1,0:T(8,128)}, f32[3,256,256]{2,1,0:T(8,128)S(1)}, u32[]{:S(2)}, u32[]{:S(2)}) collective-permute-start(f32[3,256,256]{2,1,0:T(8,128)} %bitcast.20), channel_id=1, source_target_pairs={{0,8},{4,12},{8,0},{12,4},{1,9},{5,13},{9,1},{13,5},{2,10},{6,14},... | collective-permute-start | bytes 2359304 | tf_op jit(solution)/shard_map/ppermute | solution.py:381
  3.6 0.0 collective-permute-start
  3.6 1.3 %fusion.31 = (f32[8,4,2048]{2,1,0:T(4,128)S(1)}, f32[8,4,2048]{2,1,0:T(4,128)S(1)}) fusion(f32[8,32,2048]{2,1,0:T(8,128)} %right_ref.1), kind=kLoop, calls=%fused_computation.55 | loop fusion | bytes 1048576 | tf_op jit(solution)/shard_map/slice | solution.py:384
  5.0 0.9 %pad_maximum_fusion = f32[8,8,2048]{2,1,0:T(8,128)} fusion(f32[8,4,2048]{2,1,0:T(4,128)S(1)} %get-tuple-element.21, f32[8,4,2048]{2,1,0:T(4,128)S(1)} %get-tuple-element.20), kind=kLoop, calls=%fused_computation.11 | loop fusion | flops 131072 | bytes 1048576 | tf_op jit(solution)/shard_map/concatenate | solution.py:384
  5.9 1.5 %collective-permute-start.5 = (f32[8,8,2048]{2,1,0:T(8,128)}, f32[8,8,2048]{2,1,0:T(8,128)S(1)}, u32[]{:S(2)}, u32[]{:S(2)}) collective-permute-start(f32[8,8,2048]{2,1,0:T(8,128)} %pad_maximum_fusion), channel_id=1, source_target_pairs={{0,16},{16,0},{1,17},{17,1},{2,18},{18,2},{3,19},{19,3},{4,20},{20... | collective-permute-start | bytes 1572872 | tf_op jit(solution)/shard_map/ppermute | solution.py:385
  7.4 1.0 %fusion.32 = (f32[8,32,128]{2,1,0:T(8,128)S(1)}, f32[8,32,128]{2,1,0:T(8,128)S(1)}) fusion(f32[8,32,2048]{2,1,0:T(8,128)} %right_ref.1), kind=kLoop, calls=%fused_computation.56 | loop fusion | bytes 524288 | tf_op jit(solution)/shard_map/slice | solution.py:395
  8.4 0.3 collective-permute-start.3
  8.6 1.5 %collective-permute-start.4 = (f32[8,32,128]{2,1,0:T(8,128)S(1)}, f32[8,32,128]{2,1,0:T(8,128)S(1)}, u32[]{:S(2)}, u32[]{:S(2)}) collective-permute-start(f32[8,32,128]{2,1,0:T(8,128)S(1)} %get-tuple-element.22), channel_id=1, source_target_pairs={{0,12},{4,0},{8,4},{12,8},{1,13},{5,1},{9,5},{13,9},{2,14},{6,2},{... | collective-permute-start | bytes 393224 | tf_op jit(solution)/shard_map/ppermute | solution.py:395
  10.2 0.0 copy-done.5
  10.2 0.0 copy-start.6
  10.2 3.2 %fusion.30 = (f32[4,32,2048]{2,1,0:T(8,128)}, f32[4,32,2048]{2,1,0:T(8,128)}) fusion(f32[8,32,2048]{2,1,0:T(8,128)} %right_ref.1), kind=kLoop, calls=%fused_computation.54 | loop fusion | bytes 4194304 | tf_op jit(solution)/shard_map/slice | solution.py:376
  13.4 8.9 %collective-permute-done.1.refs_2_ = f32[3,256,256]{2,1,0:T(8,128)S(1)} collective-permute-done((f32[3,256,256]{2,1,0:T(8,128)}, f32[3,256,256]{2,1,0:T(8,128)S(1)}, u32[]{:S(2)}, u32[]{:S(2)}) %collective-permute-start.1) | collective-permute-done | bytes 786464 | tf_op jit(solution)/shard_map/ppermute | solution.py:381
  22.2 0.0 collective-permute-start.2
  22.2 0.0 copy-done.6
  22.3 0.1 stack.20.info
  22.4 1.0 %collective-permute-done.3.before_ref = f32[8,32,128]{2,1,0:T(8,128)S(1)} collective-permute-done((f32[8,32,128]{2,1,0:T(8,128)S(1)}, f32[8,32,128]{2,1,0:T(8,128)S(1)}, u32[]{:S(2)}, u32[]{:S(2)}) %collective-permute-start.3) | collective-permute-done | bytes 131104 | tf_op jit(solution)/shard_map/ppermute | solution.py:394
  23.4 1.5 %collective-permute-start.6 = (f32[4,32,2048]{2,1,0:T(8,128)}, f32[4,32,2048]{2,1,0:T(8,128)S(1)}, u32[]{:S(2)}, u32[]{:S(2)}) collective-permute-start(f32[4,32,2048]{2,1,0:T(8,128)} %get-tuple-element.19), channel_id=1, source_target_pairs={{0,1},{1,2},{2,3},{3,0},{4,5},{5,6},{6,7},{7,4},{8,9},{9,10},{10,1... | collective-permute-start | bytes 3145736 | tf_op jit(solution)/shard_map/ppermute | solution.py:375
  24.9 0.0 collective-permute-done.4.after_ref
  24.9 2.3 %collective-permute-start.7 = (f32[4,32,2048]{2,1,0:T(8,128)}, f32[4,32,2048]{2,1,0:T(8,128)S(1)}, u32[]{:S(2)}, u32[]{:S(2)}) collective-permute-start(f32[4,32,2048]{2,1,0:T(8,128)} %get-tuple-element.18), channel_id=1, source_target_pairs={{0,3},{1,0},{2,1},{3,2},{4,7},{5,4},{6,5},{7,6},{8,11},{9,8},{10,9... | collective-permute-start | bytes 3145736 | tf_op jit(solution)/shard_map/ppermute | solution.py:376
  27.2 1.3 %select_select_fusion.matrix_ref = f32[256,2048]{1,0:T(8,128)S(1)} fusion(f32[2048]{0:T(1024)S(1)} %get-tuple-element.26, f32[2048]{0:T(1024)S(1)} %get-tuple-element.25, f32[2048]{0:T(1024)S(1)} %get-tuple-element.27, f32[2048]{0:T(1024)S(1)} %get-tuple-element.24, s32[2048]{0:T(1024)S(1)} %get-tuple-element.29, s32[2048]{0:T(1024)S(1)} %get-tuple-element.28, ...), kind=kLoop, calls=%fused_computation.10 | loop fusion | flops 8388608 | bytes 2154752 | tf_op jit(solution)/shard_map/jit(_where)/select_n | solution.py:157
  28.5 0.0 copy-start
  28.5 0.0 copy-start.3
  28.5 0.0 collective-permute-done.5.rows_ref
  28.6 10.3 %inner.1 = (f32[8,32,2048]{2,1,0:T(8,128)S(1)}, f32[8,32,2048]{2,1,0:T(8,128)S(1)}, f32[8,32,2048]{2,1,0:T(8,128)}, f32[8,32,2048]{2,1,0:T(8,128)}) custom-call(f32[8,32,2048]{2,1,0:T(8,128)} %right_ref.1, f32[8,32,2048]{2,1,0:T(8,128)} %right_ref.1, f32[8,32,2048]{2,1,0:T(8,128)} %right_ref.1, f32[8,32,128]{2,1,0:T(8,128)S(1)} %collective-permute-done.3.before_ref, ...), custom_call_target="tpu_custom_call" | custom-call | flops 52428800 | bytes 12582912 | tf_op jit(solution)/shard_map/inner/pallas_call | solution.py:278
  38.8 0.0 copy-start.1
  38.8 1.3 %copy-done.1 = f32[8,32,2048]{2,1,0:T(8,128)} copy-done((f32[8,32,2048]{2,1,0:T(8,128)}, f32[8,32,2048]{2,1,0:T(8,128)S(1)}, u32[]{:S(2)}) %copy-start.1) | copy-done | bytes 2097176
  40.2 0.0 copy-start.2
  40.2 1.4 %copy-done.2 = f32[8,32,2048]{2,1,0:T(8,128)} copy-done((f32[8,32,2048]{2,1,0:T(8,128)}, f32[8,32,2048]{2,1,0:T(8,128)S(1)}, u32[]{:S(2)}) %copy-start.2) | copy-done | bytes 2097176
  41.6 0.0 collective-permute-done.refs_1_
  41.6 0.0 collective-permute-done.2.refs_3_
  41.6 0.0 copy-done
  41.6 0.0 copy-done.3
  41.6 7.0 %segment.1 = (f32[3,256,256]{2,1,0:T(8,128)}, f32[3,256,128]{2,1,0:T(8,128)S(1)}) custom-call(s32[5]{0:T(128)S(1)} %stack.20.info, f32[3,256,256]{2,1,0:T(8,128)S(1)} %bitcast.22, f32[3,256,256]{2,1,0:T(8,128)S(1)} %collective-permute-done.refs_1_, f32[3,256,256]{2,1,0:T(8,128)S(1)} %collective-permute-done.1.refs_2_, ...), custom_call_target="tpu_custom_call" | custom-call | flops 3623878656 | bytes 8388608 | tf_op jit(solution)/shard_map/segment/pallas_call | solution.py:115
  48.5 0.0 copy-start.4
  48.5 1.1 %copy-done.4 = f32[3,256,256]{2,1,0:T(8,128)S(1)} copy-done((f32[3,256,256]{2,1,0:T(8,128)S(1)}, f32[3,256,256]{2,1,0:T(8,128)}, u32[]{:S(2)}) %copy-start.4) | copy-done | bytes 786456
  49.7 7.0 %combine.1 = (f32[256,2048]{1,0:T(8,128)}, f32[256,2048]{1,0:T(8,128)S(1)}) custom-call(f32[3,256,256]{2,1,0:T(8,128)S(1)} %copy-done.4, f32[3,256,128]{2,1,0:T(8,128)S(1)} %get-tuple-element.11.outer_ref, f32[256,2048]{1,0:T(8,128)S(1)} %select_select_fusion.matrix_ref, f32[256,2048]{1,0:T(8,128)} %bitcast.18, f32[256,2048]{1,0:T(8,128)} %bitcast.19, ...), custom_call_target="tpu_custom_call" | custom-call | flops 2415919104 | bytes 16777216 | tf_op jit(solution)/shard_map/combine/pallas_call | solution.py:199
  56.7 0.0 collective-permute-done.6.halo_ref
  56.7 3.5 %outer.2.part_ref = f32[8,32,2048]{2,1,0:T(8,128)} custom-call(f32[8,32,2048]{2,1,0:T(8,128)} %bitcast.24, f32[8,32,2048]{2,1,0:T(8,128)S(1)} %bitcast.16, f32[4,32,2048]{2,1,0:T(8,128)S(1)} %collective-permute-done.6.halo_ref), custom_call_target="tpu_custom_call", output_to_operand_aliasing={{}: (0, {})} | custom-call | flops 13107200 | bytes 4194304 | tf_op jit(solution)/shard_map/outer/pallas_call | solution.py:319
  60.2 12.3 %collective-permute-done.7.halo_ref = f32[4,32,2048]{2,1,0:T(8,128)S(1)} collective-permute-done((f32[4,32,2048]{2,1,0:T(8,128)}, f32[4,32,2048]{2,1,0:T(8,128)S(1)}, u32[]{:S(2)}, u32[]{:S(2)}) %collective-permute-start.7) | collective-permute-done | bytes 1048608 | tf_op jit(solution)/shard_map/ppermute | solution.py:376
  72.5 3.5 %outer.3 = f32[8,32,2048]{2,1,0:T(8,128)} custom-call(f32[8,32,2048]{2,1,0:T(8,128)} %outer.2.part_ref, f32[8,32,2048]{2,1,0:T(8,128)S(1)} %bitcast.17, f32[4,32,2048]{2,1,0:T(8,128)S(1)} %collective-permute-done.7.halo_ref), custom_call_target="tpu_custom_call", output_to_operand_aliasing={{}: (0, {})} | custom-call | flops 13107200 | bytes 4194304 | tf_op jit(solution)/shard_map/outer/pallas_call | solution.py:319
  (4 shorter events, 0.0 us)
Async XLA Ops:
  0.6 9.5 %copy-start.5 = (f32[2048]{0:T(1024)S(1)}, f32[2048]{0:T(1024)}, u32[]{:S(2)}) copy-start(f32[2048]{0:T(1024)} %param.9) | copy-start | bytes 24580
  0.6 21.6 %collective-permute-start.1 = (f32[3,256,256]{2,1,0:T(8,128)}, f32[3,256,256]{2,1,0:T(8,128)S(1)}, u32[]{:S(2)}, u32[]{:S(2)}) collective-permute-start(f32[3,256,256]{2,1,0:T(8,128)} %bitcast.20), channel_id=1, source_target_pairs={{0,8},{4,12},{8,0},{12,4},{1,9},{5,13},{9,1},{13,5},{2,10},{6,14},... | collective-permute-start | bytes 2359304 | tf_op jit(solution)/shard_map/ppermute | solution.py:381
  3.6 37.9 %collective-permute-start = (f32[3,256,256]{2,1,0:T(8,128)}, f32[3,256,256]{2,1,0:T(8,128)S(1)}, u32[]{:S(2)}, u32[]{:S(2)}) collective-permute-start(f32[3,256,256]{2,1,0:T(8,128)} %bitcast.21), channel_id=1, source_target_pairs={{0,4},{4,0},{8,12},{12,8},{1,5},{5,1},{9,13},{13,9},{2,6},{6,2},{1... | collective-permute-start | bytes 2359304 | tf_op jit(solution)/shard_map/ppermute | solution.py:382
  5.9 22.7 %collective-permute-start.5 = (f32[8,8,2048]{2,1,0:T(8,128)}, f32[8,8,2048]{2,1,0:T(8,128)S(1)}, u32[]{:S(2)}, u32[]{:S(2)}) collective-permute-start(f32[8,8,2048]{2,1,0:T(8,128)} %pad_maximum_fusion), channel_id=1, source_target_pairs={{0,16},{16,0},{1,17},{17,1},{2,18},{18,2},{3,19},{19,3},{4,20},{20... | collective-permute-start | bytes 1572872 | tf_op jit(solution)/shard_map/ppermute | solution.py:385
  8.4 15.0 %collective-permute-start.3 = (f32[8,32,128]{2,1,0:T(8,128)S(1)}, f32[8,32,128]{2,1,0:T(8,128)S(1)}, u32[]{:S(2)}, u32[]{:S(2)}) collective-permute-start(f32[8,32,128]{2,1,0:T(8,128)S(1)} %get-tuple-element.23), channel_id=1, source_target_pairs={{0,4},{4,8},{8,12},{12,0},{1,5},{5,9},{9,13},{13,1},{2,6},{6,10},{... | collective-permute-start | bytes 393224 | tf_op jit(solution)/shard_map/ppermute | solution.py:394
  8.6 16.2 %collective-permute-start.4 = (f32[8,32,128]{2,1,0:T(8,128)S(1)}, f32[8,32,128]{2,1,0:T(8,128)S(1)}, u32[]{:S(2)}, u32[]{:S(2)}) collective-permute-start(f32[8,32,128]{2,1,0:T(8,128)S(1)} %get-tuple-element.22), channel_id=1, source_target_pairs={{0,12},{4,0},{8,4},{12,8},{1,13},{5,1},{9,5},{13,9},{2,14},{6,2},{... | collective-permute-start | bytes 393224 | tf_op jit(solution)/shard_map/ppermute | solution.py:395
  10.2 12.1 %copy-start.6 = (s32[2048]{0:T(1024)S(1)}, s32[2048]{0:T(1024)}, u32[]{:S(2)}) copy-start(s32[2048]{0:T(1024)} %param.8) | copy-start | bytes 24580
  22.2 19.3 %collective-permute-start.2 = (f32[3,256,256]{2,1,0:T(8,128)S(1)}, f32[3,256,256]{2,1,0:T(8,128)S(1)}, u32[]{:S(2)}, u32[]{:S(2)}) collective-permute-start(f32[3,256,256]{2,1,0:T(8,128)S(1)} %collective-permute-done.1.refs_2_), channel_id=1, source_target_pairs={{0,4},{4,0},{8,12},{12,8},{1,5},{5,1},{9,13},{13,9},{2,6},{6,2},{1... | collective-permute-start | bytes 2359304 | tf_op jit(solution)/shard_map/ppermute | solution.py:402
  23.4 33.3 %collective-permute-start.6 = (f32[4,32,2048]{2,1,0:T(8,128)}, f32[4,32,2048]{2,1,0:T(8,128)S(1)}, u32[]{:S(2)}, u32[]{:S(2)}) collective-permute-start(f32[4,32,2048]{2,1,0:T(8,128)} %get-tuple-element.19), channel_id=1, source_target_pairs={{0,1},{1,2},{2,3},{3,0},{4,5},{5,6},{6,7},{7,4},{8,9},{9,10},{10,1... | collective-permute-start | bytes 3145736 | tf_op jit(solution)/shard_map/ppermute | solution.py:375
  24.9 47.7 %collective-permute-start.7 = (f32[4,32,2048]{2,1,0:T(8,128)}, f32[4,32,2048]{2,1,0:T(8,128)S(1)}, u32[]{:S(2)}, u32[]{:S(2)}) collective-permute-start(f32[4,32,2048]{2,1,0:T(8,128)} %get-tuple-element.18), channel_id=1, source_target_pairs={{0,3},{1,0},{2,1},{3,2},{4,7},{5,4},{6,5},{7,6},{8,11},{9,8},{10,9... | collective-permute-start | bytes 3145736 | tf_op jit(solution)/shard_map/ppermute | solution.py:376
  28.5 13.0 %copy-start = (bf16[4,256,768]{2,1,0:T(8,128)(2,1)S(1)}, bf16[4,256,768]{2,1,0:T(8,128)(2,1)}, u32[]{:S(2)}) copy-start(bf16[4,256,768]{2,1,0:T(8,128)(2,1)} %constant.129.clone.refs_4_.refs_5_.refs_6_.refs_7_) | copy-start | bytes 4718596
  28.5 13.0 %copy-start.3 = (f32[3,256,8,32]{1,3,2,0:T(8,128)S(1)}, f32[3,256,8,32]{1,3,2,0:T(8,128)}, u32[]{:S(2)}) copy-start(f32[3,256,8,32]{1,3,2,0:T(8,128)} %param.6) | copy-start | bytes 2359300
  38.8 1.3 %copy-start.1 = (f32[8,32,2048]{2,1,0:T(8,128)}, f32[8,32,2048]{2,1,0:T(8,128)S(1)}, u32[]{:S(2)}) copy-start(f32[8,32,2048]{2,1,0:T(8,128)S(1)} %get-tuple-element.12) | copy-start | bytes 6291460
  40.2 1.4 %copy-start.2 = (f32[8,32,2048]{2,1,0:T(8,128)}, f32[8,32,2048]{2,1,0:T(8,128)S(1)}, u32[]{:S(2)}) copy-start(f32[8,32,2048]{2,1,0:T(8,128)S(1)} %get-tuple-element.13) | copy-start | bytes 6291460
  48.5 1.1 %copy-start.4 = (f32[3,256,256]{2,1,0:T(8,128)S(1)}, f32[3,256,256]{2,1,0:T(8,128)}, u32[]{:S(2)}) copy-start(f32[3,256,256]{2,1,0:T(8,128)} %get-tuple-element.10.main_ref) | copy-start | bytes 2359300

commit v2 on v1

--- a/solution.py
+++ b/solution.py
@@ -1,4 +1,5 @@
 import functools
+import math
 
 import jax
 import jax.numpy as jnp
@@ -21,7 +22,8 @@
 centre_weight = 1.0 + 3.0 * diffuse_rate * second_centre
 reach = 4
 lanes = 128
-vmem_bytes = 48 * 1024 * 1024
+vmem_bytes = 60 * 1024 * 1024
+light = pl.CostEstimate(flops=1024, bytes_accessed=1024, transcendentals=0)
 
 
 def ring(axis, step):
@@ -73,63 +75,66 @@
     return high, (value - high.astype(jnp.float32)).astype(jnp.bfloat16)
 
 
-def segment_kernel(length, info, *refs):
-    v_refs, high_refs, low_refs = refs[:4], refs[4:8], refs[8:12]
-    main_ref, outer_ref = refs[12:]
-    kinds, rows, cells = v_refs[0].shape
-    blocks = [ref[...].reshape(kinds * rows, cells) for ref in v_refs]
-    total = jnp.zeros((kinds * rows, 2 * cells + 2 * lanes), jnp.float32)
-    sums = jnp.zeros((kinds * rows, 1), jnp.float32)
-    for block, high_ref, low_ref in zip(blocks, high_refs, low_refs):
-        high, low = split(block)
-        total += dot(high, high_ref[0]) + (dot(low, high_ref[0]) + dot(high, low_ref[0]))
-        sums += jnp.sum(block, axis=1, keepdims=True)
-    mean = sums * (1.0 / length)
+def segment_kernel(length, shares, info, own_ref, *refs):
+    sent, (high_refs, low_refs) = refs[: 3 * shares], (refs[3 * shares :][:4], refs[3 * shares :][4:8])
+    main_ref, outer_ref = refs[-2:]
+    kinds, rows, cells = own_ref.shape
+    part = rows // shares
+    lines = kinds * part
     even = info[4] == 0
-    after = jnp.where(even, blocks[1][:, :lanes], blocks[3][:, :lanes])
-    before = jnp.where(even, blocks[3][:, cells - lanes :], blocks[1][:, cells - lanes :])
-    place = lax.broadcasted_iota(jnp.int32, after.shape, 1)
-    outer = jnp.where(place < lanes // 2, after, before)
-
-    def advance(own, first, second):
-        lead = jnp.concatenate([own[:rows]] * kinds, axis=0)
-        return own - mean + (second - lead * first)
-
-    main = advance(blocks[0], total[:, :cells], total[:, cells : 2 * cells])
-    side = advance(outer, total[:, 2 * cells : 2 * cells + lanes], total[:, 2 * cells + lanes :])
-    main_ref[...] = main.reshape(kinds, rows, cells)
-    outer_ref[...] = side.reshape(kinds, rows, lanes)
-
-
-def segment_call(blocks, info, length):
-    kinds, rows, cells = blocks[0].shape
-    steps = 2
-    part = rows // steps
+    for h in range(shares):
+        span = slice(h * part, (h + 1) * part)
+        blocks = [own_ref[:, span].reshape(lines, cells)]
+        blocks += [sent[j * shares + h][:lines] for j in range(3)]
+        total = jnp.zeros((lines, 2 * cells + 2 * lanes), jnp.float32)
+        sums = jnp.zeros((lines, 1), jnp.float32)
+        for block, high_ref, low_ref in zip(blocks, high_refs, low_refs):
+            high, low = split(block)
+            total += dot(high, high_ref[0]) + (dot(low, high_ref[0]) + dot(high, low_ref[0]))
+            sums += jnp.sum(block, axis=1, keepdims=True)
+        mean = sums * (1.0 / length)
+        after = jnp.where(even, blocks[1][:, :lanes], blocks[3][:, :lanes])
+        before = jnp.where(even, blocks[3][:, cells - lanes :], blocks[1][:, cells - lanes :])
+        place = lax.broadcasted_iota(jnp.int32, after.shape, 1)
+        outer = jnp.where(place < lanes // 2, after, before)
+
+        def advance(own, first, second):
+            lead = jnp.concatenate([own[:part]] * kinds, axis=0)
+            return own - mean + (second - lead * first)
+
+        main = advance(blocks[0], total[:, :cells], total[:, cells : 2 * cells])
+        side = advance(outer, total[:, 2 * cells : 2 * cells + lanes], total[:, 2 * cells + lanes :])
+        main_ref[:, span] = main.reshape(kinds, part, cells)
+        outer_ref[:, span] = side.reshape(kinds, part, lanes)
+
+
+def segment_call(own, core, chip, diagonal, info, length):
+    kinds, rows, cells = own.shape
+    shares = len(core)
     high, low = circulant_tables(length, cells)
     width = high.shape[2]
-    whole = pl.BlockSpec((kinds, part, cells), lambda g, info: (0, g, 0))
+    whole = pl.BlockSpec(own.shape, lambda g, info: (0, 0, 0))
+    sent = pl.BlockSpec(core[0].shape, lambda g, info: (0, 0))
     tables = [
         pl.BlockSpec((1, cells, width), functools.partial(lambda j, g, info: (info[j], 0, 0), j))
         for j in range(4)
     ]
     return pl.pallas_call(
-        functools.partial(segment_kernel, length),
+        functools.partial(segment_kernel, length, shares),
         grid_spec=pltpu.PrefetchScalarGridSpec(
             num_scalar_prefetch=1,
-            grid=(steps,),
-            in_specs=[whole] * 4 + tables + tables,
-            out_specs=[whole, pl.BlockSpec((kinds, part, lanes), lambda g, info: (0, g, 0))],
+            grid=(1,),
+            in_specs=[whole] + [sent] * (3 * shares) + tables + tables,
+            out_specs=[whole, pl.BlockSpec((kinds, rows, lanes), lambda g, info: (0, 0, 0))],
         ),
         out_shape=[
             jax.ShapeDtypeStruct((kinds, rows, cells), jnp.float32),
             jax.ShapeDtypeStruct((kinds, rows, lanes), jnp.float32),
         ],
         compiler_params=pltpu.CompilerParams(vmem_limit_bytes=vmem_bytes),
-        cost_estimate=pl.CostEstimate(
-            flops=6 * kinds * rows * length * width, bytes_accessed=8 * 2**20, transcendentals=0
-        ),
+        cost_estimate=light,
         name="segment",
-    )(info, *blocks, *([jnp.asarray(high)] * 4), *([jnp.asarray(low)] * 4))
+    )(info, own, *core, *chip, *diagonal, *([jnp.asarray(high)] * 4), *([jnp.asarray(low)] * 4))
 
 
 def catmull_weights(fraction):
@@ -158,10 +163,25 @@
     return matrix
 
 
-def combine_kernel(tiles, main_ref, outer_ref, matrix_ref, gx_ref, gy_ref, gz_ref, base_ref,
-                   out_ref, fine_ref, seg_high, seg_low):
-    step = pl.program_id(0)
+def end_terms(halo, sign):
+    grade = curve = None
+    place = lax.broadcasted_iota(jnp.int32, halo.shape, 1)
+    halo = jnp.where(place >= lanes // 2 if sign < 0 else place < lanes // 2, halo, 0.0)
+    for m in range(1, reach + 1):
+        near = pltpu.roll(halo, (-sign * m) % lanes, 1)
+        first, second = (sign * slope[m - 1]) * near, bend[m - 1] * near
+        grade = first if grade is None else grade + first
+        curve = second if curve is None else curve + second
+    near = place < reach if sign < 0 else place >= lanes - reach
+    return jnp.where(near, grade, 0.0), jnp.where(near, curve, 0.0)
+
+
+def combine_kernel(tiles, shares, parity, main_ref, outer_ref, matrix_ref, gx_ref, gy_ref, gz_ref, base_ref, *refs):
+    core_refs, far_refs = refs[:shares], refs[shares : 2 * shares]
+    out_ref, fine_ref, seg_high, seg_low, halo_ref = refs[2 * shares :]
+    step, steps = pl.program_id(0), pl.num_programs(0)
     kinds, rows, cells = main_ref.shape
+    part = rows // shares
 
     @pl.when(step == 0)
     def _():
@@ -169,6 +189,13 @@
             high, low = split(ref[...].reshape(kinds * rows, width))
             seg_high[:, begin : begin + width] = high
             seg_low[:, begin : begin + width] = low
+        core = jnp.concatenate([ref[:, :part] for ref in core_refs], axis=1)
+        far = jnp.concatenate([ref[:, :part] for ref in far_refs], axis=1)
+        even = parity[0] == 0
+        after = jnp.where(even, core, far)[:reach]
+        before = jnp.where(even, far, core)[reach:]
+        gap = jnp.zeros((lanes - 2 * reach, rows), jnp.float32)
+        halo_ref[...] = jnp.concatenate([after, gap, before], axis=0).T
 
     own = step // 2
     other = lax.rem(own + jnp.where(lax.rem(step, 2) == 1, 1, tiles), tiles + 1)
@@ -186,43 +213,55 @@
         fine[:rows] * gx_ref[...] + fine[rows : 2 * rows] * gy_ref[...] + vertical * gz_ref[...]
     )
     fine_ref[...] = vertical
-
-
-def combine_call(main, outer, matrix, gx, gy, gz, base):
+    width = out_ref.shape[1]
+    for at, sign, begin in ((0, -1, 0), (steps - 1, 1, width - lanes)):
+
+        @pl.when(step == at)
+        def _():
+            grade, curve = end_terms(halo_ref[...], sign)
+            span = slice(begin, begin + lanes)
+            out_ref[:, span] += fine[:rows, span] * grade + curve
+
+
+def combine_call(main, outer, matrix, gx, gy, gz, base, core, diagonal, parity):
     kinds, rows, cells = main.shape
     points = matrix.shape[1]
+    shares = len(core)
     steps = 2 * (cells // lanes)
     width = points // steps
-    tile = pl.BlockSpec((rows, width), lambda t: (0, t))
-    weight = pl.BlockSpec((2 * lanes, width), lambda t: (0, t))
+    tile = pl.BlockSpec((rows, width), lambda t, parity: (0, t))
+    ends = pl.BlockSpec((2 * reach, cells), lambda t, parity: (core[0].shape[0] // (2 * reach) - 1, 0))
     flat = jax.ShapeDtypeStruct((rows, points), jnp.float32)
     return pl.pallas_call(
-        functools.partial(combine_kernel, cells // lanes),
-        grid=(steps,),
-        in_specs=[
-            pl.BlockSpec((kinds, rows, cells), lambda t: (0, 0, 0)),
-            pl.BlockSpec((kinds, rows, lanes), lambda t: (0, 0, 0)),
-            weight,
-            tile,
-            tile,
-            tile,
-            tile,
-        ],
-        out_specs=[tile, tile],
+        functools.partial(combine_kernel, cells // lanes, shares),
+        grid_spec=pltpu.PrefetchScalarGridSpec(
+            num_scalar_prefetch=1,
+            grid=(steps,),
+            in_specs=[
+                pl.BlockSpec((kinds, rows, cells), lambda t, parity: (0, 0, 0)),
+                pl.BlockSpec((kinds, rows, lanes), lambda t, parity: (0, 0, 0)),
+                pl.BlockSpec((2 * lanes, width), lambda t, parity: (0, t)),
+                tile,
+                tile,
+                tile,
+                tile,
+            ]
+            + [ends] * (2 * shares),
+            out_specs=[tile, tile],
+            scratch_shapes=[
+                pltpu.VMEM((kinds * rows, cells + lanes), jnp.bfloat16),
+                pltpu.VMEM((kinds * rows, cells + lanes), jnp.bfloat16),
+                pltpu.VMEM((rows, lanes), jnp.float32),
+            ],
+        ),
         out_shape=[flat, flat],
-        scratch_shapes=[
-            pltpu.VMEM((kinds * rows, cells + lanes), jnp.bfloat16),
-            pltpu.VMEM((kinds * rows, cells + lanes), jnp.bfloat16),
-        ],
         compiler_params=pltpu.CompilerParams(vmem_limit_bytes=vmem_bytes),
-        cost_estimate=pl.CostEstimate(
-            flops=12 * kinds * rows * lanes * points, bytes_accessed=16 * 2**20, transcendentals=0
-        ),
+        cost_estimate=light,
         name="combine",
-    )(main, outer, matrix, gx, gy, gz, base)
-
-
-def inner_kernel(steps, mid_ref, left_ref, right_ref, before_ref, after_ref, rows_ref,
+    )(parity, main, outer, matrix, gx, gy, gz, base, *core, *diagonal)
+
+
+def inner_kernel(steps, mid_ref, left_ref, right_ref, top_ref, bottom_ref,
                  gx_ref, gy_ref, gz_ref, base_ref):
     step = pl.program_id(0)
     depth, rows, width = mid_ref.shape
@@ -230,8 +269,8 @@
     place = lax.broadcasted_iota(jnp.int32, (rows, lanes), 1)
     for z in range(depth):
         mid = mid_ref[z]
-        left = jnp.where(at_first, before_ref[z], left_ref[z])
-        right = jnp.where(at_last, after_ref[z], right_ref[z])
+        left = jnp.where(at_first, 0.0, left_ref[z])
+        right = jnp.where(at_last, 0.0, right_ref[z])
         curve = centre_weight * mid
 
         ringed = jnp.concatenate([mid, jnp.where(place < lanes // 2, right, left)], axis=1)
@@ -244,7 +283,7 @@
             curve += bend[m - 1] * (ahead + behind)
         gx_ref[z] = grade
 
-        ringed = jnp.concatenate([mid, rows_ref[z]], axis=0)
+        ringed = jnp.concatenate([mid, top_ref[z], bottom_ref[z]], axis=0)
         grade = None
         for m in range(1, reach + 1):
             ahead = pltpu.roll(ringed, rows + 2 * reach - m, 0)[:rows]
@@ -266,7 +305,7 @@
         base_ref[z] = curve
 
 
-def inner_call(scalar, before, after, outer_rows):
+def inner_call(scalar, top, bottom):
     depth, rows, points = scalar.shape
     width = min(512, points)
     steps = points // width
@@ -282,18 +321,15 @@
             tile,
             pl.BlockSpec(edge, lambda t: (0, 0, jnp.maximum(t * tiles - 1, 0))),
             pl.BlockSpec(edge, lambda t: (0, 0, jnp.minimum((t + 1) * tiles, last))),
-            pl.BlockSpec(edge, lambda t: (0, 0, 0)),
-            pl.BlockSpec(edge, lambda t: (0, 0, 0)),
-            pl.BlockSpec((depth, 2 * reach, width), lambda t: (0, 0, t)),
+            pl.BlockSpec((depth, reach, width), lambda t: (0, 0, t)),
+            pl.BlockSpec((depth, reach, width), lambda t: (0, 0, t)),
         ],
         out_specs=[tile] * 4,
         out_shape=[shape] * 4,
         compiler_params=pltpu.CompilerParams(vmem_limit_bytes=vmem_bytes),
-        cost_estimate=pl.CostEstimate(
-            flops=100 * scalar.size, bytes_accessed=24 * scalar.size, transcendentals=0
-        ),
+        cost_estimate=light,
         name="inner",
-    )(scalar, scalar, scalar, before, after, outer_rows)
+    )(scalar, scalar, scalar, top, bottom)
 
 
 def outer_kernel(above, part_ref, fine_ref, halo_ref, out_ref):
@@ -310,25 +346,93 @@
         out_ref[p] = part_ref[p] + (fine_ref[p] * grade + curve)
 
 
-def outer_call(above, part, fine, halo):
+def outer_call(above, part, fine, halo, begin):
     depth, rows, points = part.shape
+    width = halo.shape[2]
     half = depth // reach - 1 if above else 0
-    steps = 4
-    width = points // steps if points % (steps * lanes) == 0 else points
-    block = pl.BlockSpec((reach, rows, width), lambda t: (half, 0, t))
+    step_width = math.gcd(width, max(begin, width), 512)
+    steps = width // step_width
+    block = pl.BlockSpec((reach, rows, step_width), lambda t: (half, 0, begin // step_width + t))
     return pl.pallas_call(
         functools.partial(outer_kernel, above),
-        grid=(points // width,),
-        in_specs=[block, block, pl.BlockSpec((reach, rows, width), lambda t: (0, 0, t))],
+        grid=(steps,),
+        in_specs=[block, block, pl.BlockSpec((reach, rows, step_width), lambda t: (0, 0, t))],
         out_specs=block,
         out_shape=jax.ShapeDtypeStruct(part.shape, jnp.float32),
         input_output_aliases={0: 0},
         compiler_params=pltpu.CompilerParams(vmem_limit_bytes=vmem_bytes),
-        cost_estimate=pl.CostEstimate(
-            flops=50 * halo.size, bytes_accessed=16 * halo.size, transcendentals=0
-        ),
+        cost_estimate=light,
         name="outer",
     )(part, fine, halo)
+
+
+def tie(value, *gates):
+    anywhere = pl.BlockSpec(memory_space=pl.ANY)
+    return pl.pallas_call(
+        lambda *refs: None,
+        in_specs=[anywhere] * (1 + len(gates)),
+        out_specs=anywhere,
+        out_shape=jax.ShapeDtypeStruct(value.shape, value.dtype),
+        input_output_aliases={0: 0},
+        cost_estimate=light,
+        name="tie",
+    )(value, *gates)
+
+
+def pack_kernel(own_ref, first_ref, last_ref, *refs):
+    outs = refs[-len(refs) :]
+    kinds, rows, cells = own_ref.shape
+    part = rows // len(outs)
+    lines = kinds * part
+    first = first_ref[...].reshape(rows, lanes).T
+    last = last_ref[...].reshape(rows, lanes).T
+    for h, out in enumerate(outs):
+        span = slice(h * part, (h + 1) * part)
+        out[:lines] = own_ref[:, span].reshape(lines, cells)
+        ends = jnp.concatenate([first[:reach, span], last[lanes - reach :, span]], axis=0)
+        out[lines:, :part] = ends
+        if part < cells:
+            out[lines:, part:] = jnp.zeros((2 * reach, cells - part), jnp.float32)
+
+
+def pack_call(own, scalar, shares):
+    kinds, rows, cells = own.shape
+    depth, height, points = scalar.shape
+    end = points // lanes - 1
+    shape = jax.ShapeDtypeStruct((kinds * (rows // shares) + 2 * reach, cells), jnp.float32)
+    return pl.pallas_call(
+        pack_kernel,
+        grid=(1,),
+        in_specs=[
+            pl.BlockSpec(own.shape, lambda t: (0, 0, 0)),
+            pl.BlockSpec((depth, height, lanes), lambda t: (0, 0, 0)),
+            pl.BlockSpec((depth, height, lanes), lambda t: (0, 0, end)),
+        ],
+        out_specs=[pl.BlockSpec(shape.shape, lambda t: (0, 0))] * shares,
+        out_shape=[shape] * shares,
+        cost_estimate=light,
+        name="pack",
+    )(own, scalar, scalar)
+
+
+def piece_kernel(source_ref, *refs):
+    refs[-1][...] = source_ref[...]
+
+
+def piece_call(source, begin, size, gates=()):
+    points = source.shape[2]
+    width = math.gcd(points, 512)
+    shape = (size,) + source.shape[1:]
+    return pl.pallas_call(
+        piece_kernel,
+        grid=(points // width,),
+        in_specs=[pl.BlockSpec(shape[:2] + (width,), lambda t: (begin // size, 0, t))]
+        + [pl.BlockSpec(memory_space=pl.ANY)] * len(gates),
+        out_specs=pl.BlockSpec(shape[:2] + (width,), lambda t: (0, 0, t)),
+        out_shape=jax.ShapeDtypeStruct(shape, source.dtype),
+        cost_estimate=light,
+        name="piece",
+    )(source, *gates)
 
 
 def general_segment(rows_of_x, block, length):
@@ -372,52 +476,49 @@
     length = cells * count
     block = lax.axis_index("blk")
 
-    lower = lax.ppermute(scalar[-reach:], "dep", ring("dep", 1))
-    upper = lax.ppermute(scalar[:reach], "dep", ring("dep", -1))
+    lower = lax.ppermute(piece_call(scalar, depth - reach, reach), "dep", ring("dep", 1))
+    upper = lax.ppermute(piece_call(scalar, 0, reach), "dep", ring("dep", -1))
+    top = lax.ppermute(scalar[:, :reach], "grp", ring("grp", -1))
+    bottom = lax.ppermute(scalar[:, -reach:], "grp", ring("grp", 1))
     rows_of_x = jnp.transpose(velocity, (0, 2, 3, 1)).reshape(kinds, rows, cells)
-
-    fast = count == 4 and cells % lanes == 0
-    if fast:
-        chip = lax.ppermute(rows_of_x, "blk", exclusive("blk", 2))
-        core = lax.ppermute(rows_of_x, "blk", exclusive("blk", 1))
-    if lax.axis_size("grp") == 2:
-        edges = jnp.concatenate([scalar[:, :reach], scalar[:, -reach:]], axis=1)
-        outer_rows = lax.ppermute(edges, "grp", ring("grp", 1))
-    else:
-        outer_rows = jnp.concatenate(
-            [
-                lax.ppermute(scalar[:, :reach], "grp", ring("grp", -1)),
-                lax.ppermute(scalar[:, -reach:], "grp", ring("grp", 1)),
-            ],
-            axis=1,
-        )
-    before = lax.ppermute(scalar[:, :, -lanes:], "blk", ring("blk", 1))
-    after = lax.ppermute(scalar[:, :, :lanes], "blk", ring("blk", -1))
-
-    gx, gy, gz, base = inner_call(scalar, before, after, outer_rows)
     local_base = spline_base - block * cells
     flat = (rows, points)
-    if fast:
+
+    shares = 1
+    if count == 4 and cells % lanes == 0 and rows // shares <= cells:
+        own = pack_call(rows_of_x, scalar, shares)
+        chip = [lax.ppermute(part, "blk", exclusive("blk", 2)) for part in own]
+        core = [lax.ppermute(part, "blk", exclusive("blk", 1)) for part in own]
+        fields = inner_call(scalar, top, bottom)
         matrix = spline_matrix(local_base, spline_frac, cells, points // cells)
-        diagonal = lax.ppermute(chip, "blk", exclusive("blk", 1))
+        chip = [tie(part, fields[3]) for part in chip]
+        diagonal = [lax.ppermute(part, "blk", exclusive("blk", 1)) for part in chip]
         info = jnp.stack([(block - (block ^ j)) % count for j in range(4)] + [block % 2])
-        main, outer = segment_call([rows_of_x, core, chip, diagonal], info.astype(jnp.int32), length)
+        info = info.astype(jnp.int32)
+        main, outer = segment_call(rows_of_x, core, chip, diagonal, info, length)
         part, vertical = combine_call(
-            main, outer, matrix, gx.reshape(flat), gy.reshape(flat), gz.reshape(flat), base.reshape(flat)
+            main, outer, matrix, *[field.reshape(flat) for field in fields], core, diagonal, info[4:]
         )
     else:
+        before = lax.ppermute(scalar[:, :, -reach:], "blk", ring("blk", 1)).reshape(rows, reach)
+        after = lax.ppermute(scalar[:, :, :reach], "blk", ring("blk", -1)).reshape(rows, reach)
+        gx, gy, gz, base = [field.reshape(flat) for field in inner_call(scalar, top, bottom)]
+        wide = jnp.concatenate([before, jnp.zeros(flat, jnp.float32), after], axis=1)
+        for m in range(1, reach + 1):
+            ahead = lax.slice_in_dim(wide, reach + m, reach + m + points, axis=1)
+            behind = lax.slice_in_dim(wide, reach - m, reach - m + points, axis=1)
+            gx = gx + slope[m - 1] * (ahead - behind)
+            base = base + bend[m - 1] * (ahead + behind)
         wide = general_segment(rows_of_x, block, length)
         main = wide[..., 2:-2]
         fine = general_fine(wide, local_base, spline_frac)
         vertical = fine[2]
-        part = base.reshape(flat) + (
-            fine[0] * gx.reshape(flat) + fine[1] * gy.reshape(flat) + vertical * gz.reshape(flat)
-        )
+        part = base + (fine[0] * gx + fine[1] * gy + vertical * gz)
     part, vertical = part.reshape(scalar.shape), vertical.reshape(scalar.shape)
-    part = outer_call(False, part, vertical, lower)
-    result = outer_call(True, part, vertical, upper)
+    part = outer_call(False, part, vertical, lower, 0)
+    part = outer_call(True, part, vertical, upper, 0)
     segment = jnp.transpose(main.reshape(kinds, depth, height, cells), (0, 3, 1, 2))
-    return segment, result
+    return segment, part
 
 
 def solution(mesh):

time: 77.3 us -> 67.9 us (0.88)
  waiting for transfers between devices: 22.1 us -> 2.98 us
  Pallas kernels: 31.3 us -> 44.7 us
  local copies, waits for them, and re-layouts: 9.4 us -> 6.28 us
    ppermute x8 -> x7, waiting for transfers between devices: 22.1 us -> 2.98 us  [the longest x1 2.93 us: per_device(): upper = lax.ppermute(piece_call(scalar, 0, reach), 'dep', ring('dep', -1))]
    pallas_call x4 -> x8, Pallas kernels: 21 us -> 34.5 us  [the longest x1 9.22 us: combine_call(): pl.pallas_call(functools.partial(combine_kernel, cells // lanes, shares),...]
    slice x3 -> x1, local copies, waits for them, and re-layouts: 5.45 us -> 2 us  [per_device(): bottom = lax.ppermute(scalar[:, -reach:], 'grp', ring('grp', 1))]
    select_n x1, other arithmetic: 1.31 us -> 2.66 us  [spline_matrix(): matrix = jnp.where(gap == tap - 1, weight[None, :], matrix)]
    concatenate x1 -> x0, other arithmetic: 0.9 us -> none  [per_device(): edges = jnp.concatenate([scalar[:, :reach], scalar[:, -reach:]], axis=1)]
    ppermute x8 -> x7, starting transfers between devices: 10.1 us -> 9.36 us  [the longest x1 2.94 us: per_device(): chip = [lax.ppermute(part, 'blk', exclusive('blk', 2)) for part in own]]
  transfers between devices with their start and end apart: 8 -> 7, of which waited for: 3 -> 1; matrix products, arithmetic and copies ran while one was open for 10% -> 8% of each run, Pallas kernels for 37% -> 58%
where the time goes in v2:
time: 67.9 us; the launch traced here: 66.7 us
  Pallas kernels  44.7 us (66%)
  starting transfers between devices  9.36 us (14%)
  local copies, waits for them, and re-layouts  6.28 us (9%)
  waiting for transfers between devices  2.98 us (4%)
  other arithmetic  2.7 us (4%)
  between operations  0.69 us (1%)
    pallas_call x1, Pallas kernels, inner_call(): pl.pallas_call(functools.partial(inner_kernel, steps), grid=(steps,), in_...  10.2 us
    pallas_call x1, Pallas kernels, combine_call(): pl.pallas_call(functools.partial(combine_kernel, cells // lanes, shares),...  9.22 us
    pallas_call x1, Pallas kernels, segment_call(): pl.pallas_call(functools.partial(segment_kernel, length, shares), grid_sp...  8.43 us
    pallas_call x2, Pallas kernels, outer_call(): pl.pallas_call(functools.partial(outer_kernel, above), grid=(steps,), in_...  7.78 us
    pallas_call x2, Pallas kernels, piece_call(): pl.pallas_call(piece_kernel, grid=(points // width,), in_specs=[pl.BlockS...  6.81 us
    unnamed x14, local copies, waits for them, and re-layouts  3.65 us
    ppermute x1, starting transfers between devices, per_device(): chip = [lax.ppermute(part, 'blk', exclusive('blk', 2)) for part in own]  2.94 us
    ppermute x1, waiting for transfers between devices, per_device(): upper = lax.ppermute(piece_call(scalar, 0, reach), 'dep', ring('dep', -1))  2.93 us
  transfers between devices with their start and end apart: 7, of which 1 were waited for; matrix products, arithmetic and copies ran while one was open for 8% of the time, Pallas kernels for 58%

profile of v2, /device:TPU:0, one launch (start us, length us, event | category | flops | bytes accessed | tf_op | source)
XLA Modules:
  0.0 66.7 jit_solution(8346958103552934294)
XLA Ops:
  0.6 2.2 %pack.1 = f32[776,256]{1,0:T(8,128)} custom-call(f32[3,256,256]{2,1,0:T(8,128)} %bitcast.20, f32[8,32,2048]{2,1,0:T(8,128)} %source_ref.3, f32[8,32,2048]{2,1,0:T(8,128)} %source_ref.3), custom_call_target="tpu_custom_call" | custom-call | flops 1024 | bytes 1024 | tf_op jit(solution)/shard_map/pack/pallas_call | solution.py:403
  2.9 2.9 %collective-permute-start.1 = (f32[776,256]{1,0:T(8,128)}, f32[776,256]{1,0:T(8,128)S(1)}, u32[]{:S(2)}, u32[]{:S(2)}) collective-permute-start(f32[776,256]{1,0:T(8,128)} %pack.1), channel_id=1, source_target_pairs={{0,8},{4,12},{8,0},{12,4},{1,9},{5,13},{9,1},{13,5},{2,10},{6,14},... | collective-permute-start | bytes 2383880 | tf_op jit(solution)/shard_map/ppermute | solution.py:490
  5.8 2.0 %fusion.30 = (f32[8,4,2048]{2,1,0:T(4,128)}, f32[8,4,2048]{2,1,0:T(4,128)S(1)}) fusion(f32[8,32,2048]{2,1,0:T(8,128)} %source_ref.3), kind=kLoop, calls=%fused_computation.53 | loop fusion | bytes 1048576 | tf_op jit(solution)/shard_map/slice | solution.py:482
  7.8 1.5 %collective-permute-start.2 = (f32[8,4,2048]{2,1,0:T(4,128)S(1)}, f32[8,4,2048]{2,1,0:T(4,128)}, u32[]{:S(2)}, u32[]{:S(2)}) collective-permute-start(f32[8,4,2048]{2,1,0:T(4,128)S(1)} %get-tuple-element.19), channel_id=1, source_target_pairs={{0,16},{16,0},{1,17},{17,1},{2,18},{18,2},{3,19},{19,3},{4,20},{20... | collective-permute-start | bytes 786440 | tf_op jit(solution)/shard_map/ppermute | solution.py:481
  9.3 0.5 collective-permute-start.3
  9.8 3.4 %piece.2 = f32[4,32,2048]{2,1,0:T(8,128)} custom-call(f32[8,32,2048]{2,1,0:T(8,128)} %source_ref.3), custom_call_target="tpu_custom_call" | custom-call | flops 1024 | bytes 1024 | tf_op jit(solution)/shard_map/piece/pallas_call | solution.py:426
  13.2 0.0 copy-start.5
  13.2 0.0 copy-start.4
  13.2 1.6 %collective-permute-start.5 = (f32[4,32,2048]{2,1,0:T(8,128)}, f32[4,32,2048]{2,1,0:T(8,128)}, u32[]{:S(2)}, u32[]{:S(2)}) collective-permute-start(f32[4,32,2048]{2,1,0:T(8,128)} %piece.2), channel_id=1, source_target_pairs={{0,1},{1,2},{2,3},{3,0},{4,5},{5,6},{6,7},{7,4},{8,9},{9,10},{10,1... | collective-permute-start | bytes 3145736 | tf_op jit(solution)/shard_map/ppermute | solution.py:479
  14.8 3.4 %piece.3 = f32[4,32,2048]{2,1,0:T(8,128)} custom-call(f32[8,32,2048]{2,1,0:T(8,128)} %source_ref.3), custom_call_target="tpu_custom_call" | custom-call | flops 1024 | bytes 1024 | tf_op jit(solution)/shard_map/piece/pallas_call | solution.py:426
  18.2 2.3 %collective-permute-start.6 = (f32[4,32,2048]{2,1,0:T(8,128)}, f32[4,32,2048]{2,1,0:T(8,128)S(1)}, u32[]{:S(2)}, u32[]{:S(2)}) collective-permute-start(f32[4,32,2048]{2,1,0:T(8,128)} %piece.3), channel_id=1, source_target_pairs={{0,3},{1,0},{2,1},{3,2},{4,7},{5,4},{6,5},{7,6},{8,11},{9,8},{10,9... | collective-permute-start | bytes 3145736 | tf_op jit(solution)/shard_map/ppermute | solution.py:480
  20.5 0.6 stack.20.info
  21.1 0.0 copy-done.5
  21.2 0.0 collective-permute-done.2.top_ref
  21.2 0.0 copy-done.4
  21.2 0.1 collective-permute-start
  21.3 0.0 collective-permute-done.3.bottom_ref
  21.3 10.2 %inner.1 = (f32[8,32,2048]{2,1,0:T(8,128)}, f32[8,32,2048]{2,1,0:T(8,128)}, f32[8,32,2048]{2,1,0:T(8,128)}, f32[8,32,2048]{2,1,0:T(8,128)}) custom-call(f32[8,32,2048]{2,1,0:T(8,128)} %source_ref.3, f32[8,32,2048]{2,1,0:T(8,128)} %source_ref.3, f32[8,32,2048]{2,1,0:T(8,128)} %source_ref.3, f32[8,4,2048]{2,1,0:T(4,128)} %collective-permute-done.2.top_ref, ...), custom_call_target="tpu_custom_call" | custom-call | flops 1024 | bytes 1024 | tf_op jit(solution)/shard_map/inner/pallas_call | solution.py:317
  31.5 0.0 copy-start.6
  31.5 0.0 collective-permute-done.1.refs_0_
  31.5 0.0 copy-start.2
  31.5 0.9 %copy-done.2 = f32[776,256]{1,0:T(8,128)} copy-done((f32[776,256]{1,0:T(8,128)}, f32[776,256]{1,0:T(8,128)S(1)}, u32[]{:S(2)}) %copy-start.2) | copy-done | bytes 794648
  32.4 0.5 collective-permute-start.4
  32.8 0.0 copy-done.6
  32.9 2.7 %select_select_fusion.matrix_ref = f32[256,2048]{1,0:T(8,128)} fusion(f32[2048]{0:T(1024)S(1)} %get-tuple-element.22, f32[2048]{0:T(1024)S(1)} %get-tuple-element.21, f32[2048]{0:T(1024)S(1)} %get-tuple-element.23, f32[2048]{0:T(1024)S(1)} %get-tuple-element.20, s32[2048]{0:T(1024)S(1)} %get-tuple-element.25, s32[2048]{0:T(1024)S(1)} %get-tuple-element.24, ...), kind=kLoop, calls=%fused_computation.10 | loop fusion | flops 8388608 | bytes 2154752 | tf_op jit(solution)/shard_map/jit(_where)/select_n | solution.py:162
  35.5 0.0 collective-permute-done.refs_0_
  35.5 0.0 copy-start
  35.5 0.0 collective-permute-done.4.refs_2_.refs_1_
  35.5 0.9 %copy-done = f32[776,256]{1,0:T(8,128)} copy-done((f32[776,256]{1,0:T(8,128)}, f32[776,256]{1,0:T(8,128)S(1)}, u32[]{:S(2)}) %copy-start) | copy-done | bytes 794648
  36.4 0.0 copy-start.1
  36.4 0.9 %copy-done.1 = f32[776,256]{1,0:T(8,128)} copy-done((f32[776,256]{1,0:T(8,128)}, f32[776,256]{1,0:T(8,128)S(1)}, u32[]{:S(2)}) %copy-start.1) | copy-done | bytes 794648
  37.3 8.4 %segment.1 = (f32[3,256,256]{2,1,0:T(8,128)}, f32[3,256,128]{2,1,0:T(8,128)}) custom-call(s32[5]{0:T(128)} %stack.20.info, f32[3,256,256]{2,1,0:T(8,128)} %bitcast.21, f32[776,256]{1,0:T(8,128)} %copy-done, f32[776,256]{1,0:T(8,128)} %tie.1.refs_1_, f32[776,256]{1,0:T(8,128)} %copy-done.1, ...), custom_call_target="tpu_custom_call" | custom-call | flops 1024 | bytes 1024 | tf_op jit(solution)/shard_map/segment/pallas_call | solution.py:122
  45.8 9.2 %combine.1 = (f32[256,2048]{1,0:T(8,128)}, f32[256,2048]{1,0:T(8,128)}) custom-call(s32[1]{0:T(128)} %bitcast.3.parity, f32[3,256,256]{2,1,0:T(8,128)} %get-tuple-element.11.main_ref, f32[3,256,128]{2,1,0:T(8,128)} %get-tuple-element.12.outer_ref, f32[256,2048]{1,0:T(8,128)} %select_select_fusion.matrix_ref, f32[256,2048]{1,0:T(8,128)} %bitcast.22, ...), custom_call_target="tpu_custom_call" | custom-call | flops 1024 | bytes 1024 | tf_op jit(solution)/shard_map/combine/pallas_call | solution.py:235
  55.0 0.0 collective-permute-done.5.halo_ref
  55.0 3.9 %outer.2.part_ref = f32[8,32,2048]{2,1,0:T(8,128)} custom-call(f32[8,32,2048]{2,1,0:T(8,128)} %bitcast.19, f32[8,32,2048]{2,1,0:T(8,128)} %bitcast.17, f32[4,32,2048]{2,1,0:T(8,128)} %collective-permute-done.5.halo_ref), custom_call_target="tpu_custom_call", output_to_operand_aliasing={{}: (0, {})} | custom-call | flops 1024 | bytes 1024 | tf_op jit(solution)/shard_map/outer/pallas_call | solution.py:356
  58.9 2.9 %collective-permute-done.6.halo_ref = f32[4,32,2048]{2,1,0:T(8,128)S(1)} collective-permute-done((f32[4,32,2048]{2,1,0:T(8,128)}, f32[4,32,2048]{2,1,0:T(8,128)S(1)}, u32[]{:S(2)}, u32[]{:S(2)}) %collective-permute-start.6) | collective-permute-done | bytes 1048608 | tf_op jit(solution)/shard_map/ppermute | solution.py:480
  61.8 0.0 copy-start.3
  61.8 1.0 %copy-done.3 = f32[4,32,2048]{2,1,0:T(8,128)} copy-done((f32[4,32,2048]{2,1,0:T(8,128)}, f32[4,32,2048]{2,1,0:T(8,128)S(1)}, u32[]{:S(2)}) %copy-start.3) | copy-done | bytes 1048600
  62.8 3.9 %outer.3 = f32[8,32,2048]{2,1,0:T(8,128)} custom-call(f32[8,32,2048]{2,1,0:T(8,128)} %outer.2.part_ref, f32[8,32,2048]{2,1,0:T(8,128)} %bitcast.18, f32[4,32,2048]{2,1,0:T(8,128)} %copy-done.3), custom_call_target="tpu_custom_call", output_to_operand_aliasing={{}: (0, {})} | custom-call | flops 1024 | bytes 1024 | tf_op jit(solution)/shard_map/outer/pallas_call | solution.py:356
  (5 shorter events, 0.0 us)
Async XLA Ops:
  2.9 28.6 %collective-permute-start.1 = (f32[776,256]{1,0:T(8,128)}, f32[776,256]{1,0:T(8,128)S(1)}, u32[]{:S(2)}, u32[]{:S(2)}) collective-permute-start(f32[776,256]{1,0:T(8,128)} %pack.1), channel_id=1, source_target_pairs={{0,8},{4,12},{8,0},{12,4},{1,9},{5,13},{9,1},{13,5},{2,10},{6,14},... | collective-permute-start | bytes 2383880 | tf_op jit(solution)/shard_map/ppermute | solution.py:490
  7.8 13.4 %collective-permute-start.2 = (f32[8,4,2048]{2,1,0:T(4,128)S(1)}, f32[8,4,2048]{2,1,0:T(4,128)}, u32[]{:S(2)}, u32[]{:S(2)}) collective-permute-start(f32[8,4,2048]{2,1,0:T(4,128)S(1)} %get-tuple-element.19), channel_id=1, source_target_pairs={{0,16},{16,0},{1,17},{17,1},{2,18},{18,2},{3,19},{19,3},{4,20},{20... | collective-permute-start | bytes 786440 | tf_op jit(solution)/shard_map/ppermute | solution.py:481
  9.3 12.0 %collective-permute-start.3 = (f32[8,4,2048]{2,1,0:T(4,128)}, f32[8,4,2048]{2,1,0:T(4,128)}, u32[]{:S(2)}, u32[]{:S(2)}) collective-permute-start(f32[8,4,2048]{2,1,0:T(4,128)} %get-tuple-element.18), channel_id=1, source_target_pairs={{0,16},{16,0},{1,17},{17,1},{2,18},{18,2},{3,19},{19,3},{4,20},{20... | collective-permute-start | bytes 786440 | tf_op jit(solution)/shard_map/ppermute | solution.py:482
  13.2 7.9 %copy-start.5 = (s32[2048]{0:T(1024)S(1)}, s32[2048]{0:T(1024)}, u32[]{:S(2)}) copy-start(s32[2048]{0:T(1024)} %param.8) | copy-start | bytes 24580
  13.2 8.0 %copy-start.4 = (f32[776,256]{1,0:T(8,128)S(1)}, f32[776,256]{1,0:T(8,128)}, u32[]{:S(2)}) copy-start(f32[776,256]{1,0:T(8,128)} %pack.1) | copy-start | bytes 2383876
  13.2 41.8 %collective-permute-start.5 = (f32[4,32,2048]{2,1,0:T(8,128)}, f32[4,32,2048]{2,1,0:T(8,128)}, u32[]{:S(2)}, u32[]{:S(2)}) collective-permute-start(f32[4,32,2048]{2,1,0:T(8,128)} %piece.2), channel_id=1, source_target_pairs={{0,1},{1,2},{2,3},{3,0},{4,5},{5,6},{6,7},{7,4},{8,9},{9,10},{10,1... | collective-permute-start | bytes 3145736 | tf_op jit(solution)/shard_map/ppermute | solution.py:479
  18.2 43.6 %collective-permute-start.6 = (f32[4,32,2048]{2,1,0:T(8,128)}, f32[4,32,2048]{2,1,0:T(8,128)S(1)}, u32[]{:S(2)}, u32[]{:S(2)}) collective-permute-start(f32[4,32,2048]{2,1,0:T(8,128)} %piece.3), channel_id=1, source_target_pairs={{0,3},{1,0},{2,1},{3,2},{4,7},{5,4},{6,5},{7,6},{8,11},{9,8},{10,9... | collective-permute-start | bytes 3145736 | tf_op jit(solution)/shard_map/ppermute | solution.py:480
  21.2 14.3 %collective-permute-start = (f32[776,256]{1,0:T(8,128)S(1)}, f32[776,256]{1,0:T(8,128)S(1)}, u32[]{:S(2)}, u32[]{:S(2)}) collective-permute-start(f32[776,256]{1,0:T(8,128)S(1)} %copy-done.4), channel_id=1, source_target_pairs={{0,4},{4,0},{8,12},{12,8},{1,5},{5,1},{9,13},{13,9},{2,6},{6,2},{1... | collective-permute-start | bytes 2383880 | tf_op jit(solution)/shard_map/ppermute | solution.py:491
  31.5 1.4 %copy-start.6 = (f32[2048]{0:T(1024)S(1)}, f32[2048]{0:T(1024)}, u32[]{:S(2)}) copy-start(f32[2048]{0:T(1024)} %param.9) | copy-start | bytes 24580
  31.5 0.9 %copy-start.2 = (f32[776,256]{1,0:T(8,128)}, f32[776,256]{1,0:T(8,128)S(1)}, u32[]{:S(2)}) copy-start(f32[776,256]{1,0:T(8,128)S(1)} %collective-permute-done.1.refs_0_) | copy-start | bytes 2383876
  32.4 3.2 %collective-permute-start.4 = (f32[776,256]{1,0:T(8,128)}, f32[776,256]{1,0:T(8,128)S(1)}, u32[]{:S(2)}, u32[]{:S(2)}) collective-permute-start(f32[776,256]{1,0:T(8,128)} %tie.1.refs_1_), channel_id=1, source_target_pairs={{0,4},{4,0},{8,12},{12,8},{1,5},{5,1},{9,13},{13,9},{2,6},{6,2},{1... | collective-permute-start | bytes 2383880 | tf_op jit(solution)/shard_map/ppermute | solution.py:495
  35.5 0.9 %copy-start = (f32[776,256]{1,0:T(8,128)}, f32[776,256]{1,0:T(8,128)S(1)}, u32[]{:S(2)}) copy-start(f32[776,256]{1,0:T(8,128)S(1)} %collective-permute-done.refs_0_) | copy-start | bytes 2383876
  36.4 0.9 %copy-start.1 = (f32[776,256]{1,0:T(8,128)}, f32[776,256]{1,0:T(8,128)S(1)}, u32[]{:S(2)}) copy-start(f32[776,256]{1,0:T(8,128)S(1)} %collective-permute-done.4.refs_2_.refs_1_) | copy-start | bytes 2383876
  61.8 1.0 %copy-start.3 = (f32[4,32,2048]{2,1,0:T(8,128)}, f32[4,32,2048]{2,1,0:T(8,128)S(1)}, u32[]{:S(2)}) copy-start(f32[4,32,2048]{2,1,0:T(8,128)S(1)} %collective-permute-done.6.halo_ref) | copy-start | bytes 3145732

commit v3 on v0

--- a/solution.py
+++ b/solution.py
@@ -1,27 +1,451 @@
+import functools
 import math
 
 import jax
 import jax.numpy as jnp
+import ml_dtypes
+import numpy as np
 from jax import lax
+from jax.experimental import pallas as pl
+from jax.experimental.pallas import tpu as pltpu
 from jax.sharding import PartitionSpec as P
 
 velocity_step = 0.002
 viscosity = 0.00125
 advect_rate = 0.2
 diffuse_rate = 0.05
-first_coeffs = (1.0 / 280.0, -4.0 / 105.0, 0.2, -0.8, 0.0, 0.8, -0.2, 4.0 / 105.0, -1.0 / 280.0)
-second_coeffs = (
-    -1.0 / 560.0,
-    8.0 / 315.0,
-    -0.2,
-    1.6,
-    -205.0 / 72.0,
-    1.6,
-    -0.2,
-    8.0 / 315.0,
-    -1.0 / 560.0,
-)
+first_side = (0.8, -0.2, 4.0 / 105.0, -1.0 / 280.0)
+second_side = (1.6, -0.2, 8.0 / 315.0, -1.0 / 560.0)
+second_centre = -205.0 / 72.0
+first_all = tuple(-a for a in reversed(first_side)) + (0.0,) + first_side
+second_all = tuple(reversed(second_side)) + (second_centre,) + second_side
+slope = tuple(-advect_rate * a for a in first_side)
+bend = tuple(diffuse_rate * b for b in second_side)
+centre_weight = 1.0 + 3.0 * diffuse_rate * second_centre
 highest = lax.Precision.HIGHEST
+reach = 4
+lanes = 128
+vmem_bytes = 32 * 1024 * 1024
+most_vmem_bytes = 60 * 1024 * 1024
+light = pl.CostEstimate(flops=1024, bytes_accessed=1024, transcendentals=0)
+
+
+def ring(axis, step):
+    count = lax.axis_size(axis)
+    return [(i, (i + step) % count) for i in range(count)]
+
+
+def exclusive(axis, mask):
+    return [(i, i ^ mask) for i in range(lax.axis_size(axis))]
+
+
+def split_table(values):
+    high = values.astype(np.float32).astype(ml_dtypes.bfloat16)
+    low = (values - high.astype(np.float64)).astype(np.float32).astype(ml_dtypes.bfloat16)
+    return high, low
+
+
+def right_table(values):
+    high, low = split_table(values)
+    return np.concatenate([high, high, low], axis=-2)
+
+
+def circulant_tables(length, cells):
+    s = np.arange(length)
+    signed = np.where(s > length // 2, s - length, s)
+    angle = signed * (np.pi / length)
+    sine = np.where(s == 0, 1.0, np.sin(angle))
+    parity = 1.0 - 2.0 * (s % 2)
+    first = np.where(s == 0, 0.0, 0.5 * parity * np.cos(angle) / sine) * velocity_step
+    second = np.where(s == 0, -(length * length) / 12.0 - 1.0 / 6.0, -0.5 * parity / (sine * sine))
+    second = second * (velocity_step * viscosity)
+    own = np.arange(cells)
+    outer = np.zeros(lanes, np.int64)
+    used = np.zeros(lanes)
+    for lane, cell in ((0, cells), (1, cells + 1), (lanes - 2, -2), (lanes - 1, -1)):
+        outer[lane] = cell
+        used[lane] = 1.0
+    blocks = []
+    for distance in range(length // cells):
+        main = (distance * cells + own[None, :] - own[:, None]) % length
+        side = (distance * cells + outer[None, :] - own[:, None]) % length
+        blocks.append(
+            np.concatenate([first[main], second[main], first[side] * used, second[side] * used], axis=1)
+        )
+    return right_table(np.stack(blocks))
+
+
+def level_table(depth, height):
+    size, side = depth * height, 2 * reach
+    table = np.zeros((3, depth, height, size + depth * side))
+    for z in range(depth):
+        for y in range(height):
+            for m in range(-reach, reach + 1):
+                if m == 0:
+                    continue
+                first = slope[m - 1] if m > 0 else -slope[-m - 1]
+                second = bend[abs(m) - 1]
+                if 0 <= y + m < height:
+                    at = z * height + y + m
+                else:
+                    at = size + z * side + (y + m - height if m > 0 else y + m + side)
+                table[0, z, y, at] += first
+                table[2, z, y, at] += second
+                if 0 <= z + m < depth:
+                    table[1, z, y, (z + m) * height + y] += first
+                    table[2, z, y, (z + m) * height + y] += second
+    high, low = split_table(table.reshape(3 * size, -1))
+    return np.concatenate([high, high, low], axis=1)
+
+
+def dot(a, b):
+    return jnp.dot(a, b, preferred_element_type=jnp.float32)
+
+
+def split(value):
+    high = value.astype(jnp.bfloat16)
+    return high, (value - high.astype(jnp.float32)).astype(jnp.bfloat16)
+
+
+def left_operand(value):
+    high, low = split(value)
+    return jnp.concatenate([high, low, high], axis=1)
+
+
+def segment_kernel(length, info, own_ref, core_ref, chip_ref, far_ref, *refs):
+    table_refs, (main_ref, outer_ref) = refs[:4], refs[4:]
+    kinds, rows, cells = own_ref.shape
+    lines = kinds * rows
+    blocks = [own_ref[...].reshape(lines, cells)] + [ref[:lines] for ref in (core_ref, chip_ref, far_ref)]
+    total = sums = None
+    for block, table_ref in zip(blocks, table_refs):
+        product = dot(left_operand(block), table_ref[0])
+        partial = jnp.sum(block, axis=1, keepdims=True)
+        total = product if total is None else total + product
+        sums = partial if sums is None else sums + partial
+    mean = sums * (1.0 / length)
+    even = info[4] == 0
+    after = jnp.where(even, blocks[1][:, :lanes], blocks[3][:, :lanes])
+    before = jnp.where(even, blocks[3][:, cells - lanes :], blocks[1][:, cells - lanes :])
+    place = lax.broadcasted_iota(jnp.int32, after.shape, 1)
+    outer = jnp.where(place < lanes // 2, after, before)
+
+    def advance(own, first, second):
+        lead = jnp.concatenate([own[:rows]] * kinds, axis=0)
+        return own - mean + (second - lead * first)
+
+    main = advance(blocks[0], total[:, :cells], total[:, cells : 2 * cells])
+    side = advance(outer, total[:, 2 * cells : 2 * cells + lanes], total[:, 2 * cells + lanes :])
+    main_ref[...] = main.reshape(kinds, rows, cells)
+    outer_ref[...] = side.reshape(kinds, rows, lanes)
+
+
+def segment_call(own, core, chip, diagonal, info, length):
+    kinds, rows, cells = own.shape
+    table = circulant_tables(length, cells)
+    whole = pl.BlockSpec(own.shape, lambda g, info: (0, 0, 0))
+    sent = pl.BlockSpec(core.shape, lambda g, info: (0, 0))
+    tables = [
+        pl.BlockSpec((1,) + table.shape[1:], functools.partial(lambda j, g, info: (info[j], 0, 0), j))
+        for j in range(4)
+    ]
+    return pl.pallas_call(
+        functools.partial(segment_kernel, length),
+        grid_spec=pltpu.PrefetchScalarGridSpec(
+            num_scalar_prefetch=1,
+            grid=(1,),
+            in_specs=[whole] + [sent] * 3 + tables,
+            out_specs=[whole, pl.BlockSpec((kinds, rows, lanes), lambda g, info: (0, 0, 0))],
+        ),
+        out_shape=[
+            jax.ShapeDtypeStruct((kinds, rows, cells), jnp.float32),
+            jax.ShapeDtypeStruct((kinds, rows, lanes), jnp.float32),
+        ],
+        compiler_params=pltpu.CompilerParams(vmem_limit_bytes=vmem_bytes),
+        cost_estimate=light,
+        name="segment",
+    )(info, own, core, chip, diagonal, *([jnp.asarray(table)] * 4))
+
+
+def catmull_weights(fraction):
+    square = fraction * fraction
+    cube = square * fraction
+    return (
+        (-cube + 2.0 * square - fraction) * 0.5,
+        (3.0 * cube - 5.0 * square + 2.0) * 0.5,
+        (-3.0 * cube + 4.0 * square + fraction) * 0.5,
+        (cube - square) * 0.5,
+    )
+
+
+def spline_matrix(local_base, fraction, cells, refine):
+    tiles = cells // lanes
+    row = lax.iota(jnp.int32, 2 * lanes)[:, None]
+    half = (lax.iota(jnp.int32, local_base.shape[0]) // (refine * (lanes // 2)))[None, :]
+    own = half // 2
+    other = (own + jnp.where(half % 2 == 1, 1, tiles)) % (tiles + 1)
+    lane = jnp.where(row < lanes, own * lanes + row, other * lanes + row - lanes)
+    cell = jnp.where(lane < cells + lanes // 2, lane, lane - cells - lanes)
+    gap = cell - local_base[None, :]
+    matrix = jnp.zeros(gap.shape, jnp.float32)
+    for tap, weight in enumerate(catmull_weights(fraction)):
+        matrix = jnp.where(gap == tap - 1, weight[None, :], matrix)
+    return matrix
+
+
+def end_terms(halo, sign):
+    grade = curve = None
+    place = lax.broadcasted_iota(jnp.int32, halo.shape, 1)
+    halo = jnp.where(place >= lanes // 2 if sign < 0 else place < lanes // 2, halo, 0.0)
+    for m in range(1, reach + 1):
+        near = pltpu.roll(halo, (-sign * m) % lanes, 1)
+        first, second = (sign * slope[m - 1]) * near, bend[m - 1] * near
+        grade = first if grade is None else grade + first
+        curve = second if curve is None else curve + second
+    near = place < reach if sign < 0 else place >= lanes - reach
+    return jnp.where(near, grade, 0.0), jnp.where(near, curve, 0.0)
+
+
+def side_terms(ringed, extent):
+    size = ringed.shape[1]
+    grade = curve = None
+    for m in range(1, reach + 1):
+        ahead = pltpu.roll(ringed, size - m, 1)[:, :extent]
+        behind = pltpu.roll(ringed, m, 1)[:, :extent]
+        first, second = slope[m - 1] * (ahead - behind), bend[m - 1] * (ahead + behind)
+        grade = first if grade is None else grade + first
+        curve = second if curve is None else curve + second
+    return grade, curve
+
+
+def combine_kernel(tiles, parity, main_ref, outer_ref, matrix_ref, mid_ref, left_ref, right_ref, rows_ref, table_ref,
+                   core_ref, far_ref, out_ref, fine_ref, seg_high, seg_low, halo_ref):
+    step, steps = pl.program_id(0), pl.num_programs(0)
+    kinds, rows, cells = main_ref.shape
+    depth, height, width = mid_ref.shape
+
+    @pl.when(step == 0)
+    def _():
+        for ref, begin, size in ((main_ref, 0, cells), (outer_ref, cells, lanes)):
+            high, low = split(ref[...].reshape(kinds * rows, size))
+            seg_high[:, begin : begin + size] = high
+            seg_low[:, begin : begin + size] = low
+        even = parity[0] == 0
+        after = jnp.where(even, core_ref[:, :rows], far_ref[:, :rows])[:reach]
+        before = jnp.where(even, far_ref[:, :rows], core_ref[:, :rows])[reach:]
+        gap = jnp.zeros((lanes - 2 * reach, rows), jnp.float32)
+        halo_ref[...] = jnp.concatenate([after, gap, before], axis=0).T
+
+    own = step // 2
+    other = lax.rem(own + jnp.where(lax.rem(step, 2) == 1, 1, tiles), tiles + 1)
+    spans = [pl.ds(pl.multiple_of(at * lanes, lanes), lanes) for at in (own, other)]
+    source = jnp.concatenate([ref[:, span] for ref in (seg_high, seg_low, seg_high) for span in spans], axis=1)
+    high, low = split(matrix_ref[...])
+    fine = dot(source, jnp.concatenate([high, high, low], axis=0))
+
+    values = jnp.concatenate([mid_ref[...].reshape(rows, width), rows_ref[...].reshape(-1, width)], axis=0)
+    high, low = split(values)
+    level = dot(table_ref[...], jnp.concatenate([high, low, high], axis=0))
+
+    place = lax.broadcasted_iota(jnp.int32, (height, lanes), 1)
+    for z in range(depth):
+        left = jnp.where(step == 0, 0.0, left_ref[z])
+        right = jnp.where(step == steps - 1, 0.0, right_ref[z])
+        mid = mid_ref[z]
+        grade, curve = side_terms(jnp.concatenate([mid, jnp.where(place < lanes // 2, right, left)], axis=1), width)
+        span = slice(z * height, (z + 1) * height)
+
+        def of(array, kind):
+            return array[kind * rows + z * height : kind * rows + (z + 1) * height]
+
+        vertical = of(fine, 2)
+        out_ref[span] = (centre_weight * mid + (curve + of(level, 2))) + (
+            of(fine, 0) * grade + of(fine, 1) * of(level, 0) + vertical * of(level, 1)
+        )
+        fine_ref[span] = vertical
+    for at, sign, begin in ((0, -1, 0), (steps - 1, 1, width - lanes)):
+
+        @pl.when(step == at)
+        def _():
+            grade, curve = end_terms(halo_ref[...], sign)
+            span = slice(begin, begin + lanes)
+            out_ref[:, span] += fine[:rows, span] * grade + curve
+
+
+def combine_call(main, outer, matrix, scalar, outer_rows, core, diagonal, parity):
+    kinds, rows, cells = main.shape
+    depth, height, points = scalar.shape
+    steps = 2 * (cells // lanes)
+    width = points // steps
+    tiles, last = width // lanes, points // lanes - 1
+    table = level_table(depth, height)
+    flat_tile = pl.BlockSpec((rows, width), lambda t, parity: (0, t))
+    edge = (depth, height, lanes)
+    ends = pl.BlockSpec((2 * reach, cells), lambda t, parity: (core.shape[0] // (2 * reach) - 1, 0))
+    flat = jax.ShapeDtypeStruct((rows, points), jnp.float32)
+    return pl.pallas_call(
+        functools.partial(combine_kernel, cells // lanes),
+        grid_spec=pltpu.PrefetchScalarGridSpec(
+            num_scalar_prefetch=1,
+            grid=(steps,),
+            in_specs=[
+                pl.BlockSpec((kinds, rows, cells), lambda t, parity: (0, 0, 0)),
+                pl.BlockSpec((kinds, rows, lanes), lambda t, parity: (0, 0, 0)),
+                pl.BlockSpec((2 * lanes, width), lambda t, parity: (0, t)),
+                pl.BlockSpec((depth, height, width), lambda t, parity: (0, 0, t)),
+                pl.BlockSpec(edge, lambda t, parity: (0, 0, jnp.maximum(t * tiles - 1, 0))),
+                pl.BlockSpec(edge, lambda t, parity: (0, 0, jnp.minimum((t + 1) * tiles, last))),
+                pl.BlockSpec((depth, 2 * reach, width), lambda t, parity: (0, 0, t)),
+                pl.BlockSpec(table.shape, lambda t, parity: (0, 0)),
+                ends,
+                ends,
+            ],
+            out_specs=[flat_tile, flat_tile],
+            scratch_shapes=[
+                pltpu.VMEM((kinds * rows, cells + lanes), jnp.bfloat16),
+                pltpu.VMEM((kinds * rows, cells + lanes), jnp.bfloat16),
+                pltpu.VMEM((rows, lanes), jnp.float32),
+            ],
+        ),
+        out_shape=[flat, flat],
+        compiler_params=pltpu.CompilerParams(vmem_limit_bytes=vmem_bytes),
+        cost_estimate=light,
+        name="combine",
+    )(parity, main, outer, matrix, scalar, scalar, scalar, outer_rows, jnp.asarray(table), core, diagonal)
+
+
+def finish_kernel(chunks, part_ref, fine_ref, low_hbm, high_hbm, out_hbm,
+                  out_ref, low_ref, high_ref, in_sems, out_sems):
+    depth, _, points = part_ref.shape
+    width = points // chunks
+    sources = ((low_hbm, low_ref), (high_hbm, high_ref))
+    arrivals, sends = [], []
+    for c in range(chunks):
+        span = slice(None), slice(None), pl.ds(c * width, width)
+        arrivals.append(
+            [
+                pltpu.make_async_copy(source.at[span], held.at[span], in_sems.at[c, i])
+                for i, (source, held) in enumerate(sources)
+            ]
+        )
+        sends.append(pltpu.make_async_copy(out_ref.at[span], out_hbm.at[span], out_sems.at[c]))
+        for copy in arrivals[-1]:
+            copy.start()
+    for c in range(chunks):
+        for copy in arrivals[c]:
+            copy.wait()
+        span = pl.ds(c * width, width)
+        for p in range(depth):
+            grade = curve = None
+            for halo_ref, first_layer in ((low_ref, -reach), (high_ref, depth)):
+                for h in range(reach):
+                    m = first_layer + h - p
+                    if abs(m) <= reach:
+                        near = halo_ref[h, :, span]
+                        first = (slope[m - 1] if m > 0 else -slope[-m - 1]) * near
+                        second = bend[abs(m) - 1] * near
+                        grade = first if grade is None else grade + first
+                        curve = second if curve is None else curve + second
+            out_ref[p, :, span] = part_ref[p, :, span] + (fine_ref[p, :, span] * grade + curve)
+        sends[c].start()
+    for send in sends:
+        send.wait()
+
+
+def finish_call(part, fine, low, high):
+    points = part.shape[2]
+    chunks = 4 if points % (4 * lanes) == 0 else 1
+    anywhere = pl.BlockSpec(memory_space=pl.ANY)
+    return pl.pallas_call(
+        functools.partial(finish_kernel, chunks),
+        in_specs=[pl.BlockSpec(memory_space=pltpu.VMEM)] * 2 + [anywhere] * 2,
+        out_specs=anywhere,
+        out_shape=jax.ShapeDtypeStruct(part.shape, jnp.float32),
+        scratch_shapes=[pltpu.VMEM(array.shape, jnp.float32) for array in (part, low, high)]
+        + [pltpu.SemaphoreType.DMA((chunks, 2)), pltpu.SemaphoreType.DMA((chunks,))],
+        compiler_params=pltpu.CompilerParams(vmem_limit_bytes=vmem_bytes),
+        cost_estimate=light,
+        name="finish",
+    )(part, fine, low, high)
+
+
+def tie(value, *gates):
+    anywhere = pl.BlockSpec(memory_space=pl.ANY)
+    return pl.pallas_call(
+        lambda *refs: None,
+        in_specs=[anywhere] * (1 + len(gates)),
+        out_specs=anywhere,
+        out_shape=jax.ShapeDtypeStruct(value.shape, value.dtype),
+        input_output_aliases={0: 0},
+        cost_estimate=light,
+        name="tie",
+    )(value, *gates)
+
+
+def depart_kernel(own_hbm, scalar_hbm, *refs):
+    outs, (own_ref, scalar_ref, sent_ref, edge_ref, in_sems, out_sems) = refs[:4], refs[4:]
+    kinds, rows, cells = own_ref.shape
+    depth, height, points = scalar_ref.shape
+    lines = kinds * rows
+    layers = [pl.ds(depth - reach, reach), pl.ds(0, reach)]
+    middle = depth - 2 * reach
+    arrivals = [
+        pltpu.make_async_copy(scalar_hbm.at[span], scalar_ref.at[span], in_sems.at[i])
+        for i, span in enumerate(layers + [pl.ds(reach, middle)] * (middle > 0))
+    ]
+    arrivals.append(pltpu.make_async_copy(own_hbm, own_ref, in_sems.at[3]))
+    for copy in arrivals:
+        copy.start()
+    sends = []
+
+    def send(source, target):
+        copy = pltpu.make_async_copy(source, target, out_sems.at[len(sends)])
+        copy.start()
+        sends.append(copy)
+
+    for i, span in enumerate(layers):
+        arrivals[i].wait()
+        send(scalar_ref.at[span], outs[i])
+    for copy in arrivals[2:]:
+        copy.wait()
+    edge_ref[:, :reach] = scalar_ref[:, :reach]
+    edge_ref[:, reach:] = scalar_ref[:, height - reach :]
+    send(edge_ref, outs[2])
+    sent_ref[:lines] = own_ref[...].reshape(lines, cells)
+    first = scalar_ref[:, :, :lanes].reshape(rows, lanes).T
+    last = scalar_ref[:, :, points - lanes :].reshape(rows, lanes).T
+    ends = jnp.concatenate([first[:reach], last[lanes - reach :]], axis=0)
+    sent_ref[lines:] = jnp.zeros((2 * reach, cells), jnp.float32)
+    sent_ref[lines:, :rows] = ends
+    send(sent_ref, outs[-1])
+    for copy in sends:
+        copy.wait()
+
+
+def depart_call(own, scalar):
+    kinds, rows, cells = own.shape
+    depth, height, points = scalar.shape
+    edge = (depth, 2 * reach, points)
+    sent = (kinds * rows + 2 * reach, cells)
+    shapes = [(reach, height, points)] * 2 + [edge] + [sent]
+    anywhere = pl.BlockSpec(memory_space=pl.ANY)
+    return pl.pallas_call(
+        depart_kernel,
+        in_specs=[anywhere] * 2,
+        out_specs=[anywhere] * len(shapes),
+        out_shape=[jax.ShapeDtypeStruct(shape, jnp.float32) for shape in shapes],
+        scratch_shapes=[
+            pltpu.VMEM(own.shape, jnp.float32),
+            pltpu.VMEM(scalar.shape, jnp.float32),
+            pltpu.VMEM(sent, jnp.float32),
+            pltpu.VMEM(edge, jnp.float32),
+            pltpu.SemaphoreType.DMA((4,)),
+            pltpu.SemaphoreType.DMA((4,)),
+        ],
+        compiler_params=pltpu.CompilerParams(vmem_limit_bytes=most_vmem_bytes),
+        cost_estimate=light,
+        name="depart",
+    )(own, scalar)
 
 
 def padded_2(block, sides, width):
@@ -53,17 +477,6 @@
     return jnp.concatenate([first, second, average], axis=0)
 
 
-def catmull_weights(fraction):
-    square = fraction * fraction
-    cube = square * fraction
-    return (
-        (-cube + 2.0 * square - fraction) * 0.5,
-        (3.0 * cube - 5.0 * square + 2.0) * 0.5,
-        (-3.0 * cube + 4.0 * square + fraction) * 0.5,
-        (cube - square) * 0.5,
-    )
-
-
 def scalar_update(padded, fine):
     extent = (padded.shape[0] - 8, padded.shape[1] - 8, padded.shape[2] - 8)
     centre = lax.slice(padded, (4, 4, 4), (4 + extent[0], 4 + extent[1], 4 + extent[2]))
@@ -76,15 +489,15 @@
             begin[axis_index] = offset
             finish = (begin[0] + extent[0], begin[1] + extent[1], begin[2] + extent[2])
             window = lax.slice(padded, tuple(begin), finish)
-            if first_coeffs[offset] != 0.0:
-                slope = slope + first_coeffs[offset] * window
-            curvature = curvature + second_coeffs[offset] * window
+            if first_all[offset] != 0.0:
+                slope = slope + first_all[offset] * window
+            curvature = curvature + second_all[offset] * window
         gradients.append(slope)
     advection = fine[2] * gradients[0] + fine[1] * gradients[1] + fine[0] * gradients[2]
     return centre - advect_rate * advection + diffuse_rate * curvature
 
 
-def per_device(velocity, scalar, spline_base, spline_frac):
+def general_per_device(velocity, scalar, spline_base, spline_frac):
     cells = velocity.shape[1]
     length = cells * lax.axis_size("blk")
     block = lax.axis_index("blk")
@@ -114,6 +527,33 @@
     return (segment, scalar_update(padded, fine))
 
 
+def per_device(velocity, scalar, spline_base, spline_frac):
+    kinds, cells, depth, height = velocity.shape
+    points = scalar.shape[2]
+    rows = depth * height
+    count = lax.axis_size("blk")
+    if count != 4 or lax.axis_size("grp") != 2 or cells % lanes or rows > cells or (points // 2) % cells:
+        return general_per_device(velocity, scalar, spline_base, spline_frac)
+    length = cells * count
+    block = lax.axis_index("blk")
+
+    rows_of_x = jnp.transpose(velocity, (0, 2, 3, 1)).reshape(kinds, rows, cells)
+    up, down, edges, own = depart_call(rows_of_x, scalar)
+    chip = lax.ppermute(own, "blk", exclusive("blk", 2))
+    lower = lax.ppermute(up, "dep", ring("dep", 1))
+    upper = lax.ppermute(down, "dep", ring("dep", -1))
+    outer_rows = lax.ppermute(tie(edges, chip), "grp", ring("grp", 1))
+    matrix = spline_matrix(spline_base - block * cells, spline_frac, cells, points // cells)
+    core = lax.ppermute(tie(own, chip), "blk", exclusive("blk", 1))
+    diagonal = lax.ppermute(chip, "blk", exclusive("blk", 1))
+    info = jnp.stack([(block - (block ^ j)) % count for j in range(4)] + [block % 2]).astype(jnp.int32)
+    main, outer = segment_call(rows_of_x, core, chip, diagonal, info, length)
+    part, vertical = combine_call(main, outer, matrix, scalar, outer_rows, core, diagonal, info[4:])
+    result = finish_call(part.reshape(scalar.shape), vertical.reshape(scalar.shape), lower, upper)
+    segment = jnp.transpose(main.reshape(kinds, depth, height, cells), (0, 3, 1, 2))
+    return segment, result
+
+
 def solution(mesh):
     in_specs = (P(None, "blk", "dep", "grp"), P("dep", "grp", "blk"), P("blk"), P("blk"))
     out_specs = (P(None, "blk", "dep", "grp"), P("dep", "grp", "blk"))

time: 141 us -> 58.5 us (0.41)
  other arithmetic: 35.5 us -> 1.36 us
  matrix products: 23.5 us -> 0 us
  waiting for transfers between devices: 43.4 us -> 20.8 us
  Pallas kernels: 0 us -> 21.7 us
  between operations: 14.2 us -> 0.75 us
  local copies, waits for them, and re-layouts: 13.2 us -> 4.48 us
    add x5 -> x0, other arithmetic: 24.1 us -> none  [the longest x1 22.9 us: scalar_update(): return centre - advect_rate * advection + diffuse_rate * curvature]
    ppermute x8 -> x6, waiting for transfers between devices: 42.7 us -> 20.8 us  [the longest x1 14.1 us: per_device(): chip = lax.ppermute(own, 'blk', exclusive('blk', 2))]
    pallas_call x0 -> x6, Pallas kernels: none -> 21.7 us  [the longest x1 10.2 us: combine_call(): pl.pallas_call(functools.partial(combine_kernel, cells // lanes), grid_sp...]
    dot_general x1 -> x0, matrix products: 13 us -> none  [per_device(): fine = jnp.einsum('cxzy,xi->czyi', widened, matrix, precision=highest)]
    unnamed x1 -> x0, matrix products: 10.4 us -> none
    slice x4 -> x0, local copies, waits for them, and re-layouts: 5.93 us -> none  [padded_2(): lax.slice_in_dim(block, block.shape[dim] - width, None, axis=dim)]
    concatenate x3 -> x0, local copies, waits for them, and re-layouts: 5.68 us -> none  [the longest x2 5.68 us: padded_2(): block = jnp.concatenate([low, block, high], axis=dim)]
    select_n x1, other arithmetic: 6.59 us -> 1.31 us  [spline_matrix(): matrix = jnp.where(gap == tap - 1, weight[None, :], matrix)]
  transfers between devices with their start and end apart: 9 -> 6, of which waited for: 5 -> 3; matrix products, arithmetic and copies ran while one was open for 35% -> 2% of each run, Pallas kernels for 0% -> 27%
where the time goes in v3:
time: 58.5 us; the launch traced here: 58.2 us
  Pallas kernels  21.7 us (37%)
  waiting for transfers between devices  20.8 us (36%)
  starting transfers between devices  9.17 us (16%)
  local copies, waits for them, and re-layouts  4.48 us (8%)
  other arithmetic  1.36 us (2%)
  between operations  0.75 us (1%)
    ppermute x1, waiting for transfers between devices, per_device(): chip = lax.ppermute(own, 'blk', exclusive('blk', 2))  14.1 us
    pallas_call x1, Pallas kernels, combine_call(): pl.pallas_call(functools.partial(combine_kernel, cells // lanes), grid_sp...  10.2 us
    pallas_call x1, Pallas kernels, segment_call(): pl.pallas_call(functools.partial(segment_kernel, length), grid_spec=pltpu...  5.65 us
    unnamed x18, local copies, waits for them, and re-layouts  4.39 us
    ppermute x1, waiting for transfers between devices, per_device(): upper = lax.ppermute(down, 'dep', ring('dep', -1))  3.65 us
    pallas_call x1, Pallas kernels, depart_call(): pl.pallas_call(depart_kernel, in_specs=[anywhere] * 2, out_specs=[anywher...  3.06 us
    ppermute x1, waiting for transfers between devices, per_device(): outer_rows = lax.ppermute(tie(edges, chip), 'grp', ring('grp', 1))  3.03 us
    ppermute x1, starting transfers between devices, per_device(): chip = lax.ppermute(own, 'blk', exclusive('blk', 2))  3 us
  transfers between devices with their start and end apart: 6, of which 3 were waited for; matrix products, arithmetic and copies ran while one was open for 2% of the time, Pallas kernels for 27%

profile of v3, /device:TPU:0, one launch (start us, length us, event | category | flops | bytes accessed | tf_op | source)
XLA Modules:
  0.0 58.2 jit_solution(9012352681051571840)
XLA Ops:
  0.6 0.0 copy-start.7
  0.6 0.0 copy-start.8
  0.6 3.1 %depart.1 = (f32[4,32,2048]{2,1,0:T(8,128)}, f32[4,32,2048]{2,1,0:T(8,128)}, f32[8,8,2048]{2,1,0:T(8,128)}, f32[776,256]{1,0:T(8,128)}) custom-call(f32[3,256,256]{2,1,0:T(8,128)} %bitcast.12, f32[8,32,2048]{2,1,0:T(8,128)} %right_ref.1), custom_call_target="tpu_custom_call" | custom-call | flops 1024 | bytes 1024 | tf_op jit(solution)/shard_map/depart/pallas_call | solution.py:432
  3.7 3.0 %collective-permute-start = (f32[776,256]{1,0:T(8,128)}, f32[776,256]{1,0:T(8,128)S(1)}, u32[]{:S(2)}, u32[]{:S(2)}) collective-permute-start(f32[776,256]{1,0:T(8,128)} %get-tuple-element.10.refs_0_), channel_id=1, source_target_pairs={{0,8},{4,12},{8,0},{12,4},{1,9},{5,13},{9,1},{13,5},{2,10},{6,14},... | collective-permute-start | bytes 2383880 | tf_op jit(solution)/shard_map/ppermute | solution.py:542
  6.7 1.6 %collective-permute-start.4 = (f32[4,32,2048]{2,1,0:T(8,128)}, f32[4,32,2048]{2,1,0:T(8,128)}, u32[]{:S(2)}, u32[]{:S(2)}) collective-permute-start(f32[4,32,2048]{2,1,0:T(8,128)} %get-tuple-element.16), channel_id=1, source_target_pairs={{0,1},{1,2},{2,3},{3,0},{4,5},{5,6},{6,7},{7,4},{8,9},{9,10},{10,1... | collective-permute-start | bytes 3145736 | tf_op jit(solution)/shard_map/ppermute | solution.py:543
  8.3 2.2 %collective-permute-start.5 = (f32[4,32,2048]{2,1,0:T(8,128)}, f32[4,32,2048]{2,1,0:T(8,128)}, u32[]{:S(2)}, u32[]{:S(2)}) collective-permute-start(f32[4,32,2048]{2,1,0:T(8,128)} %get-tuple-element.17), channel_id=1, source_target_pairs={{0,3},{1,0},{2,1},{3,2},{4,7},{5,4},{6,5},{7,6},{8,11},{9,8},{10,9... | collective-permute-start | bytes 3145736 | tf_op jit(solution)/shard_map/ppermute | solution.py:544
  10.6 0.0 copy-done.7
  10.6 14.1 %collective-permute-done.refs_1_.chip_ref = f32[776,256]{1,0:T(8,128)S(1)} collective-permute-done((f32[776,256]{1,0:T(8,128)}, f32[776,256]{1,0:T(8,128)S(1)}, u32[]{:S(2)}, u32[]{:S(2)}) %collective-permute-start) | collective-permute-done | bytes 794656 | tf_op jit(solution)/shard_map/ppermute | solution.py:542
  24.6 0.0 copy-start.2
  24.6 0.9 %copy-done.2 = f32[776,256]{1,0:T(8,128)} copy-done((f32[776,256]{1,0:T(8,128)}, f32[776,256]{1,0:T(8,128)S(1)}, u32[]{:S(2)}) %copy-start.2) | copy-done | bytes 794648
  25.6 0.0 copy-start.3
  25.6 0.0 copy-start.4
  25.6 0.0 collective-permute-start.1
  25.6 0.5 collective-permute-start.2
  26.1 0.0 copy-done.8
  26.1 1.8 %collective-permute-start.3 = (f32[8,8,2048]{2,1,0:T(8,128)}, f32[8,8,2048]{2,1,0:T(8,128)}, u32[]{:S(2)}, u32[]{:S(2)}) collective-permute-start(f32[8,8,2048]{2,1,0:T(8,128)} %tie.3), channel_id=1, source_target_pairs={{0,16},{16,0},{1,17},{17,1},{2,18},{18,2},{3,19},{19,3},{4,20},{20... | collective-permute-start | bytes 1572872 | tf_op jit(solution)/shard_map/ppermute | solution.py:545
  27.9 0.1 stack.20.info
  28.0 0.0 copy-start.1
  28.0 1.3 %select_select_fusion.matrix_ref = f32[256,2048]{1,0:T(8,128)S(1)} fusion(f32[2048]{0:T(1024)S(1)} %get-tuple-element.20, f32[2048]{0:T(1024)S(1)} %get-tuple-element.19, f32[2048]{0:T(1024)S(1)} %get-tuple-element.21, f32[2048]{0:T(1024)S(1)} %get-tuple-element.18, s32[2048]{0:T(1024)S(1)} %get-tuple-element.23, s32[2048]{0:T(1024)S(1)} %get-tuple-element.22, ...), kind=kLoop, calls=%fused_computation.10 | loop fusion | flops 8388608 | bytes 2154752 | tf_op jit(solution)/shard_map/jit(_where)/select_n | solution.py:192
  29.3 0.0 collective-permute-done.1.core_ref
  29.4 0.0 collective-permute-done.2.far_ref
  29.4 0.0 copy-done.3
  29.4 0.0 copy-done.4
  29.4 0.0 copy-start
  29.4 2.3 %copy-done = bf16[4,768,768]{2,1,0:T(8,128)(2,1)S(1)} copy-done((bf16[4,768,768]{2,1,0:T(8,128)(2,1)S(1)}, bf16[4,768,768]{2,1,0:T(8,128)(2,1)}, u32[]{:S(2)}) %copy-start) | copy-done | bytes 4718616
  31.7 0.0 copy-start.5
  31.7 5.6 %segment.1 = (f32[3,256,256]{2,1,0:T(8,128)}, f32[3,256,128]{2,1,0:T(8,128)S(1)}) custom-call(s32[5]{0:T(128)S(1)} %stack.20.info, f32[3,256,256]{2,1,0:T(8,128)S(1)} %bitcast.13, f32[776,256]{1,0:T(8,128)S(1)} %collective-permute-done.1.core_ref, f32[776,256]{1,0:T(8,128)S(1)} %copy-done.3, f32[776,256]{1,0:T(8,128)S(1)} %collective-permute-done.2.far_ref, ...), custom_call_target="tpu_custom_call" | custom-call | flops 1024 | bytes 1024 | tf_op jit(solution)/shard_map/segment/pallas_call | solution.py:152
  37.4 3.0 %collective-permute-done.3.rows_ref = f32[8,8,2048]{2,1,0:T(8,128)} collective-permute-done((f32[8,8,2048]{2,1,0:T(8,128)}, f32[8,8,2048]{2,1,0:T(8,128)}, u32[]{:S(2)}, u32[]{:S(2)}) %collective-permute-start.3) | collective-permute-done | bytes 524320 | tf_op jit(solution)/shard_map/ppermute | solution.py:545
  40.4 0.0 copy-done.1
  40.4 0.0 copy-done.5
  40.4 0.0 copy-start.6
  40.4 1.1 %copy-done.6 = f32[3,256,256]{2,1,0:T(8,128)S(1)} copy-done((f32[3,256,256]{2,1,0:T(8,128)S(1)}, f32[3,256,256]{2,1,0:T(8,128)}, u32[]{:S(2)}) %copy-start.6) | copy-done | bytes 786456
  41.6 10.2 %combine.1 = (f32[256,2048]{1,0:T(8,128)S(1)}, f32[256,2048]{1,0:T(8,128)S(1)}) custom-call(s32[1]{0:T(128)} %bitcast.3.parity, f32[3,256,256]{2,1,0:T(8,128)S(1)} %copy-done.6, f32[3,256,128]{2,1,0:T(8,128)S(1)} %get-tuple-element.12.outer_ref, f32[256,2048]{1,0:T(8,128)S(1)} %select_select_fusion.matrix_ref, f32[8,32,2048]{2,1,0:T(8,128)S(1)} %copy-done.1, ...), custom_call_target="tpu_custom_call" | custom-call | flops 1024 | bytes 1024 | tf_op jit(solution)/shard_map/combine/pallas_call | solution.py:286
  51.8 0.0 collective-permute-done.4.low_hbm
  51.8 3.6 %collective-permute-done.5.high_hbm = f32[4,32,2048]{2,1,0:T(8,128)} collective-permute-done((f32[4,32,2048]{2,1,0:T(8,128)}, f32[4,32,2048]{2,1,0:T(8,128)}, u32[]{:S(2)}, u32[]{:S(2)}) %collective-permute-start.5) | collective-permute-done | bytes 1048608 | tf_op jit(solution)/shard_map/ppermute | solution.py:544
  55.4 2.8 %finish.1 = f32[8,32,2048]{2,1,0:T(8,128)} custom-call(f32[8,32,2048]{2,1,0:T(8,128)S(1)} %bitcast.14, f32[8,32,2048]{2,1,0:T(8,128)S(1)} %bitcast.15, f32[4,32,2048]{2,1,0:T(8,128)} %collective-permute-done.4.low_hbm, f32[4,32,2048]{2,1,0:T(8,128)} %collective-permute-done.5.high_hbm), custom_call_target="tpu_custom_call" | custom-call | flops 1024 | bytes 1024 | tf_op jit(solution)/shard_map/finish/pallas_call | solution.py:359
  (6 shorter events, 0.0 us)
Async XLA Ops:
  0.6 9.9 %copy-start.7 = (f32[2048]{0:T(1024)S(1)}, f32[2048]{0:T(1024)}, u32[]{:S(2)}) copy-start(f32[2048]{0:T(1024)} %param.9) | copy-start | bytes 24580
  0.6 25.4 %copy-start.8 = (s32[2048]{0:T(1024)S(1)}, s32[2048]{0:T(1024)}, u32[]{:S(2)}) copy-start(s32[2048]{0:T(1024)} %param.8) | copy-start | bytes 24580
  3.7 20.9 %collective-permute-start = (f32[776,256]{1,0:T(8,128)}, f32[776,256]{1,0:T(8,128)S(1)}, u32[]{:S(2)}, u32[]{:S(2)}) collective-permute-start(f32[776,256]{1,0:T(8,128)} %get-tuple-element.10.refs_0_), channel_id=1, source_target_pairs={{0,8},{4,12},{8,0},{12,4},{1,9},{5,13},{9,1},{13,5},{2,10},{6,14},... | collective-permute-start | bytes 2383880 | tf_op jit(solution)/shard_map/ppermute | solution.py:542
  6.7 45.0 %collective-permute-start.4 = (f32[4,32,2048]{2,1,0:T(8,128)}, f32[4,32,2048]{2,1,0:T(8,128)}, u32[]{:S(2)}, u32[]{:S(2)}) collective-permute-start(f32[4,32,2048]{2,1,0:T(8,128)} %get-tuple-element.16), channel_id=1, source_target_pairs={{0,1},{1,2},{2,3},{3,0},{4,5},{5,6},{6,7},{7,4},{8,9},{9,10},{10,1... | collective-permute-start | bytes 3145736 | tf_op jit(solution)/shard_map/ppermute | solution.py:543
  8.3 47.1 %collective-permute-start.5 = (f32[4,32,2048]{2,1,0:T(8,128)}, f32[4,32,2048]{2,1,0:T(8,128)}, u32[]{:S(2)}, u32[]{:S(2)}) collective-permute-start(f32[4,32,2048]{2,1,0:T(8,128)} %get-tuple-element.17), channel_id=1, source_target_pairs={{0,3},{1,0},{2,1},{3,2},{4,7},{5,4},{6,5},{7,6},{8,11},{9,8},{10,9... | collective-permute-start | bytes 3145736 | tf_op jit(solution)/shard_map/ppermute | solution.py:544
  24.6 0.9 %copy-start.2 = (f32[776,256]{1,0:T(8,128)}, f32[776,256]{1,0:T(8,128)S(1)}, u32[]{:S(2)}) copy-start(f32[776,256]{1,0:T(8,128)S(1)} %collective-permute-done.refs_1_.chip_ref) | copy-start | bytes 2383876
  25.6 3.8 %copy-start.3 = (f32[776,256]{1,0:T(8,128)S(1)}, f32[776,256]{1,0:T(8,128)}, u32[]{:S(2)}) copy-start(f32[776,256]{1,0:T(8,128)} %copy-done.2) | copy-start | bytes 2383876
  25.6 3.8 %copy-start.4 = (f32[3,256,8,32]{1,3,2,0:T(8,128)S(1)}, f32[3,256,8,32]{1,3,2,0:T(8,128)}, u32[]{:S(2)}) copy-start(f32[3,256,8,32]{1,3,2,0:T(8,128)} %param.6) | copy-start | bytes 2359300
  25.6 3.8 %collective-permute-start.1 = (f32[776,256]{1,0:T(8,128)}, f32[776,256]{1,0:T(8,128)S(1)}, u32[]{:S(2)}, u32[]{:S(2)}) collective-permute-start(f32[776,256]{1,0:T(8,128)} %tie.2), channel_id=1, source_target_pairs={{0,4},{4,0},{8,12},{12,8},{1,5},{5,1},{9,13},{13,9},{2,6},{6,2},{1... | collective-permute-start | bytes 2383880 | tf_op jit(solution)/shard_map/ppermute | solution.py:547
  25.6 3.8 %collective-permute-start.2 = (f32[776,256]{1,0:T(8,128)}, f32[776,256]{1,0:T(8,128)S(1)}, u32[]{:S(2)}, u32[]{:S(2)}) collective-permute-start(f32[776,256]{1,0:T(8,128)} %copy-done.2), channel_id=1, source_target_pairs={{0,4},{4,0},{8,12},{12,8},{1,5},{5,1},{9,13},{13,9},{2,6},{6,2},{1... | collective-permute-start | bytes 2383880 | tf_op jit(solution)/shard_map/ppermute | solution.py:548
  26.1 14.3 %collective-permute-start.3 = (f32[8,8,2048]{2,1,0:T(8,128)}, f32[8,8,2048]{2,1,0:T(8,128)}, u32[]{:S(2)}, u32[]{:S(2)}) collective-permute-start(f32[8,8,2048]{2,1,0:T(8,128)} %tie.3), channel_id=1, source_target_pairs={{0,16},{16,0},{1,17},{17,1},{2,18},{18,2},{3,19},{19,3},{4,20},{20... | collective-permute-start | bytes 1572872 | tf_op jit(solution)/shard_map/ppermute | solution.py:545
  28.0 12.4 %copy-start.1 = (f32[8,32,2048]{2,1,0:T(8,128)S(1)}, f32[8,32,2048]{2,1,0:T(8,128)}, u32[]{:S(2)}) copy-start(f32[8,32,2048]{2,1,0:T(8,128)} %right_ref.1) | copy-start | bytes 6291460
  29.4 2.3 %copy-start = (bf16[4,768,768]{2,1,0:T(8,128)(2,1)S(1)}, bf16[4,768,768]{2,1,0:T(8,128)(2,1)}, u32[]{:S(2)}) copy-start(bf16[4,768,768]{2,1,0:T(8,128)(2,1)} %constant.129.clone.refs_0_.refs_1_.refs_2_.refs_3_) | copy-start | bytes 14155780
  31.7 8.7 %copy-start.5 = (bf16[768,960]{1,0:T(8,128)(2,1)S(1)}, bf16[768,960]{1,0:T(8,128)(2,1)}, u32[]{:S(2)}) copy-start(bf16[768,960]{1,0:T(8,128)(2,1)} %constant.130.clone.table_ref) | copy-start | bytes 4423684
  40.4 1.1 %copy-start.6 = (f32[3,256,256]{2,1,0:T(8,128)S(1)}, f32[3,256,256]{2,1,0:T(8,128)}, u32[]{:S(2)}) copy-start(f32[3,256,256]{2,1,0:T(8,128)} %get-tuple-element.11.main_ref) | copy-start | bytes 2359300

commit v4 on v3

--- a/solution.py
+++ b/solution.py
@@ -116,7 +116,8 @@
     table_refs, (main_ref, outer_ref) = refs[:4], refs[4:]
     kinds, rows, cells = own_ref.shape
     lines = kinds * rows
-    blocks = [own_ref[...].reshape(lines, cells)] + [ref[:lines] for ref in (core_ref, chip_ref, far_ref)]
+    blocks = [own_ref[...].reshape(lines, cells), core_ref[:lines]]
+    blocks += [ref[...].reshape(lines, cells) for ref in (chip_ref, far_ref)]
     total = sums = None
     for block, table_ref in zip(blocks, table_refs):
         product = dot(left_operand(block), table_ref[0])
@@ -154,7 +155,7 @@
         grid_spec=pltpu.PrefetchScalarGridSpec(
             num_scalar_prefetch=1,
             grid=(1,),
-            in_specs=[whole] + [sent] * 3 + tables,
+            in_specs=[whole, sent, whole, whole] + tables,
             out_specs=[whole, pl.BlockSpec((kinds, rows, lanes), lambda g, info: (0, 0, 0))],
         ),
         out_shape=[
@@ -298,7 +299,7 @@
                 pl.BlockSpec((depth, 2 * reach, width), lambda t, parity: (0, 0, t)),
                 pl.BlockSpec(table.shape, lambda t, parity: (0, 0)),
                 ends,
-                ends,
+                pl.BlockSpec((2 * reach, cells), lambda t, parity: (0, 0)),
             ],
             out_specs=[flat_tile, flat_tile],
             scratch_shapes=[
@@ -314,55 +315,60 @@
     )(parity, main, outer, matrix, scalar, scalar, scalar, outer_rows, jnp.asarray(table), core, diagonal)
 
 
-def finish_kernel(chunks, part_ref, fine_ref, low_hbm, high_hbm, out_hbm,
-                  out_ref, low_ref, high_ref, in_sems, out_sems):
+def finish_kernel(chunks, part_ref, fine_ref, low_ref, high_hbm, out_hbm, out_ref, high_ref, in_sems, out_sems):
     depth, _, points = part_ref.shape
     width = points // chunks
-    sources = ((low_hbm, low_ref), (high_hbm, high_ref))
-    arrivals, sends = [], []
-    for c in range(chunks):
-        span = slice(None), slice(None), pl.ds(c * width, width)
-        arrivals.append(
-            [
-                pltpu.make_async_copy(source.at[span], held.at[span], in_sems.at[c, i])
-                for i, (source, held) in enumerate(sources)
-            ]
-        )
-        sends.append(pltpu.make_async_copy(out_ref.at[span], out_hbm.at[span], out_sems.at[c]))
-        for copy in arrivals[-1]:
-            copy.start()
-    for c in range(chunks):
-        for copy in arrivals[c]:
-            copy.wait()
-        span = pl.ds(c * width, width)
-        for p in range(depth):
+    spans = [pl.ds(c * width, width) for c in range(chunks)]
+    arrivals = [
+        pltpu.make_async_copy(high_hbm.at[:, :, span], high_ref.at[:, :, span], in_sems.at[c])
+        for c, span in enumerate(spans)
+    ]
+    for copy in arrivals:
+        copy.start()
+    sends = []
+
+    def add(halo_ref, first_layer, layers, span):
+        for p in layers:
             grade = curve = None
-            for halo_ref, first_layer in ((low_ref, -reach), (high_ref, depth)):
-                for h in range(reach):
-                    m = first_layer + h - p
-                    if abs(m) <= reach:
-                        near = halo_ref[h, :, span]
-                        first = (slope[m - 1] if m > 0 else -slope[-m - 1]) * near
-                        second = bend[abs(m) - 1] * near
-                        grade = first if grade is None else grade + first
-                        curve = second if curve is None else curve + second
+            for h in range(reach):
+                m = first_layer + h - p
+                if abs(m) <= reach:
+                    near = halo_ref[h, :, span]
+                    first = (slope[m - 1] if m > 0 else -slope[-m - 1]) * near
+                    second = bend[abs(m) - 1] * near
+                    grade = first if grade is None else grade + first
+                    curve = second if curve is None else curve + second
             out_ref[p, :, span] = part_ref[p, :, span] + (fine_ref[p, :, span] * grade + curve)
-        sends[c].start()
-    for send in sends:
-        send.wait()
+        at = pl.ds(layers[0], len(layers)), slice(None), span
+        copy = pltpu.make_async_copy(out_ref.at[at], out_hbm.at[at], out_sems.at[len(sends)])
+        copy.start()
+        sends.append(copy)
+
+    for span in spans:
+        add(low_ref, -reach, range(reach), span)
+    for arrival, span in zip(arrivals, spans):
+        arrival.wait()
+        add(high_ref, depth, range(depth - reach, depth), span)
+    for copy in sends:
+        copy.wait()
 
 
 def finish_call(part, fine, low, high):
     points = part.shape[2]
     chunks = 4 if points % (4 * lanes) == 0 else 1
+    held = pl.BlockSpec(memory_space=pltpu.VMEM)
     anywhere = pl.BlockSpec(memory_space=pl.ANY)
     return pl.pallas_call(
         functools.partial(finish_kernel, chunks),
-        in_specs=[pl.BlockSpec(memory_space=pltpu.VMEM)] * 2 + [anywhere] * 2,
+        in_specs=[held, held, held, anywhere],
         out_specs=anywhere,
         out_shape=jax.ShapeDtypeStruct(part.shape, jnp.float32),
-        scratch_shapes=[pltpu.VMEM(array.shape, jnp.float32) for array in (part, low, high)]
-        + [pltpu.SemaphoreType.DMA((chunks, 2)), pltpu.SemaphoreType.DMA((chunks,))],
+        scratch_shapes=[
+            pltpu.VMEM(part.shape, jnp.float32),
+            pltpu.VMEM(high.shape, jnp.float32),
+            pltpu.SemaphoreType.DMA((chunks,)),
+            pltpu.SemaphoreType.DMA((2 * chunks,)),
+        ],
         compiler_params=pltpu.CompilerParams(vmem_limit_bytes=vmem_bytes),
         cost_estimate=light,
         name="finish",
@@ -382,11 +388,10 @@
     )(value, *gates)
 
 
-def depart_kernel(own_hbm, scalar_hbm, *refs):
-    outs, (own_ref, scalar_ref, sent_ref, edge_ref, in_sems, out_sems) = refs[:4], refs[4:]
+def depart_kernel(own_hbm, scalar_hbm, gate, down_hbm, edge_hbm, sent_hbm, end_hbm,
+                  own_ref, scalar_ref, ends_ref, edge_ref, in_sems, out_sems):
     kinds, rows, cells = own_ref.shape
     depth, height, points = scalar_ref.shape
-    lines = kinds * rows
     layers = [pl.ds(depth - reach, reach), pl.ds(0, reach)]
     middle = depth - 2 * reach
     arrivals = [
@@ -394,7 +399,7 @@
         for i, span in enumerate(layers + [pl.ds(reach, middle)] * (middle > 0))
     ]
     arrivals.append(pltpu.make_async_copy(own_hbm, own_ref, in_sems.at[3]))
-    for copy in arrivals:
+    for copy in arrivals[::-1]:
         copy.start()
     sends = []
 
@@ -403,49 +408,48 @@
         copy.start()
         sends.append(copy)
 
-    for i, span in enumerate(layers):
-        arrivals[i].wait()
-        send(scalar_ref.at[span], outs[i])
-    for copy in arrivals[2:]:
+    arrivals[-1].wait()
+    for kind in range(kinds):
+        send(own_ref.at[kind], sent_hbm.at[pl.ds(kind * rows, rows)])
+    for copy in arrivals[:-1]:
         copy.wait()
+    send(scalar_ref.at[layers[1]], down_hbm)
     edge_ref[:, :reach] = scalar_ref[:, :reach]
     edge_ref[:, reach:] = scalar_ref[:, height - reach :]
-    send(edge_ref, outs[2])
-    sent_ref[:lines] = own_ref[...].reshape(lines, cells)
+    send(edge_ref, edge_hbm)
     first = scalar_ref[:, :, :lanes].reshape(rows, lanes).T
     last = scalar_ref[:, :, points - lanes :].reshape(rows, lanes).T
-    ends = jnp.concatenate([first[:reach], last[lanes - reach :]], axis=0)
-    sent_ref[lines:] = jnp.zeros((2 * reach, cells), jnp.float32)
-    sent_ref[lines:, :rows] = ends
-    send(sent_ref, outs[-1])
+    ends_ref[...] = jnp.zeros_like(ends_ref)
+    ends_ref[:, :rows] = jnp.concatenate([first[:reach], last[lanes - reach :]], axis=0)
+    send(ends_ref, sent_hbm.at[pl.ds(kinds * rows, 2 * reach)])
+    send(ends_ref, end_hbm)
     for copy in sends:
         copy.wait()
 
 
-def depart_call(own, scalar):
+def depart_call(own, scalar, gate):
     kinds, rows, cells = own.shape
     depth, height, points = scalar.shape
-    edge = (depth, 2 * reach, points)
-    sent = (kinds * rows + 2 * reach, cells)
-    shapes = [(reach, height, points)] * 2 + [edge] + [sent]
+    edge, ends = (depth, 2 * reach, points), (2 * reach, cells)
+    shapes = [(reach, height, points), edge, (kinds * rows + 2 * reach, cells), ends]
     anywhere = pl.BlockSpec(memory_space=pl.ANY)
     return pl.pallas_call(
         depart_kernel,
-        in_specs=[anywhere] * 2,
+        in_specs=[anywhere] * 3,
         out_specs=[anywhere] * len(shapes),
         out_shape=[jax.ShapeDtypeStruct(shape, jnp.float32) for shape in shapes],
         scratch_shapes=[
             pltpu.VMEM(own.shape, jnp.float32),
             pltpu.VMEM(scalar.shape, jnp.float32),
-            pltpu.VMEM(sent, jnp.float32),
+            pltpu.VMEM(ends, jnp.float32),
             pltpu.VMEM(edge, jnp.float32),
             pltpu.SemaphoreType.DMA((4,)),
-            pltpu.SemaphoreType.DMA((4,)),
+            pltpu.SemaphoreType.DMA((4 + kinds,)),
         ],
         compiler_params=pltpu.CompilerParams(vmem_limit_bytes=most_vmem_bytes),
         cost_estimate=light,
         name="depart",
-    )(own, scalar)
+    )(own, scalar, gate)
 
 
 def padded_2(block, sides, width):
@@ -532,23 +536,26 @@
     points = scalar.shape[2]
     rows = depth * height
     count = lax.axis_size("blk")
-    if count != 4 or lax.axis_size("grp") != 2 or cells % lanes or rows > cells or (points // 2) % cells:
+    if count != 4 or lax.axis_size("grp") != 2 or cells % lanes or rows > cells or (points // 2) % cells or depth != 2 * reach:
         return general_per_device(velocity, scalar, spline_base, spline_frac)
     length = cells * count
     block = lax.axis_index("blk")
 
     rows_of_x = jnp.transpose(velocity, (0, 2, 3, 1)).reshape(kinds, rows, cells)
-    up, down, edges, own = depart_call(rows_of_x, scalar)
-    chip = lax.ppermute(own, "blk", exclusive("blk", 2))
+    chip = lax.ppermute(rows_of_x, "blk", exclusive("blk", 2))
+    up = scalar[-reach:]
     lower = lax.ppermute(up, "dep", ring("dep", 1))
+    down, edges, own, ends = depart_call(rows_of_x, scalar, up)
     upper = lax.ppermute(down, "dep", ring("dep", -1))
-    outer_rows = lax.ppermute(tie(edges, chip), "grp", ring("grp", 1))
+    far_ends = lax.ppermute(ends, "blk", exclusive("blk", 3))
     matrix = spline_matrix(spline_base - block * cells, spline_frac, cells, points // cells)
+    outer_rows = lax.ppermute(edges, "grp", ring("grp", 1))
     core = lax.ppermute(tie(own, chip), "blk", exclusive("blk", 1))
+    chip = tie(chip, far_ends, matrix, outer_rows)
     diagonal = lax.ppermute(chip, "blk", exclusive("blk", 1))
     info = jnp.stack([(block - (block ^ j)) % count for j in range(4)] + [block % 2]).astype(jnp.int32)
     main, outer = segment_call(rows_of_x, core, chip, diagonal, info, length)
-    part, vertical = combine_call(main, outer, matrix, scalar, outer_rows, core, diagonal, info[4:])
+    part, vertical = combine_call(main, outer, matrix, scalar, outer_rows, core, far_ends, info[4:])
     result = finish_call(part.reshape(scalar.shape), vertical.reshape(scalar.shape), lower, upper)
     segment = jnp.transpose(main.reshape(kinds, depth, height, cells), (0, 3, 1, 2))
     return segment, result

time: 58.5 us -> 58.1 us (level)
  waiting for transfers between devices: 20.8 us -> 14.4 us
  local copies, waits for them, and re-layouts: 4.48 us -> 8.96 us
  other arithmetic: 1.36 us -> 2.68 us
    ppermute x2 -> x3, waiting for transfers between devices: 17.1 us -> 7.24 us  [the longest x1 6.89 us: per_device(): chip = lax.ppermute(rows_of_x, 'blk', exclusive('blk', 2))]
    slice x0 -> x1, local copies, waits for them, and re-layouts: none -> 2.33 us  [per_device(): up = scalar[-reach:]]
    ppermute x1, waiting for transfers between devices: 0.01 us -> 2.17 us  [per_device(): diagonal = lax.ppermute(chip, 'blk', exclusive('blk', 1))]
    unnamed x18 -> x28, local copies, waits for them, and re-layouts: 4.39 us -> 6.55 us
    select_n x1, other arithmetic: 1.31 us -> 2.63 us  [spline_matrix(): matrix = jnp.where(gap == tap - 1, weight[None, :], matrix)]
    pallas_call x1, Pallas kernels: 5.65 us -> 6.95 us  [segment_call(): pl.pallas_call(functools.partial(segment_kernel, length), grid_spec=pltpu...]
    ppermute x1, waiting for transfers between devices: 3.65 us -> 4.94 us  [per_device(): upper = lax.ppermute(down, 'dep', ring('dep', -1))]
    pallas_call x1, Pallas kernels: 10.2 us -> 9.5 us  [combine_call(): pl.pallas_call(functools.partial(combine_kernel, cells // lanes), grid_sp...]
  transfers between devices with their start and end apart: 6 -> 7, of which waited for: 3 -> 4; matrix products, arithmetic and copies ran while one was open for 2% -> 9% of each run, Pallas kernels for 27% -> 34%
where the time goes in v4:
time: 58.1 us; the launch traced here: 57.7 us
  Pallas kernels  22 us (38%)
  waiting for transfers between devices  14.4 us (25%)
  starting transfers between devices  8.99 us (15%)
  local copies, waits for them, and re-layouts  8.96 us (15%)
  other arithmetic  2.68 us (5%)
  between operations  0.74 us (1%)
    pallas_call x1, Pallas kernels, combine_call(): pl.pallas_call(functools.partial(combine_kernel, cells // lanes), grid_sp...  9.5 us
    pallas_call x1, Pallas kernels, segment_call(): pl.pallas_call(functools.partial(segment_kernel, length), grid_spec=pltpu...  6.95 us
    ppermute x1, waiting for transfers between devices, per_device(): chip = lax.ppermute(rows_of_x, 'blk', exclusive('blk', 2))  6.89 us
    unnamed x28, local copies, waits for them, and re-layouts  6.55 us
    ppermute x1, waiting for transfers between devices, per_device(): upper = lax.ppermute(down, 'dep', ring('dep', -1))  4.94 us
    pallas_call x1, Pallas kernels, depart_call(): pl.pallas_call(depart_kernel, in_specs=[anywhere] * 3, out_specs=[anywher...  3.05 us
    ppermute x1, starting transfers between devices, per_device(): chip = lax.ppermute(rows_of_x, 'blk', exclusive('blk', 2))  3 us
    select_n x1, other arithmetic, spline_matrix(): matrix = jnp.where(gap == tap - 1, weight[None, :], matrix)  2.63 us
  transfers between devices with their start and end apart: 7, of which 4 were waited for; matrix products, arithmetic and copies ran while one was open for 9% of the time, Pallas kernels for 34%

profile of v4, /device:TPU:0, one launch (start us, length us, event | category | flops | bytes accessed | tf_op | source)
XLA Modules:
  0.0 57.7 jit_solution(16881138504019524119)
XLA Ops:
  0.6 3.0 %collective-permute-start = (f32[3,256,256]{2,1,0:T(8,128)}, f32[3,256,256]{2,1,0:T(8,128)S(1)}, u32[]{:S(2)}, u32[]{:S(2)}) collective-permute-start(f32[3,256,256]{2,1,0:T(8,128)} %bitcast.12), channel_id=1, source_target_pairs={{0,8},{4,12},{8,0},{12,4},{1,9},{5,13},{9,1},{13,5},{2,10},{6,14},... | collective-permute-start | bytes 2359304 | tf_op jit(solution)/shard_map/ppermute | solution.py:545
  3.6 2.3 %slice.3.gate = f32[4,32,2048]{2,1,0:T(8,128)} slice(f32[8,32,2048]{2,1,0:T(8,128)} %right_ref.1), slice={[4:8], [0:32], [0:2048]} | slice | bytes 2097152 | tf_op jit(solution)/shard_map/slice | solution.py:546
  6.0 0.0 copy-start.12
  6.0 1.6 %collective-permute-start.5 = (f32[4,32,2048]{2,1,0:T(8,128)}, f32[4,32,2048]{2,1,0:T(8,128)S(1)}, u32[]{:S(2)}, u32[]{:S(2)}) collective-permute-start(f32[4,32,2048]{2,1,0:T(8,128)} %slice.3.gate), channel_id=1, source_target_pairs={{0,1},{1,2},{2,3},{3,0},{4,5},{5,6},{6,7},{7,4},{8,9},{9,10},{10,1... | collective-permute-start | bytes 3145736 | tf_op jit(solution)/shard_map/ppermute | solution.py:547
  7.5 3.0 %depart.1 = (f32[4,32,2048]{2,1,0:T(8,128)}, f32[8,8,2048]{2,1,0:T(8,128)}, f32[776,256]{1,0:T(8,128)}, f32[8,256]{1,0:T(8,128)}) custom-call(f32[3,256,256]{2,1,0:T(8,128)} %bitcast.13, f32[8,32,2048]{2,1,0:T(8,128)} %right_ref.1, f32[4,32,2048]{2,1,0:T(8,128)} %slice.3.gate), custom_call_target="tpu_custom_call" | custom-call | flops 1024 | bytes 1024 | tf_op jit(solution)/shard_map/depart/pallas_call | solution.py:436
  10.6 0.1 collective-permute-start.2
  10.7 1.6 %collective-permute-start.3 = (f32[8,8,2048]{2,1,0:T(8,128)}, f32[8,8,2048]{2,1,0:T(8,128)S(1)}, u32[]{:S(2)}, u32[]{:S(2)}) collective-permute-start(f32[8,8,2048]{2,1,0:T(8,128)} %get-tuple-element.12), channel_id=1, source_target_pairs={{0,16},{16,0},{1,17},{17,1},{2,18},{18,2},{3,19},{19,3},{4,20},{20... | collective-permute-start | bytes 1572872 | tf_op jit(solution)/shard_map/ppermute | solution.py:552
  12.3 2.2 %collective-permute-start.6 = (f32[4,32,2048]{2,1,0:T(8,128)}, f32[4,32,2048]{2,1,0:T(8,128)}, u32[]{:S(2)}, u32[]{:S(2)}) collective-permute-start(f32[4,32,2048]{2,1,0:T(8,128)} %get-tuple-element.17), channel_id=1, source_target_pairs={{0,3},{1,0},{2,1},{3,2},{4,7},{5,4},{6,5},{7,6},{8,11},{9,8},{10,9... | collective-permute-start | bytes 3145736 | tf_op jit(solution)/shard_map/ppermute | solution.py:549
  14.5 0.0 copy-done.12
  14.5 0.0 copy-done.13
  14.6 6.9 %collective-permute-done.refs_1_.refs_0_ = f32[3,256,256]{2,1,0:T(8,128)S(1)} collective-permute-done((f32[3,256,256]{2,1,0:T(8,128)}, f32[3,256,256]{2,1,0:T(8,128)S(1)}, u32[]{:S(2)}, u32[]{:S(2)}) %collective-permute-start) | collective-permute-done | bytes 786464 | tf_op jit(solution)/shard_map/ppermute | solution.py:545
  21.5 0.0 copy-start.3
  21.5 0.9 %copy-done.3 = f32[3,256,256]{2,1,0:T(8,128)} copy-done((f32[3,256,256]{2,1,0:T(8,128)}, f32[3,256,256]{2,1,0:T(8,128)S(1)}, u32[]{:S(2)}) %copy-start.3) | copy-done | bytes 786456
  22.4 0.0 collective-permute-start.1
  22.4 2.6 %select_select_fusion.refs_2_.matrix_ref = f32[256,2048]{1,0:T(8,128)} fusion(f32[2048]{0:T(1024)S(1)} %get-tuple-element.20, f32[2048]{0:T(1024)S(1)} %get-tuple-element.19, f32[2048]{0:T(1024)S(1)} %get-tuple-element.21, f32[2048]{0:T(1024)S(1)} %get-tuple-element.18, s32[2048]{0:T(1024)S(1)} %get-tuple-element.23, s32[2048]{0:T(1024)S(1)} %get-tuple-element.22, ...), kind=kLoop, calls=%fused_computation.10 | loop fusion | flops 8388608 | bytes 2154752 | tf_op jit(solution)/shard_map/jit(_where)/select_n | solution.py:193
  25.0 0.0 copy-start.5
  25.0 0.0 collective-permute-done.2.refs_1_.far_ref
  25.0 0.0 copy-start.10
  25.0 0.3 collective-permute-done.3.refs_3_.rows_ref
  25.4 0.2 copy-done.10
  25.6 0.0 copy-start.6
  25.6 0.8 %copy-done.6 = f32[8,8,2048]{2,1,0:T(8,128)} copy-done((f32[8,8,2048]{2,1,0:T(8,128)}, f32[8,8,2048]{2,1,0:T(8,128)S(1)}, u32[]{:S(2)}) %copy-start.6) | copy-done | bytes 524312
  26.4 0.5 collective-permute-start.4
  26.9 0.1 stack.20.info
  27.0 2.2 %collective-permute-done.4.far_ref = f32[3,256,256]{2,1,0:T(8,128)} collective-permute-done((f32[3,256,256]{2,1,0:T(8,128)}, f32[3,256,256]{2,1,0:T(8,128)}, u32[]{:S(2)}, u32[]{:S(2)}) %collective-permute-start.4) | collective-permute-done | bytes 786464 | tf_op jit(solution)/shard_map/ppermute | solution.py:555
  29.2 0.0 collective-permute-done.1.core_ref
  29.2 0.0 copy-done.5
  29.2 0.0 copy-start
  29.2 2.3 %copy-done = bf16[4,768,768]{2,1,0:T(8,128)(2,1)S(1)} copy-done((bf16[4,768,768]{2,1,0:T(8,128)(2,1)S(1)}, bf16[4,768,768]{2,1,0:T(8,128)(2,1)}, u32[]{:S(2)}) %copy-start) | copy-done | bytes 4718616
  31.5 0.0 copy-start.4
  31.5 1.1 %copy-done.4 = f32[3,256,256]{2,1,0:T(8,128)S(1)} copy-done((f32[3,256,256]{2,1,0:T(8,128)S(1)}, f32[3,256,256]{2,1,0:T(8,128)}, u32[]{:S(2)}) %copy-start.4) | copy-done | bytes 786456
  32.6 0.0 copy-start.1
  32.6 0.0 copy-start.2
  32.6 0.0 copy-start.7
  32.6 0.0 copy-start.8
  32.6 0.0 copy-start.11
  32.7 7.0 %segment.1 = (f32[3,256,256]{2,1,0:T(8,128)}, f32[3,256,128]{2,1,0:T(8,128)S(1)}) custom-call(s32[5]{0:T(128)S(1)} %stack.20.info, f32[3,256,256]{2,1,0:T(8,128)S(1)} %bitcast.14, f32[776,256]{1,0:T(8,128)S(1)} %collective-permute-done.1.core_ref, f32[3,256,256]{2,1,0:T(8,128)S(1)} %copy-done.4, f32[3,256,256]{2,1,0:T(8,128)} %collective-permute-done.4.far_ref, ...), custom_call_target="tpu_custom_call" | custom-call | flops 1024 | bytes 1024 | tf_op jit(solution)/shard_map/segment/pallas_call | solution.py:153
  39.6 0.0 copy-done.1
  39.6 0.0 copy-done.2
  39.6 0.0 copy-done.7
  39.6 0.0 copy-done.8
  39.6 0.0 copy-done.11
  39.6 0.0 copy-start.9
  39.7 1.1 %copy-done.9 = f32[3,256,256]{2,1,0:T(8,128)S(1)} copy-done((f32[3,256,256]{2,1,0:T(8,128)S(1)}, f32[3,256,256]{2,1,0:T(8,128)}, u32[]{:S(2)}) %copy-start.9) | copy-done | bytes 786456
  40.8 9.5 %combine.1 = (f32[256,2048]{1,0:T(8,128)S(1)}, f32[256,2048]{1,0:T(8,128)S(1)}) custom-call(s32[1]{0:T(128)} %bitcast.3.parity, f32[3,256,256]{2,1,0:T(8,128)S(1)} %copy-done.9, f32[3,256,128]{2,1,0:T(8,128)S(1)} %get-tuple-element.14.outer_ref, f32[256,2048]{1,0:T(8,128)S(1)} %copy-done.2, f32[8,32,2048]{2,1,0:T(8,128)S(1)} %copy-done.1, ...), custom_call_target="tpu_custom_call" | custom-call | flops 1024 | bytes 1024 | tf_op jit(solution)/shard_map/combine/pallas_call | solution.py:287
  50.3 0.0 collective-permute-done.5.low_ref
  50.3 4.9 %collective-permute-done.6.high_hbm = f32[4,32,2048]{2,1,0:T(8,128)} collective-permute-done((f32[4,32,2048]{2,1,0:T(8,128)}, f32[4,32,2048]{2,1,0:T(8,128)}, u32[]{:S(2)}, u32[]{:S(2)}) %collective-permute-start.6) | collective-permute-done | bytes 1048608 | tf_op jit(solution)/shard_map/ppermute | solution.py:549
  55.2 2.5 %finish.1 = f32[8,32,2048]{2,1,0:T(8,128)} custom-call(f32[8,32,2048]{2,1,0:T(8,128)S(1)} %bitcast.15, f32[8,32,2048]{2,1,0:T(8,128)S(1)} %bitcast.16, f32[4,32,2048]{2,1,0:T(8,128)S(1)} %collective-permute-done.5.low_ref, f32[4,32,2048]{2,1,0:T(8,128)} %collective-permute-done.6.high_hbm), custom_call_target="tpu_custom_call" | custom-call | flops 1024 | bytes 1024 | tf_op jit(solution)/shard_map/finish/pallas_call | solution.py:361
  (7 shorter events, 0.1 us)
Async XLA Ops:
  0.6 20.8 %collective-permute-start = (f32[3,256,256]{2,1,0:T(8,128)}, f32[3,256,256]{2,1,0:T(8,128)S(1)}, u32[]{:S(2)}, u32[]{:S(2)}) collective-permute-start(f32[3,256,256]{2,1,0:T(8,128)} %bitcast.12), channel_id=1, source_target_pairs={{0,8},{4,12},{8,0},{12,4},{1,9},{5,13},{9,1},{13,5},{2,10},{6,14},... | collective-permute-start | bytes 2359304 | tf_op jit(solution)/shard_map/ppermute | solution.py:545
  6.0 8.6 %copy-start.12 = (s32[2048]{0:T(1024)S(1)}, s32[2048]{0:T(1024)}, u32[]{:S(2)}) copy-start(s32[2048]{0:T(1024)} %param.8) | copy-start | bytes 24580
  6.0 8.6 %copy-start.13 = (f32[2048]{0:T(1024)S(1)}, f32[2048]{0:T(1024)}, u32[]{:S(2)}) copy-start(f32[2048]{0:T(1024)} %param.9) | copy-start | bytes 24580
  6.0 44.3 %collective-permute-start.5 = (f32[4,32,2048]{2,1,0:T(8,128)}, f32[4,32,2048]{2,1,0:T(8,128)S(1)}, u32[]{:S(2)}, u32[]{:S(2)}) collective-permute-start(f32[4,32,2048]{2,1,0:T(8,128)} %slice.3.gate), channel_id=1, source_target_pairs={{0,1},{1,2},{2,3},{3,0},{4,5},{5,6},{6,7},{7,4},{8,9},{9,10},{10,1... | collective-permute-start | bytes 3145736 | tf_op jit(solution)/shard_map/ppermute | solution.py:547
  10.6 14.4 %collective-permute-start.2 = (f32[8,256]{1,0:T(8,128)}, f32[8,256]{1,0:T(8,128)S(1)}, u32[]{:S(2)}, u32[]{:S(2)}) collective-permute-start(f32[8,256]{1,0:T(8,128)} %get-tuple-element.11), channel_id=1, source_target_pairs={{0,12},{4,8},{8,4},{12,0},{1,13},{5,9},{9,5},{13,1},{2,14},{6,10},... | collective-permute-start | bytes 24584 | tf_op jit(solution)/shard_map/ppermute | solution.py:550
  10.7 14.7 %collective-permute-start.3 = (f32[8,8,2048]{2,1,0:T(8,128)}, f32[8,8,2048]{2,1,0:T(8,128)S(1)}, u32[]{:S(2)}, u32[]{:S(2)}) collective-permute-start(f32[8,8,2048]{2,1,0:T(8,128)} %get-tuple-element.12), channel_id=1, source_target_pairs={{0,16},{16,0},{1,17},{17,1},{2,18},{18,2},{3,19},{19,3},{4,20},{20... | collective-permute-start | bytes 1572872 | tf_op jit(solution)/shard_map/ppermute | solution.py:552
  12.3 43.0 %collective-permute-start.6 = (f32[4,32,2048]{2,1,0:T(8,128)}, f32[4,32,2048]{2,1,0:T(8,128)}, u32[]{:S(2)}, u32[]{:S(2)}) collective-permute-start(f32[4,32,2048]{2,1,0:T(8,128)} %get-tuple-element.17), channel_id=1, source_target_pairs={{0,3},{1,0},{2,1},{3,2},{4,7},{5,4},{6,5},{7,6},{8,11},{9,8},{10,9... | collective-permute-start | bytes 3145736 | tf_op jit(solution)/shard_map/ppermute | solution.py:549
  21.5 0.9 %copy-start.3 = (f32[3,256,256]{2,1,0:T(8,128)}, f32[3,256,256]{2,1,0:T(8,128)S(1)}, u32[]{:S(2)}) copy-start(f32[3,256,256]{2,1,0:T(8,128)S(1)} %collective-permute-done.refs_1_.refs_0_) | copy-start | bytes 2359300
  22.4 6.8 %collective-permute-start.1 = (f32[776,256]{1,0:T(8,128)}, f32[776,256]{1,0:T(8,128)S(1)}, u32[]{:S(2)}, u32[]{:S(2)}) collective-permute-start(f32[776,256]{1,0:T(8,128)} %tie.2), channel_id=1, source_target_pairs={{0,4},{4,0},{8,12},{12,8},{1,5},{5,1},{9,13},{13,9},{2,6},{6,2},{1... | collective-permute-start | bytes 2383880 | tf_op jit(solution)/shard_map/ppermute | solution.py:553
  25.0 4.2 %copy-start.5 = (f32[3,256,8,32]{1,3,2,0:T(8,128)S(1)}, f32[3,256,8,32]{1,3,2,0:T(8,128)}, u32[]{:S(2)}) copy-start(f32[3,256,8,32]{1,3,2,0:T(8,128)} %param.6) | copy-start | bytes 2359300
  25.0 0.6 %copy-start.10 = (f32[8,256]{1,0:T(8,128)}, f32[8,256]{1,0:T(8,128)S(1)}, u32[]{:S(2)}) copy-start(f32[8,256]{1,0:T(8,128)S(1)} %collective-permute-done.2.refs_1_.far_ref) | copy-start | bytes 24580
  25.6 0.8 %copy-start.6 = (f32[8,8,2048]{2,1,0:T(8,128)}, f32[8,8,2048]{2,1,0:T(8,128)S(1)}, u32[]{:S(2)}) copy-start(f32[8,8,2048]{2,1,0:T(8,128)S(1)} %collective-permute-done.3.refs_3_.rows_ref) | copy-start | bytes 1572868
  26.4 2.8 %collective-permute-start.4 = (f32[3,256,256]{2,1,0:T(8,128)}, f32[3,256,256]{2,1,0:T(8,128)}, u32[]{:S(2)}, u32[]{:S(2)}) collective-permute-start(f32[3,256,256]{2,1,0:T(8,128)} %tie.3.chip_ref), channel_id=1, source_target_pairs={{0,4},{4,0},{8,12},{12,8},{1,5},{5,1},{9,13},{13,9},{2,6},{6,2},{1... | collective-permute-start | bytes 2359304 | tf_op jit(solution)/shard_map/ppermute | solution.py:555
  29.2 2.3 %copy-start = (bf16[4,768,768]{2,1,0:T(8,128)(2,1)S(1)}, bf16[4,768,768]{2,1,0:T(8,128)(2,1)}, u32[]{:S(2)}) copy-start(bf16[4,768,768]{2,1,0:T(8,128)(2,1)} %constant.129.clone.refs_0_.refs_1_.refs_2_.refs_3_) | copy-start | bytes 14155780
  31.5 1.1 %copy-start.4 = (f32[3,256,256]{2,1,0:T(8,128)S(1)}, f32[3,256,256]{2,1,0:T(8,128)}, u32[]{:S(2)}) copy-start(f32[3,256,256]{2,1,0:T(8,128)} %tie.3.chip_ref) | copy-start | bytes 2359300
  32.6 7.0 %copy-start.1 = (f32[8,32,2048]{2,1,0:T(8,128)S(1)}, f32[8,32,2048]{2,1,0:T(8,128)}, u32[]{:S(2)}) copy-start(f32[8,32,2048]{2,1,0:T(8,128)} %right_ref.1) | copy-start | bytes 6291460
  32.6 7.0 %copy-start.2 = (f32[256,2048]{1,0:T(8,128)S(1)}, f32[256,2048]{1,0:T(8,128)}, u32[]{:S(2)}) copy-start(f32[256,2048]{1,0:T(8,128)} %select_select_fusion.refs_2_.matrix_ref) | copy-start | bytes 6291460
  32.6 7.0 %copy-start.7 = (f32[8,8,2048]{2,1,0:T(8,128)S(1)}, f32[8,8,2048]{2,1,0:T(8,128)}, u32[]{:S(2)}) copy-start(f32[8,8,2048]{2,1,0:T(8,128)} %copy-done.6) | copy-start | bytes 1572868
  32.6 7.0 %copy-start.8 = (bf16[768,960]{1,0:T(8,128)(2,1)S(1)}, bf16[768,960]{1,0:T(8,128)(2,1)}, u32[]{:S(2)}) copy-start(bf16[768,960]{1,0:T(8,128)(2,1)} %constant.130.clone.table_ref) | copy-start | bytes 4423684
  32.6 7.0 %copy-start.11 = (f32[8,256]{1,0:T(8,128)S(1)}, f32[8,256]{1,0:T(8,128)}, u32[]{:S(2)}) copy-start(f32[8,256]{1,0:T(8,128)} %copy-done.10) | copy-start | bytes 24580
  39.6 1.1 %copy-start.9 = (f32[3,256,256]{2,1,0:T(8,128)S(1)}, f32[3,256,256]{2,1,0:T(8,128)}, u32[]{:S(2)}) copy-start(f32[3,256,256]{2,1,0:T(8,128)} %get-tuple-element.13.main_ref) | copy-start | bytes 2359300

commit v5 on v4

--- a/solution.py
+++ b/solution.py
@@ -24,6 +24,7 @@
 centre_weight = 1.0 + 3.0 * diffuse_rate * second_centre
 highest = lax.Precision.HIGHEST
 reach = 4
+slab_chunks = 4
 lanes = 128
 vmem_bytes = 32 * 1024 * 1024
 most_vmem_bytes = 60 * 1024 * 1024
@@ -315,12 +316,13 @@
     )(parity, main, outer, matrix, scalar, scalar, scalar, outer_rows, jnp.asarray(table), core, diagonal)
 
 
-def finish_kernel(chunks, part_ref, fine_ref, low_ref, high_hbm, out_hbm, out_ref, high_ref, in_sems, out_sems):
+def finish_kernel(chunks, part_ref, fine_ref, low_hbm, high_hbm, out_hbm, out_ref, low_ref, high_ref, in_sems, out_sems):
     depth, _, points = part_ref.shape
     width = points // chunks
     spans = [pl.ds(c * width, width) for c in range(chunks)]
     arrivals = [
-        pltpu.make_async_copy(high_hbm.at[:, :, span], high_ref.at[:, :, span], in_sems.at[c])
+        pltpu.make_async_copy(source.at[:, :, span], target.at[:, :, span], in_sems.at[i, c])
+        for i, (source, target) in enumerate(((low_hbm, low_ref), (high_hbm, high_ref)))
         for c, span in enumerate(spans)
     ]
     for copy in arrivals:
@@ -344,9 +346,10 @@
         copy.start()
         sends.append(copy)
 
-    for span in spans:
+    for arrival, span in zip(arrivals, spans):
+        arrival.wait()
         add(low_ref, -reach, range(reach), span)
-    for arrival, span in zip(arrivals, spans):
+    for arrival, span in zip(arrivals[chunks:], spans):
         arrival.wait()
         add(high_ref, depth, range(depth - reach, depth), span)
     for copy in sends:
@@ -360,13 +363,14 @@
     anywhere = pl.BlockSpec(memory_space=pl.ANY)
     return pl.pallas_call(
         functools.partial(finish_kernel, chunks),
-        in_specs=[held, held, held, anywhere],
+        in_specs=[held, held, anywhere, anywhere],
         out_specs=anywhere,
         out_shape=jax.ShapeDtypeStruct(part.shape, jnp.float32),
         scratch_shapes=[
             pltpu.VMEM(part.shape, jnp.float32),
+            pltpu.VMEM(low.shape, jnp.float32),
             pltpu.VMEM(high.shape, jnp.float32),
-            pltpu.SemaphoreType.DMA((chunks,)),
+            pltpu.SemaphoreType.DMA((2, chunks)),
             pltpu.SemaphoreType.DMA((2 * chunks,)),
         ],
         compiler_params=pltpu.CompilerParams(vmem_limit_bytes=vmem_bytes),
@@ -386,6 +390,45 @@
         cost_estimate=light,
         name="tie",
     )(value, *gates)
+
+
+def slab_kernel(begin, source_hbm, out_ref, held_ref, in_sems, out_sems):
+    layers, _, points = held_ref.shape
+    width = points // slab_chunks
+    spans = [pl.ds(c * width, width) for c in range(slab_chunks)]
+    arrivals = [
+        pltpu.make_async_copy(
+            source_hbm.at[pl.ds(begin, layers), :, span], held_ref.at[:, :, span], in_sems.at[c]
+        )
+        for c, span in enumerate(spans)
+    ]
+    sends = [
+        pltpu.make_async_copy(held_ref.at[:, :, span], out_ref.at[:, :, span], out_sems.at[c])
+        for c, span in enumerate(spans)
+    ]
+    for copy in arrivals:
+        copy.start()
+    for copy, send in zip(arrivals, sends):
+        copy.wait()
+        send.start()
+    for send in sends:
+        send.wait()
+
+
+def slab_call(scalar, width):
+    depth, height, _ = scalar.shape
+    shape = (reach, height, width)
+    anywhere = pl.BlockSpec(memory_space=pl.ANY)
+    return pl.pallas_call(
+        functools.partial(slab_kernel, depth - reach),
+        in_specs=[anywhere],
+        out_specs=anywhere,
+        out_shape=jax.ShapeDtypeStruct(shape, jnp.float32),
+        scratch_shapes=[pltpu.VMEM(shape, jnp.float32)] + [pltpu.SemaphoreType.DMA((slab_chunks,))] * 2,
+        compiler_params=pltpu.CompilerParams(vmem_limit_bytes=52 * 1024 * 1024),
+        cost_estimate=light,
+        name="slab",
+    )(scalar)
 
 
 def depart_kernel(own_hbm, scalar_hbm, gate, down_hbm, edge_hbm, sent_hbm, end_hbm,
@@ -543,7 +586,7 @@
 
     rows_of_x = jnp.transpose(velocity, (0, 2, 3, 1)).reshape(kinds, rows, cells)
     chip = lax.ppermute(rows_of_x, "blk", exclusive("blk", 2))
-    up = scalar[-reach:]
+    up = slab_call(scalar, points)
     lower = lax.ppermute(up, "dep", ring("dep", 1))
     down, edges, own, ends = depart_call(rows_of_x, scalar, up)
     upper = lax.ppermute(down, "dep", ring("dep", -1))

time: 58.1 us -> 57.1 us (0.983)
  local copies, waits for them, and re-layouts: 8.96 us -> 6.99 us
  starting transfers between devices: 8.99 us -> 9.7 us
    slice x1 -> x0, local copies, waits for them, and re-layouts: 2.33 us -> none  [per_device(): up = scalar[-reach:]]
    pallas_call x1, Pallas kernels: 6.95 us -> 5.63 us  [segment_call(): pl.pallas_call(functools.partial(segment_kernel, length), grid_spec=pltpu...]
    pallas_call x0 -> x1, Pallas kernels: none -> 1.28 us  [slab_call(): pl.pallas_call(functools.partial(slab_kernel, depth - reach), in_specs=[a...]
    ppermute x1, starting transfers between devices: 2.25 us -> 2.91 us  [per_device(): upper = lax.ppermute(down, 'dep', ring('dep', -1))]
    unnamed x28 -> x30, local copies, waits for them, and re-layouts: 6.55 us -> 6.9 us
  transfers between devices with their start and end apart: 7 -> 7, of which waited for: 4 -> 3; matrix products, arithmetic and copies ran while one was open for 9% -> 5% of each run, Pallas kernels for 34% -> 34%
where the time goes in v5:
time: 57.1 us; the launch traced here: 56.7 us
  Pallas kernels  22.1 us (39%)
  waiting for transfers between devices  14.4 us (25%)
  starting transfers between devices  9.7 us (17%)
  local copies, waits for them, and re-layouts  6.99 us (12%)
  other arithmetic  2.68 us (5%)
  between operations  0.77 us (1%)
    pallas_call x1, Pallas kernels, combine_call(): pl.pallas_call(functools.partial(combine_kernel, cells // lanes), grid_sp...  9.51 us
    ppermute x1, waiting for transfers between devices, per_device(): chip = lax.ppermute(rows_of_x, 'blk', exclusive('blk', 2))  7.18 us
    unnamed x30, local copies, waits for them, and re-layouts  6.9 us
    pallas_call x1, Pallas kernels, segment_call(): pl.pallas_call(functools.partial(segment_kernel, length), grid_spec=pltpu...  5.63 us
    ppermute x1, waiting for transfers between devices, per_device(): upper = lax.ppermute(down, 'dep', ring('dep', -1))  5.22 us
    pallas_call x1, Pallas kernels, depart_call(): pl.pallas_call(depart_kernel, in_specs=[anywhere] * 3, out_specs=[anywher...  3.05 us
    ppermute x1, starting transfers between devices, per_device(): chip = lax.ppermute(rows_of_x, 'blk', exclusive('blk', 2))  3 us
    ppermute x1, starting transfers between devices, per_device(): upper = lax.ppermute(down, 'dep', ring('dep', -1))  2.91 us
  transfers between devices with their start and end apart: 7, of which 3 were waited for; matrix products, arithmetic and copies ran while one was open for 5% of the time, Pallas kernels for 34%

profile of v5, /device:TPU:0, one launch (start us, length us, event | category | flops | bytes accessed | tf_op | source)
XLA Modules:
  0.0 56.7 jit_solution(13051350757544043088)
XLA Ops:
  0.6 3.0 %collective-permute-start = (f32[3,256,256]{2,1,0:T(8,128)}, f32[3,256,256]{2,1,0:T(8,128)S(1)}, u32[]{:S(2)}, u32[]{:S(2)}) collective-permute-start(f32[3,256,256]{2,1,0:T(8,128)} %bitcast.12), channel_id=1, source_target_pairs={{0,8},{4,12},{8,0},{12,4},{1,9},{5,13},{9,1},{13,5},{2,10},{6,14},... | collective-permute-start | bytes 2359304 | tf_op jit(solution)/shard_map/ppermute | solution.py:588
  3.6 1.3 %slab.1.gate = f32[4,32,2048]{2,1,0:T(8,128)S(1)} custom-call(f32[8,32,2048]{2,1,0:T(8,128)} %right_ref.1), custom_call_target="tpu_custom_call" | custom-call | flops 1024 | bytes 1024 | tf_op jit(solution)/shard_map/slab/pallas_call | solution.py:422
  4.9 0.0 copy-start.5
  4.9 0.0 copy-start.13
  4.9 0.0 copy-start.14
  5.0 1.6 %collective-permute-start.5 = (f32[4,32,2048]{2,1,0:T(8,128)S(1)}, f32[4,32,2048]{2,1,0:T(8,128)}, u32[]{:S(2)}, u32[]{:S(2)}) collective-permute-start(f32[4,32,2048]{2,1,0:T(8,128)S(1)} %slab.1.gate), channel_id=1, source_target_pairs={{0,1},{1,2},{2,3},{3,0},{4,5},{5,6},{6,7},{7,4},{8,9},{9,10},{10,1... | collective-permute-start | bytes 3145736 | tf_op jit(solution)/shard_map/ppermute | solution.py:590
  6.6 0.0 copy-done.5
  6.6 3.0 %depart.1 = (f32[4,32,2048]{2,1,0:T(8,128)}, f32[8,8,2048]{2,1,0:T(8,128)}, f32[776,256]{1,0:T(8,128)}, f32[8,256]{1,0:T(8,128)}) custom-call(f32[3,256,256]{2,1,0:T(8,128)} %bitcast.13, f32[8,32,2048]{2,1,0:T(8,128)} %right_ref.1, f32[4,32,2048]{2,1,0:T(8,128)} %copy-done.5), custom_call_target="tpu_custom_call" | custom-call | flops 1024 | bytes 1024 | tf_op jit(solution)/shard_map/depart/pallas_call | solution.py:479
  9.6 0.1 collective-permute-start.2
  9.7 1.6 %collective-permute-start.3 = (f32[8,8,2048]{2,1,0:T(8,128)}, f32[8,8,2048]{2,1,0:T(8,128)S(1)}, u32[]{:S(2)}, u32[]{:S(2)}) collective-permute-start(f32[8,8,2048]{2,1,0:T(8,128)} %get-tuple-element.12), channel_id=1, source_target_pairs={{0,16},{16,0},{1,17},{17,1},{2,18},{18,2},{3,19},{19,3},{4,20},{20... | collective-permute-start | bytes 1572872 | tf_op jit(solution)/shard_map/ppermute | solution.py:595
  11.3 2.9 %collective-permute-start.6 = (f32[4,32,2048]{2,1,0:T(8,128)}, f32[4,32,2048]{2,1,0:T(8,128)}, u32[]{:S(2)}, u32[]{:S(2)}) collective-permute-start(f32[4,32,2048]{2,1,0:T(8,128)} %get-tuple-element.17), channel_id=1, source_target_pairs={{0,3},{1,0},{2,1},{3,2},{4,7},{5,4},{6,5},{7,6},{8,11},{9,8},{10,9... | collective-permute-start | bytes 3145736 | tf_op jit(solution)/shard_map/ppermute | solution.py:592
  14.2 0.0 copy-done.13
  14.3 0.0 copy-done.14
  14.3 7.2 %collective-permute-done.refs_1_.refs_0_ = f32[3,256,256]{2,1,0:T(8,128)S(1)} collective-permute-done((f32[3,256,256]{2,1,0:T(8,128)}, f32[3,256,256]{2,1,0:T(8,128)S(1)}, u32[]{:S(2)}, u32[]{:S(2)}) %collective-permute-start) | collective-permute-done | bytes 786464 | tf_op jit(solution)/shard_map/ppermute | solution.py:588
  21.5 0.0 copy-start.3
  21.5 0.9 %copy-done.3 = f32[3,256,256]{2,1,0:T(8,128)} copy-done((f32[3,256,256]{2,1,0:T(8,128)}, f32[3,256,256]{2,1,0:T(8,128)S(1)}, u32[]{:S(2)}) %copy-start.3) | copy-done | bytes 786456
  22.4 0.0 collective-permute-start.1
  22.4 2.6 %select_select_fusion.refs_2_.matrix_ref = f32[256,2048]{1,0:T(8,128)} fusion(f32[2048]{0:T(1024)S(1)} %get-tuple-element.20, f32[2048]{0:T(1024)S(1)} %get-tuple-element.19, f32[2048]{0:T(1024)S(1)} %get-tuple-element.21, f32[2048]{0:T(1024)S(1)} %get-tuple-element.18, s32[2048]{0:T(1024)S(1)} %get-tuple-element.23, s32[2048]{0:T(1024)S(1)} %get-tuple-element.22, ...), kind=kLoop, calls=%fused_computation.10 | loop fusion | flops 8388608 | bytes 2154752 | tf_op jit(solution)/shard_map/jit(_where)/select_n | solution.py:194
  25.0 0.0 copy-start.6
  25.0 0.0 collective-permute-done.2.refs_1_.far_ref
  25.0 0.0 copy-start.11
  25.0 0.0 collective-permute-done.3.refs_3_.rows_ref
  25.0 0.6 %copy-done.11 = f32[8,256]{1,0:T(8,128)} copy-done((f32[8,256]{1,0:T(8,128)}, f32[8,256]{1,0:T(8,128)S(1)}, u32[]{:S(2)}) %copy-start.11) | copy-done | bytes 8216
  25.6 0.0 copy-start.7
  25.6 0.8 %copy-done.7 = f32[8,8,2048]{2,1,0:T(8,128)} copy-done((f32[8,8,2048]{2,1,0:T(8,128)}, f32[8,8,2048]{2,1,0:T(8,128)S(1)}, u32[]{:S(2)}) %copy-start.7) | copy-done | bytes 524312
  26.4 0.5 collective-permute-start.4
  26.9 0.1 stack.20.info
  27.0 2.0 %collective-permute-done.4.far_ref = f32[3,256,256]{2,1,0:T(8,128)S(1)} collective-permute-done((f32[3,256,256]{2,1,0:T(8,128)}, f32[3,256,256]{2,1,0:T(8,128)S(1)}, u32[]{:S(2)}, u32[]{:S(2)}) %collective-permute-start.4) | collective-permute-done | bytes 786464 | tf_op jit(solution)/shard_map/ppermute | solution.py:598
  29.0 0.0 collective-permute-done.1.core_ref
  29.0 0.0 copy-done.6
  29.0 0.0 copy-start
  29.0 2.3 %copy-done = bf16[4,768,768]{2,1,0:T(8,128)(2,1)S(1)} copy-done((bf16[4,768,768]{2,1,0:T(8,128)(2,1)S(1)}, bf16[4,768,768]{2,1,0:T(8,128)(2,1)}, u32[]{:S(2)}) %copy-start) | copy-done | bytes 4718616
  31.4 0.0 copy-start.4
  31.4 1.1 %copy-done.4 = f32[3,256,256]{2,1,0:T(8,128)S(1)} copy-done((f32[3,256,256]{2,1,0:T(8,128)S(1)}, f32[3,256,256]{2,1,0:T(8,128)}, u32[]{:S(2)}) %copy-start.4) | copy-done | bytes 786456
  32.5 0.0 copy-start.1
  32.5 0.0 copy-start.12
  32.5 5.6 %segment.1 = (f32[3,256,256]{2,1,0:T(8,128)}, f32[3,256,128]{2,1,0:T(8,128)S(1)}) custom-call(s32[5]{0:T(128)S(1)} %stack.20.info, f32[3,256,256]{2,1,0:T(8,128)S(1)} %bitcast.14, f32[776,256]{1,0:T(8,128)S(1)} %collective-permute-done.1.core_ref, f32[3,256,256]{2,1,0:T(8,128)S(1)} %copy-done.4, f32[3,256,256]{2,1,0:T(8,128)S(1)} %collective-permute-done.4.far_ref, ...), custom_call_target="tpu_custom_call" | custom-call | flops 1024 | bytes 1024 | tf_op jit(solution)/shard_map/segment/pallas_call | solution.py:154
  38.2 0.0 copy-done.1
  38.2 0.0 copy-done.2
  38.2 0.0 copy-done.8
  38.2 0.0 copy-done.9
  38.2 0.0 copy-done.12
  38.2 0.0 copy-start.10
  38.2 1.1 %copy-done.10 = f32[3,256,256]{2,1,0:T(8,128)S(1)} copy-done((f32[3,256,256]{2,1,0:T(8,128)S(1)}, f32[3,256,256]{2,1,0:T(8,128)}, u32[]{:S(2)}) %copy-start.10) | copy-done | bytes 786456
  39.3 9.5 %combine.1 = (f32[256,2048]{1,0:T(8,128)S(1)}, f32[256,2048]{1,0:T(8,128)S(1)}) custom-call(s32[1]{0:T(128)} %bitcast.3.parity, f32[3,256,256]{2,1,0:T(8,128)S(1)} %copy-done.10, f32[3,256,128]{2,1,0:T(8,128)S(1)} %get-tuple-element.14.outer_ref, f32[256,2048]{1,0:T(8,128)S(1)} %copy-done.2, f32[8,32,2048]{2,1,0:T(8,128)S(1)} %copy-done.1, ...), custom_call_target="tpu_custom_call" | custom-call | flops 1024 | bytes 1024 | tf_op jit(solution)/shard_map/combine/pallas_call | solution.py:288
  48.8 0.0 collective-permute-done.5.low_hbm
  48.8 5.2 %collective-permute-done.6.high_hbm = f32[4,32,2048]{2,1,0:T(8,128)} collective-permute-done((f32[4,32,2048]{2,1,0:T(8,128)}, f32[4,32,2048]{2,1,0:T(8,128)}, u32[]{:S(2)}, u32[]{:S(2)}) %collective-permute-start.6) | collective-permute-done | bytes 1048608 | tf_op jit(solution)/shard_map/ppermute | solution.py:592
  54.1 2.7 %finish.1 = f32[8,32,2048]{2,1,0:T(8,128)} custom-call(f32[8,32,2048]{2,1,0:T(8,128)S(1)} %bitcast.15, f32[8,32,2048]{2,1,0:T(8,128)S(1)} %bitcast.16, f32[4,32,2048]{2,1,0:T(8,128)} %collective-permute-done.5.low_hbm, f32[4,32,2048]{2,1,0:T(8,128)} %collective-permute-done.6.high_hbm), custom_call_target="tpu_custom_call" | custom-call | flops 1024 | bytes 1024 | tf_op jit(solution)/shard_map/finish/pallas_call | solution.py:364
  (9 shorter events, 0.1 us)
Async XLA Ops:
  0.6 20.8 %collective-permute-start = (f32[3,256,256]{2,1,0:T(8,128)}, f32[3,256,256]{2,1,0:T(8,128)S(1)}, u32[]{:S(2)}, u32[]{:S(2)}) collective-permute-start(f32[3,256,256]{2,1,0:T(8,128)} %bitcast.12), channel_id=1, source_target_pairs={{0,8},{4,12},{8,0},{12,4},{1,9},{5,13},{9,1},{13,5},{2,10},{6,14},... | collective-permute-start | bytes 2359304 | tf_op jit(solution)/shard_map/ppermute | solution.py:588
  4.9 1.7 %copy-start.5 = (f32[4,32,2048]{2,1,0:T(8,128)}, f32[4,32,2048]{2,1,0:T(8,128)S(1)}, u32[]{:S(2)}) copy-start(f32[4,32,2048]{2,1,0:T(8,128)S(1)} %slab.1.gate) | copy-start | bytes 3145732
  4.9 9.3 %copy-start.13 = (s32[2048]{0:T(1024)S(1)}, s32[2048]{0:T(1024)}, u32[]{:S(2)}) copy-start(s32[2048]{0:T(1024)} %param.8) | copy-start | bytes 24580
  4.9 9.3 %copy-start.14 = (f32[2048]{0:T(1024)S(1)}, f32[2048]{0:T(1024)}, u32[]{:S(2)}) copy-start(f32[2048]{0:T(1024)} %param.9) | copy-start | bytes 24580
  5.0 43.9 %collective-permute-start.5 = (f32[4,32,2048]{2,1,0:T(8,128)S(1)}, f32[4,32,2048]{2,1,0:T(8,128)}, u32[]{:S(2)}, u32[]{:S(2)}) collective-permute-start(f32[4,32,2048]{2,1,0:T(8,128)S(1)} %slab.1.gate), channel_id=1, source_target_pairs={{0,1},{1,2},{2,3},{3,0},{4,5},{5,6},{6,7},{7,4},{8,9},{9,10},{10,1... | collective-permute-start | bytes 3145736 | tf_op jit(solution)/shard_map/ppermute | solution.py:590
  9.6 15.3 %collective-permute-start.2 = (f32[8,256]{1,0:T(8,128)}, f32[8,256]{1,0:T(8,128)S(1)}, u32[]{:S(2)}, u32[]{:S(2)}) collective-permute-start(f32[8,256]{1,0:T(8,128)} %get-tuple-element.11), channel_id=1, source_target_pairs={{0,12},{4,8},{8,4},{12,0},{1,13},{5,9},{9,5},{13,1},{2,14},{6,10},... | collective-permute-start | bytes 24584 | tf_op jit(solution)/shard_map/ppermute | solution.py:593
  9.7 15.3 %collective-permute-start.3 = (f32[8,8,2048]{2,1,0:T(8,128)}, f32[8,8,2048]{2,1,0:T(8,128)S(1)}, u32[]{:S(2)}, u32[]{:S(2)}) collective-permute-start(f32[8,8,2048]{2,1,0:T(8,128)} %get-tuple-element.12), channel_id=1, source_target_pairs={{0,16},{16,0},{1,17},{17,1},{2,18},{18,2},{3,19},{19,3},{4,20},{20... | collective-permute-start | bytes 1572872 | tf_op jit(solution)/shard_map/ppermute | solution.py:595
  11.3 42.8 %collective-permute-start.6 = (f32[4,32,2048]{2,1,0:T(8,128)}, f32[4,32,2048]{2,1,0:T(8,128)}, u32[]{:S(2)}, u32[]{:S(2)}) collective-permute-start(f32[4,32,2048]{2,1,0:T(8,128)} %get-tuple-element.17), channel_id=1, source_target_pairs={{0,3},{1,0},{2,1},{3,2},{4,7},{5,4},{6,5},{7,6},{8,11},{9,8},{10,9... | collective-permute-start | bytes 3145736 | tf_op jit(solution)/shard_map/ppermute | solution.py:592
  21.5 0.9 %copy-start.3 = (f32[3,256,256]{2,1,0:T(8,128)}, f32[3,256,256]{2,1,0:T(8,128)S(1)}, u32[]{:S(2)}) copy-start(f32[3,256,256]{2,1,0:T(8,128)S(1)} %collective-permute-done.refs_1_.refs_0_) | copy-start | bytes 2359300
  22.4 6.7 %collective-permute-start.1 = (f32[776,256]{1,0:T(8,128)}, f32[776,256]{1,0:T(8,128)S(1)}, u32[]{:S(2)}, u32[]{:S(2)}) collective-permute-start(f32[776,256]{1,0:T(8,128)} %tie.2), channel_id=1, source_target_pairs={{0,4},{4,0},{8,12},{12,8},{1,5},{5,1},{9,13},{13,9},{2,6},{6,2},{1... | collective-permute-start | bytes 2383880 | tf_op jit(solution)/shard_map/ppermute | solution.py:596
  25.0 4.0 %copy-start.6 = (f32[3,256,8,32]{1,3,2,0:T(8,128)S(1)}, f32[3,256,8,32]{1,3,2,0:T(8,128)}, u32[]{:S(2)}) copy-start(f32[3,256,8,32]{1,3,2,0:T(8,128)} %param.6) | copy-start | bytes 2359300
  25.0 0.6 %copy-start.11 = (f32[8,256]{1,0:T(8,128)}, f32[8,256]{1,0:T(8,128)S(1)}, u32[]{:S(2)}) copy-start(f32[8,256]{1,0:T(8,128)S(1)} %collective-permute-done.2.refs_1_.far_ref) | copy-start | bytes 24580
  25.6 0.8 %copy-start.7 = (f32[8,8,2048]{2,1,0:T(8,128)}, f32[8,8,2048]{2,1,0:T(8,128)S(1)}, u32[]{:S(2)}) copy-start(f32[8,8,2048]{2,1,0:T(8,128)S(1)} %collective-permute-done.3.refs_3_.rows_ref) | copy-start | bytes 1572868
  26.4 2.6 %collective-permute-start.4 = (f32[3,256,256]{2,1,0:T(8,128)}, f32[3,256,256]{2,1,0:T(8,128)S(1)}, u32[]{:S(2)}, u32[]{:S(2)}) collective-permute-start(f32[3,256,256]{2,1,0:T(8,128)} %tie.3.chip_ref), channel_id=1, source_target_pairs={{0,4},{4,0},{8,12},{12,8},{1,5},{5,1},{9,13},{13,9},{2,6},{6,2},{1... | collective-permute-start | bytes 2359304 | tf_op jit(solution)/shard_map/ppermute | solution.py:598
  29.0 2.3 %copy-start = (bf16[4,768,768]{2,1,0:T(8,128)(2,1)S(1)}, bf16[4,768,768]{2,1,0:T(8,128)(2,1)}, u32[]{:S(2)}) copy-start(bf16[4,768,768]{2,1,0:T(8,128)(2,1)} %constant.129.clone.refs_0_.refs_1_.refs_2_.refs_3_) | copy-start | bytes 14155780
  31.4 1.1 %copy-start.4 = (f32[3,256,256]{2,1,0:T(8,128)S(1)}, f32[3,256,256]{2,1,0:T(8,128)}, u32[]{:S(2)}) copy-start(f32[3,256,256]{2,1,0:T(8,128)} %tie.3.chip_ref) | copy-start | bytes 2359300
  32.5 5.7 %copy-start.1 = (f32[8,32,2048]{2,1,0:T(8,128)S(1)}, f32[8,32,2048]{2,1,0:T(8,128)}, u32[]{:S(2)}) copy-start(f32[8,32,2048]{2,1,0:T(8,128)} %right_ref.1) | copy-start | bytes 6291460
  32.5 5.7 %copy-start.2 = (f32[256,2048]{1,0:T(8,128)S(1)}, f32[256,2048]{1,0:T(8,128)}, u32[]{:S(2)}) copy-start(f32[256,2048]{1,0:T(8,128)} %select_select_fusion.refs_2_.matrix_ref) | copy-start | bytes 6291460
  32.5 5.7 %copy-start.8 = (f32[8,8,2048]{2,1,0:T(8,128)S(1)}, f32[8,8,2048]{2,1,0:T(8,128)}, u32[]{:S(2)}) copy-start(f32[8,8,2048]{2,1,0:T(8,128)} %copy-done.7) | copy-start | bytes 1572868
  32.5 5.7 %copy-start.9 = (bf16[768,960]{1,0:T(8,128)(2,1)S(1)}, bf16[768,960]{1,0:T(8,128)(2,1)}, u32[]{:S(2)}) copy-start(bf16[768,960]{1,0:T(8,128)(2,1)} %constant.130.clone.table_ref) | copy-start | bytes 4423684
  32.5 5.7 %copy-start.12 = (f32[8,256]{1,0:T(8,128)S(1)}, f32[8,256]{1,0:T(8,128)}, u32[]{:S(2)}) copy-start(f32[8,256]{1,0:T(8,128)} %copy-done.11) | copy-start | bytes 24580
  38.2 1.1 %copy-start.10 = (f32[3,256,256]{2,1,0:T(8,128)S(1)}, f32[3,256,256]{2,1,0:T(8,128)}, u32[]{:S(2)}) copy-start(f32[3,256,256]{2,1,0:T(8,128)} %get-tuple-element.13.main_ref) | copy-start | bytes 2359300

commit v6 on v5

--- a/solution.py
+++ b/solution.py
@@ -316,67 +316,66 @@
     )(parity, main, outer, matrix, scalar, scalar, scalar, outer_rows, jnp.asarray(table), core, diagonal)
 
 
-def finish_kernel(chunks, part_ref, fine_ref, low_hbm, high_hbm, out_hbm, out_ref, low_ref, high_ref, in_sems, out_sems):
-    depth, _, points = part_ref.shape
-    width = points // chunks
-    spans = [pl.ds(c * width, width) for c in range(chunks)]
-    arrivals = [
-        pltpu.make_async_copy(source.at[:, :, span], target.at[:, :, span], in_sems.at[i, c])
-        for i, (source, target) in enumerate(((low_hbm, low_ref), (high_hbm, high_ref)))
-        for c, span in enumerate(spans)
-    ]
-    for copy in arrivals:
-        copy.start()
-    sends = []
-
-    def add(halo_ref, first_layer, layers, span):
-        for p in layers:
+def finish_kernel(parts, aliased, part_ref, fine_ref, *refs):
+    halos, (out_hbm, out_ref, held_ref, in_sems, out_sems) = refs[: len(parts)], refs[len(parts) + aliased :]
+    work, arrivals, sends = [], [], []
+    for i, (halo, (first_layer, begin, start, size, chunk)) in enumerate(zip(halos, parts)):
+        for x in range(0, size, chunk):
+            held = held_ref.at[i, :, :, pl.ds(x, chunk)]
+            copy = pltpu.make_async_copy(halo.at[:, :, pl.ds(x, chunk)], held, in_sems.at[len(arrivals)])
+            copy.start()
+            arrivals.append(copy)
+            work.append((i, first_layer, begin, pl.ds(x, chunk), pl.ds(start + x, chunk)))
+    for (i, first_layer, begin, held, span), arrival in zip(work, arrivals):
+        arrival.wait()
+        for p in range(begin, begin + reach):
             grade = curve = None
             for h in range(reach):
                 m = first_layer + h - p
                 if abs(m) <= reach:
-                    near = halo_ref[h, :, span]
+                    near = held_ref[i, h, :, held]
                     first = (slope[m - 1] if m > 0 else -slope[-m - 1]) * near
                     second = bend[abs(m) - 1] * near
                     grade = first if grade is None else grade + first
                     curve = second if curve is None else curve + second
             out_ref[p, :, span] = part_ref[p, :, span] + (fine_ref[p, :, span] * grade + curve)
-        at = pl.ds(layers[0], len(layers)), slice(None), span
+        at = pl.ds(begin, reach), slice(None), span
         copy = pltpu.make_async_copy(out_ref.at[at], out_hbm.at[at], out_sems.at[len(sends)])
         copy.start()
         sends.append(copy)
-
-    for arrival, span in zip(arrivals, spans):
-        arrival.wait()
-        add(low_ref, -reach, range(reach), span)
-    for arrival, span in zip(arrivals[chunks:], spans):
-        arrival.wait()
-        add(high_ref, depth, range(depth - reach, depth), span)
     for copy in sends:
         copy.wait()
 
 
-def finish_call(part, fine, low, high):
-    points = part.shape[2]
-    chunks = 4 if points % (4 * lanes) == 0 else 1
+def finish_call(part, fine, halos, started=None):
+    depth = part.shape[0]
+    parts, count = [], 0
+    for above, start, halo in halos:
+        size = halo.shape[2]
+        chunk = math.gcd(size, 512)
+        half = (depth, depth - reach) if above else (-reach, 0)
+        parts.append(half + (start, size, chunk))
+        count += size // chunk
+    aliased = started is not None
     held = pl.BlockSpec(memory_space=pltpu.VMEM)
     anywhere = pl.BlockSpec(memory_space=pl.ANY)
+    widest = max(halo.shape[2] for _, _, halo in halos)
     return pl.pallas_call(
-        functools.partial(finish_kernel, chunks),
-        in_specs=[held, held, anywhere, anywhere],
+        functools.partial(finish_kernel, parts, aliased),
+        in_specs=[held, held] + [anywhere] * (len(halos) + aliased),
         out_specs=anywhere,
         out_shape=jax.ShapeDtypeStruct(part.shape, jnp.float32),
+        input_output_aliases={2 + len(halos): 0} if aliased else {},
         scratch_shapes=[
             pltpu.VMEM(part.shape, jnp.float32),
-            pltpu.VMEM(low.shape, jnp.float32),
-            pltpu.VMEM(high.shape, jnp.float32),
-            pltpu.SemaphoreType.DMA((2, chunks)),
-            pltpu.SemaphoreType.DMA((2 * chunks,)),
+            pltpu.VMEM((len(halos), reach, part.shape[1], widest), jnp.float32),
+            pltpu.SemaphoreType.DMA((count,)),
+            pltpu.SemaphoreType.DMA((count,)),
         ],
         compiler_params=pltpu.CompilerParams(vmem_limit_bytes=vmem_bytes),
         cost_estimate=light,
         name="finish",
-    )(part, fine, low, high)
+    )(part, fine, *[halo for _, _, halo in halos], *([started] if aliased else []))
 
 
 def tie(value, *gates):
@@ -431,7 +430,7 @@
     )(scalar)
 
 
-def depart_kernel(own_hbm, scalar_hbm, gate, down_hbm, edge_hbm, sent_hbm, end_hbm,
+def depart_kernel(own_hbm, scalar_hbm, gate, down_hbm, late_hbm, edge_hbm, sent_hbm, end_hbm,
                   own_ref, scalar_ref, ends_ref, edge_ref, in_sems, out_sems):
     kinds, rows, cells = own_ref.shape
     depth, height, points = scalar_ref.shape
@@ -456,7 +455,9 @@
         send(own_ref.at[kind], sent_hbm.at[pl.ds(kind * rows, rows)])
     for copy in arrivals[:-1]:
         copy.wait()
-    send(scalar_ref.at[layers[1]], down_hbm)
+    cut = down_hbm.shape[2]
+    send(scalar_ref.at[layers[1], :, pl.ds(0, cut)], down_hbm)
+    send(scalar_ref.at[layers[1], :, pl.ds(cut, points - cut)], late_hbm)
     edge_ref[:, :reach] = scalar_ref[:, :reach]
     edge_ref[:, reach:] = scalar_ref[:, height - reach :]
     send(edge_ref, edge_hbm)
@@ -470,11 +471,11 @@
         copy.wait()
 
 
-def depart_call(own, scalar, gate):
+def depart_call(own, scalar, cut, gate):
     kinds, rows, cells = own.shape
     depth, height, points = scalar.shape
     edge, ends = (depth, 2 * reach, points), (2 * reach, cells)
-    shapes = [(reach, height, points), edge, (kinds * rows + 2 * reach, cells), ends]
+    shapes = [(reach, height, cut), (reach, height, points - cut), edge, (kinds * rows + 2 * reach, cells), ends]
     anywhere = pl.BlockSpec(memory_space=pl.ANY)
     return pl.pallas_call(
         depart_kernel,
@@ -487,7 +488,7 @@
             pltpu.VMEM(ends, jnp.float32),
             pltpu.VMEM(edge, jnp.float32),
             pltpu.SemaphoreType.DMA((4,)),
-            pltpu.SemaphoreType.DMA((4 + kinds,)),
+            pltpu.SemaphoreType.DMA((5 + kinds,)),
         ],
         compiler_params=pltpu.CompilerParams(vmem_limit_bytes=most_vmem_bytes),
         cost_estimate=light,
@@ -579,7 +580,7 @@
     points = scalar.shape[2]
     rows = depth * height
     count = lax.axis_size("blk")
-    if count != 4 or lax.axis_size("grp") != 2 or cells % lanes or rows > cells or (points // 2) % cells or depth != 2 * reach:
+    if count != 4 or lax.axis_size("grp") != 2 or cells % lanes or rows > cells or (points // 2) % cells or depth != 2 * reach or points % (8 * lanes):
         return general_per_device(velocity, scalar, spline_base, spline_frac)
     length = cells * count
     block = lax.axis_index("blk")
@@ -588,8 +589,10 @@
     chip = lax.ppermute(rows_of_x, "blk", exclusive("blk", 2))
     up = slab_call(scalar, points)
     lower = lax.ppermute(up, "dep", ring("dep", 1))
-    down, edges, own, ends = depart_call(rows_of_x, scalar, up)
+    cut = points - points // 8
+    down, late, edges, own, ends = depart_call(rows_of_x, scalar, cut, up)
     upper = lax.ppermute(down, "dep", ring("dep", -1))
+    late = lax.ppermute(late, "dep", ring("dep", -1))
     far_ends = lax.ppermute(ends, "blk", exclusive("blk", 3))
     matrix = spline_matrix(spline_base - block * cells, spline_frac, cells, points // cells)
     outer_rows = lax.ppermute(edges, "grp", ring("grp", 1))
@@ -599,7 +602,9 @@
     info = jnp.stack([(block - (block ^ j)) % count for j in range(4)] + [block % 2]).astype(jnp.int32)
     main, outer = segment_call(rows_of_x, core, chip, diagonal, info, length)
     part, vertical = combine_call(main, outer, matrix, scalar, outer_rows, core, far_ends, info[4:])
-    result = finish_call(part.reshape(scalar.shape), vertical.reshape(scalar.shape), lower, upper)
+    part, vertical = part.reshape(scalar.shape), vertical.reshape(scalar.shape)
+    result = finish_call(part, vertical, [(False, 0, lower), (True, 0, upper)])
+    result = finish_call(part, vertical, [(True, cut, late)], result)
     segment = jnp.transpose(main.reshape(kinds, depth, height, cells), (0, 3, 1, 2))
     return segment, result
 

time: 57.1 us -> 55.3 us (0.968)
  waiting for transfers between devices: 14.4 us -> 7.88 us
  starting transfers between devices: 9.7 us -> 13.6 us
  Pallas kernels: 22.1 us -> 23.1 us
    ppermute x1, waiting for transfers between devices: 5.22 us -> 0.7 us  [per_device(): upper = lax.ppermute(down, 'dep', ring('dep', -1))]
    ppermute x0 -> x1, starting transfers between devices: none -> 3.85 us  [per_device(): late = lax.ppermute(late, 'dep', ring('dep', -1))]
    ppermute x1, waiting for transfers between devices: 2.04 us -> 0.01 us  [per_device(): diagonal = lax.ppermute(chip, 'blk', exclusive('blk', 1))]
    pallas_call x1 -> x2, Pallas kernels: 2.67 us -> 3.59 us  [finish_call(): pl.pallas_call(functools.partial(finish_kernel, parts, aliased), in_specs...]
  transfers between devices with their start and end apart: 7 -> 8, of which waited for: 3 -> 2; matrix products, arithmetic and copies ran while one was open for 5% -> 5% of each run, Pallas kernels for 34% -> 40%
where the time goes in v6:
time: 55.3 us; the launch traced here: 54.9 us
  Pallas kernels  23.1 us (42%)
  starting transfers between devices  13.6 us (25%)
  waiting for transfers between devices  7.88 us (14%)
  local copies, waits for them, and re-layouts  6.97 us (13%)
  other arithmetic  2.68 us (5%)
  between operations  0.79 us (1%)
    pallas_call x1, Pallas kernels, combine_call(): pl.pallas_call(functools.partial(combine_kernel, cells // lanes), grid_sp...  9.5 us
    ppermute x1, waiting for transfers between devices, per_device(): chip = lax.ppermute(rows_of_x, 'blk', exclusive('blk', 2))  7.17 us
    unnamed x30, local copies, waits for them, and re-layouts  6.88 us
    pallas_call x1, Pallas kernels, segment_call(): pl.pallas_call(functools.partial(segment_kernel, length), grid_spec=pltpu...  5.63 us
    ppermute x1, starting transfers between devices, per_device(): late = lax.ppermute(late, 'dep', ring('dep', -1))  3.85 us
    pallas_call x2, Pallas kernels, finish_call(): pl.pallas_call(functools.partial(finish_kernel, parts, aliased), in_specs...  3.59 us
    pallas_call x1, Pallas kernels, depart_call(): pl.pallas_call(depart_kernel, in_specs=[anywhere] * 3, out_specs=[anywher...  3.05 us
    ppermute x1, starting transfers between devices, per_device(): chip = lax.ppermute(rows_of_x, 'blk', exclusive('blk', 2))  3 us
  transfers between devices with their start and end apart: 8, of which 2 were waited for; matrix products, arithmetic and copies ran while one was open for 5% of the time, Pallas kernels for 40%

profile of v6, /device:TPU:0, one launch (start us, length us, event | category | flops | bytes accessed | tf_op | source)
XLA Modules:
  0.0 54.9 jit_solution(12360179083180654130)
XLA Ops:
  0.6 3.0 %collective-permute-start = (f32[3,256,256]{2,1,0:T(8,128)}, f32[3,256,256]{2,1,0:T(8,128)S(1)}, u32[]{:S(2)}, u32[]{:S(2)}) collective-permute-start(f32[3,256,256]{2,1,0:T(8,128)} %bitcast.16), channel_id=1, source_target_pairs={{0,8},{4,12},{8,0},{12,4},{1,9},{5,13},{9,1},{13,5},{2,10},{6,14},... | collective-permute-start | bytes 2359304 | tf_op jit(solution)/shard_map/ppermute | solution.py:589
  3.6 1.3 %slab.1.gate = f32[4,32,2048]{2,1,0:T(8,128)S(1)} custom-call(f32[8,32,2048]{2,1,0:T(8,128)} %right_ref.1), custom_call_target="tpu_custom_call" | custom-call | flops 1024 | bytes 1024 | tf_op jit(solution)/shard_map/slab/pallas_call | solution.py:421
  4.9 0.0 copy-start.5
  4.9 0.0 copy-start.13
  4.9 0.0 copy-start.14
  5.0 1.6 %collective-permute-start.6 = (f32[4,32,2048]{2,1,0:T(8,128)S(1)}, f32[4,32,2048]{2,1,0:T(8,128)}, u32[]{:S(2)}, u32[]{:S(2)}) collective-permute-start(f32[4,32,2048]{2,1,0:T(8,128)S(1)} %slab.1.gate), channel_id=1, source_target_pairs={{0,1},{1,2},{2,3},{3,0},{4,5},{5,6},{6,7},{7,4},{8,9},{9,10},{10,1... | collective-permute-start | bytes 3145736 | tf_op jit(solution)/shard_map/ppermute | solution.py:591
  6.6 0.0 copy-done.5
  6.6 3.1 %depart.1 = (f32[4,32,1792]{2,1,0:T(8,128)}, f32[4,32,256]{2,1,0:T(8,128)}, f32[8,8,2048]{2,1,0:T(8,128)}, f32[776,256]{1,0:T(8,128)}, f32[8,256]{1,0:T(8,128)}) custom-call(f32[3,256,256]{2,1,0:T(8,128)} %bitcast.17, f32[8,32,2048]{2,1,0:T(8,128)} %right_ref.1, f32[4,32,2048]{2,1,0:T(8,128)} %copy-done.5), custom_call_target="tpu_custom_call" | custom-call | flops 1024 | bytes 1024 | tf_op jit(solution)/shard_map/depart/pallas_call | solution.py:480
  9.7 0.1 collective-permute-start.2
  9.7 1.6 %collective-permute-start.3 = (f32[8,8,2048]{2,1,0:T(8,128)}, f32[8,8,2048]{2,1,0:T(8,128)S(1)}, u32[]{:S(2)}, u32[]{:S(2)}) collective-permute-start(f32[8,8,2048]{2,1,0:T(8,128)} %get-tuple-element.13), channel_id=1, source_target_pairs={{0,16},{16,0},{1,17},{17,1},{2,18},{18,2},{3,19},{19,3},{4,20},{20... | collective-permute-start | bytes 1572872 | tf_op jit(solution)/shard_map/ppermute | solution.py:598
  11.3 2.9 %collective-permute-start.7 = (f32[4,32,1792]{2,1,0:T(8,128)}, f32[4,32,1792]{2,1,0:T(8,128)}, u32[]{:S(2)}, u32[]{:S(2)}) collective-permute-start(f32[4,32,1792]{2,1,0:T(8,128)} %get-tuple-element.19), channel_id=1, source_target_pairs={{0,3},{1,0},{2,1},{3,2},{4,7},{5,4},{6,5},{7,6},{8,11},{9,8},{10,9... | collective-permute-start | bytes 2752520 | tf_op jit(solution)/shard_map/ppermute | solution.py:594
  14.2 0.0 copy-done.13
  14.3 0.0 copy-done.14
  14.3 7.2 %collective-permute-done.refs_1_.refs_0_ = f32[3,256,256]{2,1,0:T(8,128)S(1)} collective-permute-done((f32[3,256,256]{2,1,0:T(8,128)}, f32[3,256,256]{2,1,0:T(8,128)S(1)}, u32[]{:S(2)}, u32[]{:S(2)}) %collective-permute-start) | collective-permute-done | bytes 786464 | tf_op jit(solution)/shard_map/ppermute | solution.py:589
  21.5 0.0 copy-start.3
  21.5 0.9 %copy-done.3 = f32[3,256,256]{2,1,0:T(8,128)} copy-done((f32[3,256,256]{2,1,0:T(8,128)}, f32[3,256,256]{2,1,0:T(8,128)S(1)}, u32[]{:S(2)}) %copy-start.3) | copy-done | bytes 786456
  22.4 0.0 collective-permute-start.1
  22.4 2.6 %select_select_fusion.refs_2_.matrix_ref = f32[256,2048]{1,0:T(8,128)} fusion(f32[2048]{0:T(1024)S(1)} %get-tuple-element.22, f32[2048]{0:T(1024)S(1)} %get-tuple-element.21, f32[2048]{0:T(1024)S(1)} %get-tuple-element.23, f32[2048]{0:T(1024)S(1)} %get-tuple-element.20, s32[2048]{0:T(1024)S(1)} %get-tuple-element.25, s32[2048]{0:T(1024)S(1)} %get-tuple-element.24, ...), kind=kLoop, calls=%fused_computation.10 | loop fusion | flops 8388608 | bytes 2154752 | tf_op jit(solution)/shard_map/jit(_where)/select_n | solution.py:194
  25.0 0.0 copy-start.6
  25.0 0.0 collective-permute-done.2.refs_1_.far_ref
  25.0 0.0 copy-start.11
  25.0 0.0 collective-permute-done.3.refs_3_.rows_ref
  25.0 0.6 %copy-done.11 = f32[8,256]{1,0:T(8,128)} copy-done((f32[8,256]{1,0:T(8,128)}, f32[8,256]{1,0:T(8,128)S(1)}, u32[]{:S(2)}) %copy-start.11) | copy-done | bytes 8216
  25.6 0.8 %copy-done.7 = f32[8,8,2048]{2,1,0:T(8,128)} copy-done((f32[8,8,2048]{2,1,0:T(8,128)}, f32[8,8,2048]{2,1,0:T(8,128)S(1)}, u32[]{:S(2)}) %copy-start.7) | copy-done | bytes 524312
  26.4 0.5 collective-permute-start.4
  26.9 3.8 %collective-permute-start.5 = (f32[4,32,256]{2,1,0:T(8,128)}, f32[4,32,256]{2,1,0:T(8,128)S(1)}, u32[]{:S(2)}, u32[]{:S(2)}) collective-permute-start(f32[4,32,256]{2,1,0:T(8,128)} %get-tuple-element.18), channel_id=1, source_target_pairs={{0,3},{1,0},{2,1},{3,2},{4,7},{5,4},{6,5},{7,6},{8,11},{9,8},{10,9... | collective-permute-start | bytes 393224 | tf_op jit(solution)/shard_map/ppermute | solution.py:595
  30.7 0.1 stack.20.info
  30.8 0.0 collective-permute-done.4.far_ref
  30.8 0.0 collective-permute-done.1.core_ref
  30.8 0.0 copy-done.6
  30.8 0.0 copy-start
  30.8 2.3 %copy-done = bf16[4,768,768]{2,1,0:T(8,128)(2,1)S(1)} copy-done((bf16[4,768,768]{2,1,0:T(8,128)(2,1)S(1)}, bf16[4,768,768]{2,1,0:T(8,128)(2,1)}, u32[]{:S(2)}) %copy-start) | copy-done | bytes 4718616
  33.2 1.1 %copy-done.4 = f32[3,256,256]{2,1,0:T(8,128)S(1)} copy-done((f32[3,256,256]{2,1,0:T(8,128)S(1)}, f32[3,256,256]{2,1,0:T(8,128)}, u32[]{:S(2)}) %copy-start.4) | copy-done | bytes 786456
  34.3 0.0 copy-start.12
  34.3 5.6 %segment.1 = (f32[3,256,256]{2,1,0:T(8,128)}, f32[3,256,128]{2,1,0:T(8,128)S(1)}) custom-call(s32[5]{0:T(128)S(1)} %stack.20.info, f32[3,256,256]{2,1,0:T(8,128)S(1)} %bitcast.18, f32[776,256]{1,0:T(8,128)S(1)} %collective-permute-done.1.core_ref, f32[3,256,256]{2,1,0:T(8,128)S(1)} %copy-done.4, f32[3,256,256]{2,1,0:T(8,128)S(1)} %collective-permute-done.4.far_ref, ...), custom_call_target="tpu_custom_call" | custom-call | flops 1024 | bytes 1024 | tf_op jit(solution)/shard_map/segment/pallas_call | solution.py:154
  40.0 0.0 copy-done.1
  40.0 0.0 copy-done.2
  40.0 0.0 copy-done.8
  40.0 0.0 copy-done.9
  40.0 0.0 copy-done.12
  40.0 0.0 copy-start.10
  40.0 1.1 %copy-done.10 = f32[3,256,256]{2,1,0:T(8,128)S(1)} copy-done((f32[3,256,256]{2,1,0:T(8,128)S(1)}, f32[3,256,256]{2,1,0:T(8,128)}, u32[]{:S(2)}) %copy-start.10) | copy-done | bytes 786456
  41.1 9.5 %combine.1 = (f32[256,2048]{1,0:T(8,128)S(1)}, f32[256,2048]{1,0:T(8,128)S(1)}) custom-call(s32[1]{0:T(128)} %bitcast.3.parity, f32[3,256,256]{2,1,0:T(8,128)S(1)} %copy-done.10, f32[3,256,128]{2,1,0:T(8,128)S(1)} %get-tuple-element.15.outer_ref, f32[256,2048]{1,0:T(8,128)S(1)} %copy-done.2, f32[8,32,2048]{2,1,0:T(8,128)S(1)} %copy-done.1, ...), custom_call_target="tpu_custom_call" | custom-call | flops 1024 | bytes 1024 | tf_op jit(solution)/shard_map/combine/pallas_call | solution.py:288
  50.6 0.7 %collective-permute-done.7.refs_1_ = f32[4,32,1792]{2,1,0:T(8,128)} collective-permute-done((f32[4,32,1792]{2,1,0:T(8,128)}, f32[4,32,1792]{2,1,0:T(8,128)}, u32[]{:S(2)}, u32[]{:S(2)}) %collective-permute-start.7) | collective-permute-done | bytes 917536 | tf_op jit(solution)/shard_map/ppermute | solution.py:594
  51.3 0.0 collective-permute-done.6.refs_0_
  51.3 2.7 %finish.2.refs_1_ = f32[8,32,2048]{2,1,0:T(8,128)} custom-call(f32[8,32,2048]{2,1,0:T(8,128)S(1)} %bitcast.12, f32[8,32,2048]{2,1,0:T(8,128)S(1)} %bitcast.14, f32[4,32,2048]{2,1,0:T(8,128)} %collective-permute-done.6.refs_0_, f32[4,32,1792]{2,1,0:T(8,128)} %collective-permute-done.7.refs_1_), custom_call_target="tpu_custom_call" | custom-call | flops 1024 | bytes 1024 | tf_op jit(solution)/shard_map/finish/pallas_call | solution.py:363
  54.0 0.0 collective-permute-done.5.refs_0_
  54.0 0.9 %finish.3 = f32[8,32,2048]{2,1,0:T(8,128)} custom-call(f32[8,32,2048]{2,1,0:T(8,128)S(1)} %bitcast.13, f32[8,32,2048]{2,1,0:T(8,128)S(1)} %bitcast.15, f32[4,32,256]{2,1,0:T(8,128)S(1)} %collective-permute-done.5.refs_0_, f32[8,32,2048]{2,1,0:T(8,128)} %finish.2.refs_1_), custom_call_target="tpu_custom_call", output_to_operand_aliasing={{}: (3, {})} | custom-call | flops 1024 | bytes 1024 | tf_op jit(solution)/shard_map/finish/pallas_call | solution.py:363
  (12 shorter events, 0.1 us)
Async XLA Ops:
  0.6 20.8 %collective-permute-start = (f32[3,256,256]{2,1,0:T(8,128)}, f32[3,256,256]{2,1,0:T(8,128)S(1)}, u32[]{:S(2)}, u32[]{:S(2)}) collective-permute-start(f32[3,256,256]{2,1,0:T(8,128)} %bitcast.16), channel_id=1, source_target_pairs={{0,8},{4,12},{8,0},{12,4},{1,9},{5,13},{9,1},{13,5},{2,10},{6,14},... | collective-permute-start | bytes 2359304 | tf_op jit(solution)/shard_map/ppermute | solution.py:589
  4.9 1.7 %copy-start.5 = (f32[4,32,2048]{2,1,0:T(8,128)}, f32[4,32,2048]{2,1,0:T(8,128)S(1)}, u32[]{:S(2)}) copy-start(f32[4,32,2048]{2,1,0:T(8,128)S(1)} %slab.1.gate) | copy-start | bytes 3145732
  4.9 9.3 %copy-start.13 = (s32[2048]{0:T(1024)S(1)}, s32[2048]{0:T(1024)}, u32[]{:S(2)}) copy-start(s32[2048]{0:T(1024)} %param.8) | copy-start | bytes 24580
  4.9 9.3 %copy-start.14 = (f32[2048]{0:T(1024)S(1)}, f32[2048]{0:T(1024)}, u32[]{:S(2)}) copy-start(f32[2048]{0:T(1024)} %param.9) | copy-start | bytes 24580
  5.0 46.4 %collective-permute-start.6 = (f32[4,32,2048]{2,1,0:T(8,128)S(1)}, f32[4,32,2048]{2,1,0:T(8,128)}, u32[]{:S(2)}, u32[]{:S(2)}) collective-permute-start(f32[4,32,2048]{2,1,0:T(8,128)S(1)} %slab.1.gate), channel_id=1, source_target_pairs={{0,1},{1,2},{2,3},{3,0},{4,5},{5,6},{6,7},{7,4},{8,9},{9,10},{10,1... | collective-permute-start | bytes 3145736 | tf_op jit(solution)/shard_map/ppermute | solution.py:591
  9.7 15.3 %collective-permute-start.2 = (f32[8,256]{1,0:T(8,128)}, f32[8,256]{1,0:T(8,128)S(1)}, u32[]{:S(2)}, u32[]{:S(2)}) collective-permute-start(f32[8,256]{1,0:T(8,128)} %get-tuple-element.12), channel_id=1, source_target_pairs={{0,12},{4,8},{8,4},{12,0},{1,13},{5,9},{9,5},{13,1},{2,14},{6,10},... | collective-permute-start | bytes 24584 | tf_op jit(solution)/shard_map/ppermute | solution.py:596
  9.7 15.3 %collective-permute-start.3 = (f32[8,8,2048]{2,1,0:T(8,128)}, f32[8,8,2048]{2,1,0:T(8,128)S(1)}, u32[]{:S(2)}, u32[]{:S(2)}) collective-permute-start(f32[8,8,2048]{2,1,0:T(8,128)} %get-tuple-element.13), channel_id=1, source_target_pairs={{0,16},{16,0},{1,17},{17,1},{2,18},{18,2},{3,19},{19,3},{4,20},{20... | collective-permute-start | bytes 1572872 | tf_op jit(solution)/shard_map/ppermute | solution.py:598
  11.3 40.0 %collective-permute-start.7 = (f32[4,32,1792]{2,1,0:T(8,128)}, f32[4,32,1792]{2,1,0:T(8,128)}, u32[]{:S(2)}, u32[]{:S(2)}) collective-permute-start(f32[4,32,1792]{2,1,0:T(8,128)} %get-tuple-element.19), channel_id=1, source_target_pairs={{0,3},{1,0},{2,1},{3,2},{4,7},{5,4},{6,5},{7,6},{8,11},{9,8},{10,9... | collective-permute-start | bytes 2752520 | tf_op jit(solution)/shard_map/ppermute | solution.py:594
  21.5 0.9 %copy-start.3 = (f32[3,256,256]{2,1,0:T(8,128)}, f32[3,256,256]{2,1,0:T(8,128)S(1)}, u32[]{:S(2)}) copy-start(f32[3,256,256]{2,1,0:T(8,128)S(1)} %collective-permute-done.refs_1_.refs_0_) | copy-start | bytes 2359300
  22.4 8.5 %collective-permute-start.1 = (f32[776,256]{1,0:T(8,128)}, f32[776,256]{1,0:T(8,128)S(1)}, u32[]{:S(2)}, u32[]{:S(2)}) collective-permute-start(f32[776,256]{1,0:T(8,128)} %tie.2), channel_id=1, source_target_pairs={{0,4},{4,0},{8,12},{12,8},{1,5},{5,1},{9,13},{13,9},{2,6},{6,2},{1... | collective-permute-start | bytes 2383880 | tf_op jit(solution)/shard_map/ppermute | solution.py:599
  25.0 5.8 %copy-start.6 = (f32[3,256,8,32]{1,3,2,0:T(8,128)S(1)}, f32[3,256,8,32]{1,3,2,0:T(8,128)}, u32[]{:S(2)}) copy-start(f32[3,256,8,32]{1,3,2,0:T(8,128)} %param.6) | copy-start | bytes 2359300
  25.0 0.6 %copy-start.11 = (f32[8,256]{1,0:T(8,128)}, f32[8,256]{1,0:T(8,128)S(1)}, u32[]{:S(2)}) copy-start(f32[8,256]{1,0:T(8,128)S(1)} %collective-permute-done.2.refs_1_.far_ref) | copy-start | bytes 24580
  25.6 0.8 %copy-start.7 = (f32[8,8,2048]{2,1,0:T(8,128)}, f32[8,8,2048]{2,1,0:T(8,128)S(1)}, u32[]{:S(2)}) copy-start(f32[8,8,2048]{2,1,0:T(8,128)S(1)} %collective-permute-done.3.refs_3_.rows_ref) | copy-start | bytes 1572868
  26.4 4.4 %collective-permute-start.4 = (f32[3,256,256]{2,1,0:T(8,128)}, f32[3,256,256]{2,1,0:T(8,128)S(1)}, u32[]{:S(2)}, u32[]{:S(2)}) collective-permute-start(f32[3,256,256]{2,1,0:T(8,128)} %tie.3.chip_ref), channel_id=1, source_target_pairs={{0,4},{4,0},{8,12},{12,8},{1,5},{5,1},{9,13},{13,9},{2,6},{6,2},{1... | collective-permute-start | bytes 2359304 | tf_op jit(solution)/shard_map/ppermute | solution.py:601
  26.9 27.1 %collective-permute-start.5 = (f32[4,32,256]{2,1,0:T(8,128)}, f32[4,32,256]{2,1,0:T(8,128)S(1)}, u32[]{:S(2)}, u32[]{:S(2)}) collective-permute-start(f32[4,32,256]{2,1,0:T(8,128)} %get-tuple-element.18), channel_id=1, source_target_pairs={{0,3},{1,0},{2,1},{3,2},{4,7},{5,4},{6,5},{7,6},{8,11},{9,8},{10,9... | collective-permute-start | bytes 393224 | tf_op jit(solution)/shard_map/ppermute | solution.py:595
  30.8 2.3 %copy-start = (bf16[4,768,768]{2,1,0:T(8,128)(2,1)S(1)}, bf16[4,768,768]{2,1,0:T(8,128)(2,1)}, u32[]{:S(2)}) copy-start(bf16[4,768,768]{2,1,0:T(8,128)(2,1)} %constant.129.clone.refs_0_.refs_1_.refs_2_.refs_3_) | copy-start | bytes 14155780
  33.2 1.1 %copy-start.4 = (f32[3,256,256]{2,1,0:T(8,128)S(1)}, f32[3,256,256]{2,1,0:T(8,128)}, u32[]{:S(2)}) copy-start(f32[3,256,256]{2,1,0:T(8,128)} %tie.3.chip_ref) | copy-start | bytes 2359300
  34.3 5.7 %copy-start.1 = (f32[8,32,2048]{2,1,0:T(8,128)S(1)}, f32[8,32,2048]{2,1,0:T(8,128)}, u32[]{:S(2)}) copy-start(f32[8,32,2048]{2,1,0:T(8,128)} %right_ref.1) | copy-start | bytes 6291460
  34.3 5.7 %copy-start.2 = (f32[256,2048]{1,0:T(8,128)S(1)}, f32[256,2048]{1,0:T(8,128)}, u32[]{:S(2)}) copy-start(f32[256,2048]{1,0:T(8,128)} %select_select_fusion.refs_2_.matrix_ref) | copy-start | bytes 6291460
  34.3 5.7 %copy-start.8 = (f32[8,8,2048]{2,1,0:T(8,128)S(1)}, f32[8,8,2048]{2,1,0:T(8,128)}, u32[]{:S(2)}) copy-start(f32[8,8,2048]{2,1,0:T(8,128)} %copy-done.7) | copy-start | bytes 1572868
  34.3 5.7 %copy-start.9 = (bf16[768,960]{1,0:T(8,128)(2,1)S(1)}, bf16[768,960]{1,0:T(8,128)(2,1)}, u32[]{:S(2)}) copy-start(bf16[768,960]{1,0:T(8,128)(2,1)} %constant.130.clone.table_ref) | copy-start | bytes 4423684
  34.3 5.7 %copy-start.12 = (f32[8,256]{1,0:T(8,128)S(1)}, f32[8,256]{1,0:T(8,128)}, u32[]{:S(2)}) copy-start(f32[8,256]{1,0:T(8,128)} %copy-done.11) | copy-start | bytes 24580
  40.0 1.1 %copy-start.10 = (f32[3,256,256]{2,1,0:T(8,128)S(1)}, f32[3,256,256]{2,1,0:T(8,128)}, u32[]{:S(2)}) copy-start(f32[3,256,256]{2,1,0:T(8,128)} %get-tuple-element.14.main_ref) | copy-start | bytes 2359300

commit v7 on v6

--- a/solution.py
+++ b/solution.py
@@ -24,7 +24,7 @@
 centre_weight = 1.0 + 3.0 * diffuse_rate * second_centre
 highest = lax.Precision.HIGHEST
 reach = 4
-slab_chunks = 4
+slab_chunks = 2
 lanes = 128
 vmem_bytes = 32 * 1024 * 1024
 most_vmem_bytes = 60 * 1024 * 1024
@@ -316,24 +316,30 @@
     )(parity, main, outer, matrix, scalar, scalar, scalar, outer_rows, jnp.asarray(table), core, diagonal)
 
 
-def finish_kernel(parts, aliased, part_ref, fine_ref, *refs):
+def finish_kernel(parts, aliased, direct, part_ref, fine_ref, *refs):
     halos, (out_hbm, out_ref, held_ref, in_sems, out_sems) = refs[: len(parts)], refs[len(parts) + aliased :]
     work, arrivals, sends = [], [], []
     for i, (halo, (first_layer, begin, start, size, chunk)) in enumerate(zip(halos, parts)):
         for x in range(0, size, chunk):
-            held = held_ref.at[i, :, :, pl.ds(x, chunk)]
-            copy = pltpu.make_async_copy(halo.at[:, :, pl.ds(x, chunk)], held, in_sems.at[len(arrivals)])
+            span, place = pl.ds(x, chunk), pl.ds(start + x, chunk)
+            if direct:
+                work.append((halo, first_layer, begin, span, place))
+                continue
+            copy = pltpu.make_async_copy(
+                halo.at[:, :, span], held_ref.at[i, :, :, span], in_sems.at[len(arrivals)]
+            )
             copy.start()
             arrivals.append(copy)
-            work.append((i, first_layer, begin, pl.ds(x, chunk), pl.ds(start + x, chunk)))
-    for (i, first_layer, begin, held, span), arrival in zip(work, arrivals):
-        arrival.wait()
+            work.append((held_ref.at[i], first_layer, begin, span, place))
+    for c, (near_ref, first_layer, begin, held, span) in enumerate(work):
+        if not direct:
+            arrivals[c].wait()
         for p in range(begin, begin + reach):
             grade = curve = None
             for h in range(reach):
                 m = first_layer + h - p
                 if abs(m) <= reach:
-                    near = held_ref[i, h, :, held]
+                    near = near_ref[h, :, held]
                     first = (slope[m - 1] if m > 0 else -slope[-m - 1]) * near
                     second = bend[abs(m) - 1] * near
                     grade = first if grade is None else grade + first
@@ -361,8 +367,8 @@
     anywhere = pl.BlockSpec(memory_space=pl.ANY)
     widest = max(halo.shape[2] for _, _, halo in halos)
     return pl.pallas_call(
-        functools.partial(finish_kernel, parts, aliased),
-        in_specs=[held, held] + [anywhere] * (len(halos) + aliased),
+        functools.partial(finish_kernel, parts, aliased, aliased),
+        in_specs=[held, held] + [held if aliased else anywhere] * len(halos) + [anywhere] * aliased,
         out_specs=anywhere,
         out_shape=jax.ShapeDtypeStruct(part.shape, jnp.float32),
         input_output_aliases={2 + len(halos): 0} if aliased else {},
@@ -393,8 +399,8 @@
 
 def slab_kernel(begin, source_hbm, out_ref, held_ref, in_sems, out_sems):
     layers, _, points = held_ref.shape
-    width = points // slab_chunks
-    spans = [pl.ds(c * width, width) for c in range(slab_chunks)]
+    share = points // slab_chunks
+    spans = [pl.ds(c * share, share) for c in range(slab_chunks)]
     arrivals = [
         pltpu.make_async_copy(
             source_hbm.at[pl.ds(begin, layers), :, span], held_ref.at[:, :, span], in_sems.at[c]
@@ -430,7 +436,7 @@
     )(scalar)
 
 
-def depart_kernel(own_hbm, scalar_hbm, gate, down_hbm, late_hbm, edge_hbm, sent_hbm, end_hbm,
+def depart_kernel(own_hbm, scalar_hbm, gate, down_hbm, late_down_hbm, late_up_hbm, edge_hbm, sent_hbm, end_hbm,
                   own_ref, scalar_ref, ends_ref, edge_ref, in_sems, out_sems):
     kinds, rows, cells = own_ref.shape
     depth, height, points = scalar_ref.shape
@@ -457,7 +463,8 @@
         copy.wait()
     cut = down_hbm.shape[2]
     send(scalar_ref.at[layers[1], :, pl.ds(0, cut)], down_hbm)
-    send(scalar_ref.at[layers[1], :, pl.ds(cut, points - cut)], late_hbm)
+    send(scalar_ref.at[layers[1], :, pl.ds(cut, points - cut)], late_down_hbm)
+    send(scalar_ref.at[layers[0], :, pl.ds(cut, points - cut)], late_up_hbm)
     edge_ref[:, :reach] = scalar_ref[:, :reach]
     edge_ref[:, reach:] = scalar_ref[:, height - reach :]
     send(edge_ref, edge_hbm)
@@ -475,7 +482,7 @@
     kinds, rows, cells = own.shape
     depth, height, points = scalar.shape
     edge, ends = (depth, 2 * reach, points), (2 * reach, cells)
-    shapes = [(reach, height, cut), (reach, height, points - cut), edge, (kinds * rows + 2 * reach, cells), ends]
+    shapes = [(reach, height, cut)] + [(reach, height, points - cut)] * 2 + [edge, (kinds * rows + 2 * reach, cells), ends]
     anywhere = pl.BlockSpec(memory_space=pl.ANY)
     return pl.pallas_call(
         depart_kernel,
@@ -488,7 +495,7 @@
             pltpu.VMEM(ends, jnp.float32),
             pltpu.VMEM(edge, jnp.float32),
             pltpu.SemaphoreType.DMA((4,)),
-            pltpu.SemaphoreType.DMA((5 + kinds,)),
+            pltpu.SemaphoreType.DMA((6 + kinds,)),
         ],
         compiler_params=pltpu.CompilerParams(vmem_limit_bytes=most_vmem_bytes),
         cost_estimate=light,
@@ -587,24 +594,25 @@
 
     rows_of_x = jnp.transpose(velocity, (0, 2, 3, 1)).reshape(kinds, rows, cells)
     chip = lax.ppermute(rows_of_x, "blk", exclusive("blk", 2))
-    up = slab_call(scalar, points)
+    cut = points - points // 8
+    up = slab_call(scalar, cut)
     lower = lax.ppermute(up, "dep", ring("dep", 1))
-    cut = points - points // 8
-    down, late, edges, own, ends = depart_call(rows_of_x, scalar, cut, up)
+    down, late_down, late_up, edges, own, ends = depart_call(rows_of_x, scalar, cut, up)
     upper = lax.ppermute(down, "dep", ring("dep", -1))
-    late = lax.ppermute(late, "dep", ring("dep", -1))
+    late_upper = lax.ppermute(late_down, "dep", ring("dep", -1))
     far_ends = lax.ppermute(ends, "blk", exclusive("blk", 3))
     matrix = spline_matrix(spline_base - block * cells, spline_frac, cells, points // cells)
     outer_rows = lax.ppermute(edges, "grp", ring("grp", 1))
     core = lax.ppermute(tie(own, chip), "blk", exclusive("blk", 1))
     chip = tie(chip, far_ends, matrix, outer_rows)
     diagonal = lax.ppermute(chip, "blk", exclusive("blk", 1))
+    late_lower = lax.ppermute(tie(late_up, diagonal), "dep", ring("dep", 1))
     info = jnp.stack([(block - (block ^ j)) % count for j in range(4)] + [block % 2]).astype(jnp.int32)
     main, outer = segment_call(rows_of_x, core, chip, diagonal, info, length)
     part, vertical = combine_call(main, outer, matrix, scalar, outer_rows, core, far_ends, info[4:])
     part, vertical = part.reshape(scalar.shape), vertical.reshape(scalar.shape)
     result = finish_call(part, vertical, [(False, 0, lower), (True, 0, upper)])
-    result = finish_call(part, vertical, [(True, cut, late)], result)
+    result = finish_call(part, vertical, [(False, cut, late_lower), (True, cut, late_upper)], result)
     segment = jnp.transpose(main.reshape(kinds, depth, height, cells), (0, 3, 1, 2))
     return segment, result
 

time: 55.3 us -> 55.1 us (level)
  local copies, waits for them, and re-layouts: 6.97 us -> 8.42 us
  waiting for transfers between devices: 7.88 us -> 6.81 us
    ppermute x1, waiting for transfers between devices: 7.17 us -> 4.6 us  [per_device(): chip = lax.ppermute(rows_of_x, 'blk', exclusive('blk', 2))]
    ppermute x1, waiting for transfers between devices: 0.01 us -> 2.02 us  [per_device(): outer_rows = lax.ppermute(edges, 'grp', ring('grp', 1))]
    unnamed x30 -> x34, local copies, waits for them, and re-layouts: 6.88 us -> 8.34 us
    ppermute x1, waiting for transfers between devices: 0.7 us -> 0.01 us  [per_device(): upper = lax.ppermute(down, 'dep', ring('dep', -1))]
    ppermute x1 -> x2, starting transfers between devices: 3.85 us -> 3.56 us  [the longest x1 2.86 us: per_device(): late_upper = lax.ppermute(late_down, 'dep', ring('dep', -1))]
  transfers between devices with their start and end apart: 8 -> 9, of which waited for: 2 -> 3; matrix products, arithmetic and copies ran while one was open for 5% -> 5% of each run, Pallas kernels for 40% -> 40%
where the time goes in v7:
time: 55.1 us; the launch traced here: 54.8 us
  Pallas kernels  22.8 us (41%)
  starting transfers between devices  13.2 us (24%)
  local copies, waits for them, and re-layouts  8.42 us (15%)
  waiting for transfers between devices  6.81 us (12%)
  other arithmetic  2.68 us (5%)
  between operations  0.81 us (1%)
    pallas_call x1, Pallas kernels, combine_call(): pl.pallas_call(functools.partial(combine_kernel, cells // lanes), grid_sp...  9.5 us
    unnamed x34, local copies, waits for them, and re-layouts  8.34 us
    pallas_call x1, Pallas kernels, segment_call(): pl.pallas_call(functools.partial(segment_kernel, length), grid_spec=pltpu...  5.53 us
    ppermute x1, waiting for transfers between devices, per_device(): chip = lax.ppermute(rows_of_x, 'blk', exclusive('blk', 2))  4.6 us
    pallas_call x2, Pallas kernels, finish_call(): pl.pallas_call(functools.partial(finish_kernel, parts, aliased, aliased),...  3.47 us
    pallas_call x1, Pallas kernels, depart_call(): pl.pallas_call(depart_kernel, in_specs=[anywhere] * 3, out_specs=[anywher...  3.09 us
    ppermute x1, starting transfers between devices, per_device(): chip = lax.ppermute(rows_of_x, 'blk', exclusive('blk', 2))  3 us
    ppermute x1, starting transfers between devices, per_device(): upper = lax.ppermute(down, 'dep', ring('dep', -1))  2.86 us
  transfers between devices with their start and end apart: 9, of which 3 were waited for; matrix products, arithmetic and copies ran while one was open for 5% of the time, Pallas kernels for 40%

profile of v7, /device:TPU:0, one launch (start us, length us, event | category | flops | bytes accessed | tf_op | source)
XLA Modules:
  0.0 54.8 jit_solution(7174380655506674871)
XLA Ops:
  0.6 3.0 %collective-permute-start = (f32[3,256,256]{2,1,0:T(8,128)}, f32[3,256,256]{2,1,0:T(8,128)S(1)}, u32[]{:S(2)}, u32[]{:S(2)}) collective-permute-start(f32[3,256,256]{2,1,0:T(8,128)} %bitcast.16), channel_id=1, source_target_pairs={{0,8},{4,12},{8,0},{12,4},{1,9},{5,13},{9,1},{13,5},{2,10},{6,14},... | collective-permute-start | bytes 2359304 | tf_op jit(solution)/shard_map/ppermute | solution.py:596
  3.6 1.2 %slab.1.gate = f32[4,32,1792]{2,1,0:T(8,128)S(1)} custom-call(f32[8,32,2048]{2,1,0:T(8,128)} %right_ref.1), custom_call_target="tpu_custom_call" | custom-call | flops 1024 | bytes 1024 | tf_op jit(solution)/shard_map/slab/pallas_call | solution.py:427
  4.9 0.0 copy-start.5
  4.9 0.0 copy-start.15
  4.9 0.0 copy-start.16
  4.9 1.6 %collective-permute-start.7 = (f32[4,32,1792]{2,1,0:T(8,128)S(1)}, f32[4,32,1792]{2,1,0:T(8,128)}, u32[]{:S(2)}, u32[]{:S(2)}) collective-permute-start(f32[4,32,1792]{2,1,0:T(8,128)S(1)} %slab.1.gate), channel_id=1, source_target_pairs={{0,1},{1,2},{2,3},{3,0},{4,5},{5,6},{6,7},{7,4},{8,9},{9,10},{10,1... | collective-permute-start | bytes 2752520 | tf_op jit(solution)/shard_map/ppermute | solution.py:599
  6.5 0.0 copy-done.5
  6.5 3.1 %depart.1 = (f32[4,32,1792]{2,1,0:T(8,128)}, f32[4,32,256]{2,1,0:T(8,128)}, f32[4,32,256]{2,1,0:T(8,128)}, f32[8,8,2048]{2,1,0:T(8,128)}, f32[776,256]{1,0:T(8,128)}, /*index=5*/f32[8,256]{1,0:T(8,128)}) custom-call(f32[3,256,256]{2,1,0:T(8,128)} %bitcast.17, f32[8,32,2048]{2,1,0:T(8,128)} %right_ref.1, f32[4,32,1792]{2,1,0:T(8,128)} %copy-done.5), custom_call_target="tpu_custom_call" | custom-call | flops 1024 | bytes 1024 | tf_op jit(solution)/shard_map/depart/pallas_call | solution.py:487
  9.6 0.1 collective-permute-start.2
  9.7 1.6 %collective-permute-start.3 = (f32[8,8,2048]{2,1,0:T(8,128)}, f32[8,8,2048]{2,1,0:T(8,128)S(1)}, u32[]{:S(2)}, u32[]{:S(2)}) collective-permute-start(f32[8,8,2048]{2,1,0:T(8,128)} %get-tuple-element.14), channel_id=1, source_target_pairs={{0,16},{16,0},{1,17},{17,1},{2,18},{18,2},{3,19},{19,3},{4,20},{20... | collective-permute-start | bytes 1572872 | tf_op jit(solution)/shard_map/ppermute | solution.py:605
  11.3 2.9 %collective-permute-start.8 = (f32[4,32,1792]{2,1,0:T(8,128)}, f32[4,32,1792]{2,1,0:T(8,128)}, u32[]{:S(2)}, u32[]{:S(2)}) collective-permute-start(f32[4,32,1792]{2,1,0:T(8,128)} %get-tuple-element.21), channel_id=1, source_target_pairs={{0,3},{1,0},{2,1},{3,2},{4,7},{5,4},{6,5},{7,6},{8,11},{9,8},{10,9... | collective-permute-start | bytes 2752520 | tf_op jit(solution)/shard_map/ppermute | solution.py:601
  14.2 0.0 copy-done.15
  14.2 0.0 copy-done.16
  14.2 2.6 %select_select_fusion.refs_2_.matrix_ref = f32[256,2048]{1,0:T(8,128)} fusion(f32[2048]{0:T(1024)S(1)} %get-tuple-element.24, f32[2048]{0:T(1024)S(1)} %get-tuple-element.23, f32[2048]{0:T(1024)S(1)} %get-tuple-element.25, f32[2048]{0:T(1024)S(1)} %get-tuple-element.22, s32[2048]{0:T(1024)S(1)} %get-tuple-element.27, s32[2048]{0:T(1024)S(1)} %get-tuple-element.26, ...), kind=kLoop, calls=%fused_computation.10 | loop fusion | flops 8388608 | bytes 2154752 | tf_op jit(solution)/shard_map/jit(_where)/select_n | solution.py:194
  16.9 4.6 %collective-permute-done.refs_1_.refs_0_ = f32[3,256,256]{2,1,0:T(8,128)S(1)} collective-permute-done((f32[3,256,256]{2,1,0:T(8,128)}, f32[3,256,256]{2,1,0:T(8,128)S(1)}, u32[]{:S(2)}, u32[]{:S(2)}) %collective-permute-start) | collective-permute-done | bytes 786464 | tf_op jit(solution)/shard_map/ppermute | solution.py:596
  21.5 0.9 %copy-done.3 = f32[3,256,256]{2,1,0:T(8,128)} copy-done((f32[3,256,256]{2,1,0:T(8,128)}, f32[3,256,256]{2,1,0:T(8,128)S(1)}, u32[]{:S(2)}) %copy-start.3) | copy-done | bytes 786456
  22.4 0.0 collective-permute-done.2.refs_1_.far_ref
  22.4 2.0 %collective-permute-done.3.refs_3_.rows_ref = f32[8,8,2048]{2,1,0:T(8,128)S(1)} collective-permute-done((f32[8,8,2048]{2,1,0:T(8,128)}, f32[8,8,2048]{2,1,0:T(8,128)S(1)}, u32[]{:S(2)}, u32[]{:S(2)}) %collective-permute-start.3) | collective-permute-done | bytes 524320 | tf_op jit(solution)/shard_map/ppermute | solution.py:605
  24.4 0.0 copy-done.13
  24.4 0.8 %copy-done.9 = f32[8,8,2048]{2,1,0:T(8,128)} copy-done((f32[8,8,2048]{2,1,0:T(8,128)}, f32[8,8,2048]{2,1,0:T(8,128)S(1)}, u32[]{:S(2)}) %copy-start.9) | copy-done | bytes 524312
  25.2 0.0 collective-permute-start.4
  25.2 0.5 collective-permute-start.1
  25.7 2.9 %collective-permute-start.6 = (f32[4,32,256]{2,1,0:T(8,128)}, f32[4,32,256]{2,1,0:T(8,128)S(1)}, u32[]{:S(2)}, u32[]{:S(2)}) collective-permute-start(f32[4,32,256]{2,1,0:T(8,128)} %get-tuple-element.20), channel_id=1, source_target_pairs={{0,3},{1,0},{2,1},{3,2},{4,7},{5,4},{6,5},{7,6},{8,11},{9,8},{10,9... | collective-permute-start | bytes 393224 | tf_op jit(solution)/shard_map/ppermute | solution.py:602
  28.6 0.0 collective-permute-done.4.far_ref.refs_1_
  28.6 0.9 %copy-done.6 = f32[3,256,256]{2,1,0:T(8,128)} copy-done((f32[3,256,256]{2,1,0:T(8,128)}, f32[3,256,256]{2,1,0:T(8,128)S(1)}, u32[]{:S(2)}) %copy-start.6) | copy-done | bytes 786456
  29.5 0.7 %collective-permute-start.5 = (f32[4,32,256]{2,1,0:T(8,128)}, f32[4,32,256]{2,1,0:T(8,128)S(1)}, u32[]{:S(2)}, u32[]{:S(2)}) collective-permute-start(f32[4,32,256]{2,1,0:T(8,128)} %tie.5), channel_id=1, source_target_pairs={{0,1},{1,2},{2,3},{3,0},{4,5},{5,6},{6,7},{7,4},{8,9},{9,10},{10,1... | collective-permute-start | bytes 393224 | tf_op jit(solution)/shard_map/ppermute | solution.py:609
  30.2 0.1 stack.20.info
  30.2 0.0 collective-permute-done.1.core_ref
  30.2 0.0 copy-done.8
  30.2 0.0 copy-start
  30.3 2.3 %copy-done = bf16[4,768,768]{2,1,0:T(8,128)(2,1)S(1)} copy-done((bf16[4,768,768]{2,1,0:T(8,128)(2,1)S(1)}, bf16[4,768,768]{2,1,0:T(8,128)(2,1)}, u32[]{:S(2)}) %copy-start) | copy-done | bytes 4718616
  32.6 1.1 %copy-done.4 = f32[3,256,256]{2,1,0:T(8,128)S(1)} copy-done((f32[3,256,256]{2,1,0:T(8,128)S(1)}, f32[3,256,256]{2,1,0:T(8,128)}, u32[]{:S(2)}) %copy-start.4) | copy-done | bytes 786456
  33.7 1.1 %copy-done.7 = f32[3,256,256]{2,1,0:T(8,128)S(1)} copy-done((f32[3,256,256]{2,1,0:T(8,128)S(1)}, f32[3,256,256]{2,1,0:T(8,128)}, u32[]{:S(2)}) %copy-start.7) | copy-done | bytes 786456
  34.9 0.0 copy-start.14
  34.9 5.5 %segment.1 = (f32[3,256,256]{2,1,0:T(8,128)}, f32[3,256,128]{2,1,0:T(8,128)S(1)}) custom-call(s32[5]{0:T(128)S(1)} %stack.20.info, f32[3,256,256]{2,1,0:T(8,128)S(1)} %bitcast.18, f32[776,256]{1,0:T(8,128)S(1)} %collective-permute-done.1.core_ref, f32[3,256,256]{2,1,0:T(8,128)S(1)} %copy-done.4, f32[3,256,256]{2,1,0:T(8,128)S(1)} %copy-done.7, ...), custom_call_target="tpu_custom_call" | custom-call | flops 1024 | bytes 1024 | tf_op jit(solution)/shard_map/segment/pallas_call | solution.py:154
  40.4 0.0 copy-done.1
  40.4 0.0 copy-done.2
  40.4 0.0 copy-done.10
  40.4 0.0 copy-done.11
  40.4 0.0 copy-start.12
  40.4 1.1 %copy-done.12 = f32[3,256,256]{2,1,0:T(8,128)S(1)} copy-done((f32[3,256,256]{2,1,0:T(8,128)S(1)}, f32[3,256,256]{2,1,0:T(8,128)}, u32[]{:S(2)}) %copy-start.12) | copy-done | bytes 786456
  41.6 9.5 %combine.1 = (f32[256,2048]{1,0:T(8,128)S(1)}, f32[256,2048]{1,0:T(8,128)S(1)}) custom-call(s32[1]{0:T(128)} %bitcast.3.parity, f32[3,256,256]{2,1,0:T(8,128)S(1)} %copy-done.12, f32[3,256,128]{2,1,0:T(8,128)S(1)} %get-tuple-element.16.outer_ref, f32[256,2048]{1,0:T(8,128)S(1)} %copy-done.2, f32[8,32,2048]{2,1,0:T(8,128)S(1)} %copy-done.1, ...), custom_call_target="tpu_custom_call" | custom-call | flops 1024 | bytes 1024 | tf_op jit(solution)/shard_map/combine/pallas_call | solution.py:288
  51.1 0.0 collective-permute-done.7.refs_0_
  51.1 0.0 collective-permute-done.8.refs_1_
  51.1 2.7 %finish.2.refs_2_ = f32[8,32,2048]{2,1,0:T(8,128)} custom-call(f32[8,32,2048]{2,1,0:T(8,128)S(1)} %bitcast.12, f32[8,32,2048]{2,1,0:T(8,128)S(1)} %bitcast.14, f32[4,32,1792]{2,1,0:T(8,128)} %collective-permute-done.7.refs_0_, f32[4,32,1792]{2,1,0:T(8,128)} %collective-permute-done.8.refs_1_), custom_call_target="tpu_custom_call" | custom-call | flops 1024 | bytes 1024 | tf_op jit(solution)/shard_map/finish/pallas_call | solution.py:369
  53.8 0.0 collective-permute-done.6.refs_1_
  53.8 0.2 collective-permute-done.5.refs_0_
  54.0 0.8 %finish.3 = f32[8,32,2048]{2,1,0:T(8,128)} custom-call(f32[8,32,2048]{2,1,0:T(8,128)S(1)} %bitcast.13, f32[8,32,2048]{2,1,0:T(8,128)S(1)} %bitcast.15, f32[4,32,256]{2,1,0:T(8,128)S(1)} %collective-permute-done.5.refs_0_, f32[4,32,256]{2,1,0:T(8,128)S(1)} %collective-permute-done.6.refs_1_, f32[8,32,2048]{2,1,0:T(8,128)} %finish.2.refs_2_), custom_call_target="tpu_custom_call", output_to_operand_aliasing={{}: (4, {})} | custom-call | flops 1024 | bytes 1024 | tf_op jit(solution)/shard_map/finish/pallas_call | solution.py:369
  (19 shorter events, 0.1 us)
Async XLA Ops:
  0.6 20.8 %collective-permute-start = (f32[3,256,256]{2,1,0:T(8,128)}, f32[3,256,256]{2,1,0:T(8,128)S(1)}, u32[]{:S(2)}, u32[]{:S(2)}) collective-permute-start(f32[3,256,256]{2,1,0:T(8,128)} %bitcast.16), channel_id=1, source_target_pairs={{0,8},{4,12},{8,0},{12,4},{1,9},{5,13},{9,1},{13,5},{2,10},{6,14},... | collective-permute-start | bytes 2359304 | tf_op jit(solution)/shard_map/ppermute | solution.py:596
  4.9 1.7 %copy-start.5 = (f32[4,32,1792]{2,1,0:T(8,128)}, f32[4,32,1792]{2,1,0:T(8,128)S(1)}, u32[]{:S(2)}) copy-start(f32[4,32,1792]{2,1,0:T(8,128)S(1)} %slab.1.gate) | copy-start | bytes 2752516
  4.9 9.3 %copy-start.15 = (f32[2048]{0:T(1024)S(1)}, f32[2048]{0:T(1024)}, u32[]{:S(2)}) copy-start(f32[2048]{0:T(1024)} %param.9) | copy-start | bytes 24580
  4.9 9.3 %copy-start.16 = (s32[2048]{0:T(1024)S(1)}, s32[2048]{0:T(1024)}, u32[]{:S(2)}) copy-start(s32[2048]{0:T(1024)} %param.8) | copy-start | bytes 24580
  4.9 46.2 %collective-permute-start.7 = (f32[4,32,1792]{2,1,0:T(8,128)S(1)}, f32[4,32,1792]{2,1,0:T(8,128)}, u32[]{:S(2)}, u32[]{:S(2)}) collective-permute-start(f32[4,32,1792]{2,1,0:T(8,128)S(1)} %slab.1.gate), channel_id=1, source_target_pairs={{0,1},{1,2},{2,3},{3,0},{4,5},{5,6},{6,7},{7,4},{8,9},{9,10},{10,1... | collective-permute-start | bytes 2752520 | tf_op jit(solution)/shard_map/ppermute | solution.py:599
  9.6 12.7 %collective-permute-start.2 = (f32[8,256]{1,0:T(8,128)}, f32[8,256]{1,0:T(8,128)S(1)}, u32[]{:S(2)}, u32[]{:S(2)}) collective-permute-start(f32[8,256]{1,0:T(8,128)} %get-tuple-element.13), channel_id=1, source_target_pairs={{0,12},{4,8},{8,4},{12,0},{1,13},{5,9},{9,5},{13,1},{2,14},{6,10},... | collective-permute-start | bytes 24584 | tf_op jit(solution)/shard_map/ppermute | solution.py:603
  9.7 14.7 %collective-permute-start.3 = (f32[8,8,2048]{2,1,0:T(8,128)}, f32[8,8,2048]{2,1,0:T(8,128)S(1)}, u32[]{:S(2)}, u32[]{:S(2)}) collective-permute-start(f32[8,8,2048]{2,1,0:T(8,128)} %get-tuple-element.14), channel_id=1, source_target_pairs={{0,16},{16,0},{1,17},{17,1},{2,18},{18,2},{3,19},{19,3},{4,20},{20... | collective-permute-start | bytes 1572872 | tf_op jit(solution)/shard_map/ppermute | solution.py:605
  11.3 39.8 %collective-permute-start.8 = (f32[4,32,1792]{2,1,0:T(8,128)}, f32[4,32,1792]{2,1,0:T(8,128)}, u32[]{:S(2)}, u32[]{:S(2)}) collective-permute-start(f32[4,32,1792]{2,1,0:T(8,128)} %get-tuple-element.21), channel_id=1, source_target_pairs={{0,3},{1,0},{2,1},{3,2},{4,7},{5,4},{6,5},{7,6},{8,11},{9,8},{10,9... | collective-permute-start | bytes 2752520 | tf_op jit(solution)/shard_map/ppermute | solution.py:601
  21.5 0.9 %copy-start.3 = (f32[3,256,256]{2,1,0:T(8,128)}, f32[3,256,256]{2,1,0:T(8,128)S(1)}, u32[]{:S(2)}) copy-start(f32[3,256,256]{2,1,0:T(8,128)S(1)} %collective-permute-done.refs_1_.refs_0_) | copy-start | bytes 2359300
  22.4 7.9 %copy-start.8 = (f32[3,256,8,32]{1,3,2,0:T(8,128)S(1)}, f32[3,256,8,32]{1,3,2,0:T(8,128)}, u32[]{:S(2)}) copy-start(f32[3,256,8,32]{1,3,2,0:T(8,128)} %param.6) | copy-start | bytes 2359300
  22.4 2.0 %copy-start.13 = (f32[8,256]{1,0:T(8,128)}, f32[8,256]{1,0:T(8,128)S(1)}, u32[]{:S(2)}) copy-start(f32[8,256]{1,0:T(8,128)S(1)} %collective-permute-done.2.refs_1_.far_ref) | copy-start | bytes 24580
  24.4 0.8 %copy-start.9 = (f32[8,8,2048]{2,1,0:T(8,128)}, f32[8,8,2048]{2,1,0:T(8,128)S(1)}, u32[]{:S(2)}) copy-start(f32[8,8,2048]{2,1,0:T(8,128)S(1)} %collective-permute-done.3.refs_3_.rows_ref) | copy-start | bytes 1572868
  25.2 3.4 %collective-permute-start.4 = (f32[3,256,256]{2,1,0:T(8,128)}, f32[3,256,256]{2,1,0:T(8,128)S(1)}, u32[]{:S(2)}, u32[]{:S(2)}) collective-permute-start(f32[3,256,256]{2,1,0:T(8,128)} %tie.4.chip_ref), channel_id=1, source_target_pairs={{0,4},{4,0},{8,12},{12,8},{1,5},{5,1},{9,13},{13,9},{2,6},{6,2},{1... | collective-permute-start | bytes 2359304 | tf_op jit(solution)/shard_map/ppermute | solution.py:608
  25.2 5.1 %collective-permute-start.1 = (f32[776,256]{1,0:T(8,128)}, f32[776,256]{1,0:T(8,128)S(1)}, u32[]{:S(2)}, u32[]{:S(2)}) collective-permute-start(f32[776,256]{1,0:T(8,128)} %tie.3), channel_id=1, source_target_pairs={{0,4},{4,0},{8,12},{12,8},{1,5},{5,1},{9,13},{13,9},{2,6},{6,2},{1... | collective-permute-start | bytes 2383880 | tf_op jit(solution)/shard_map/ppermute | solution.py:606
  25.7 28.1 %collective-permute-start.6 = (f32[4,32,256]{2,1,0:T(8,128)}, f32[4,32,256]{2,1,0:T(8,128)S(1)}, u32[]{:S(2)}, u32[]{:S(2)}) collective-permute-start(f32[4,32,256]{2,1,0:T(8,128)} %get-tuple-element.20), channel_id=1, source_target_pairs={{0,3},{1,0},{2,1},{3,2},{4,7},{5,4},{6,5},{7,6},{8,11},{9,8},{10,9... | collective-permute-start | bytes 393224 | tf_op jit(solution)/shard_map/ppermute | solution.py:602
  28.6 0.9 %copy-start.6 = (f32[3,256,256]{2,1,0:T(8,128)}, f32[3,256,256]{2,1,0:T(8,128)S(1)}, u32[]{:S(2)}) copy-start(f32[3,256,256]{2,1,0:T(8,128)S(1)} %collective-permute-done.4.far_ref.refs_1_) | copy-start | bytes 2359300
  29.5 24.5 %collective-permute-start.5 = (f32[4,32,256]{2,1,0:T(8,128)}, f32[4,32,256]{2,1,0:T(8,128)S(1)}, u32[]{:S(2)}, u32[]{:S(2)}) collective-permute-start(f32[4,32,256]{2,1,0:T(8,128)} %tie.5), channel_id=1, source_target_pairs={{0,1},{1,2},{2,3},{3,0},{4,5},{5,6},{6,7},{7,4},{8,9},{9,10},{10,1... | collective-permute-start | bytes 393224 | tf_op jit(solution)/shard_map/ppermute | solution.py:609
  30.2 2.3 %copy-start = (bf16[4,768,768]{2,1,0:T(8,128)(2,1)S(1)}, bf16[4,768,768]{2,1,0:T(8,128)(2,1)}, u32[]{:S(2)}) copy-start(bf16[4,768,768]{2,1,0:T(8,128)(2,1)} %constant.129.clone.refs_0_.refs_1_.refs_2_.refs_3_) | copy-start | bytes 14155780
  32.6 1.1 %copy-start.4 = (f32[3,256,256]{2,1,0:T(8,128)S(1)}, f32[3,256,256]{2,1,0:T(8,128)}, u32[]{:S(2)}) copy-start(f32[3,256,256]{2,1,0:T(8,128)} %tie.4.chip_ref) | copy-start | bytes 2359300
  33.7 1.1 %copy-start.7 = (f32[3,256,256]{2,1,0:T(8,128)S(1)}, f32[3,256,256]{2,1,0:T(8,128)}, u32[]{:S(2)}) copy-start(f32[3,256,256]{2,1,0:T(8,128)} %copy-done.6) | copy-start | bytes 2359300
  34.9 5.6 %copy-start.1 = (f32[8,32,2048]{2,1,0:T(8,128)S(1)}, f32[8,32,2048]{2,1,0:T(8,128)}, u32[]{:S(2)}) copy-start(f32[8,32,2048]{2,1,0:T(8,128)} %right_ref.1) | copy-start | bytes 6291460
  34.9 5.6 %copy-start.2 = (f32[256,2048]{1,0:T(8,128)S(1)}, f32[256,2048]{1,0:T(8,128)}, u32[]{:S(2)}) copy-start(f32[256,2048]{1,0:T(8,128)} %select_select_fusion.refs_2_.matrix_ref) | copy-start | bytes 6291460
  34.9 5.6 %copy-start.10 = (f32[8,8,2048]{2,1,0:T(8,128)S(1)}, f32[8,8,2048]{2,1,0:T(8,128)}, u32[]{:S(2)}) copy-start(f32[8,8,2048]{2,1,0:T(8,128)} %copy-done.9) | copy-start | bytes 1572868
  34.9 5.6 %copy-start.11 = (bf16[768,960]{1,0:T(8,128)(2,1)S(1)}, bf16[768,960]{1,0:T(8,128)(2,1)}, u32[]{:S(2)}) copy-start(bf16[768,960]{1,0:T(8,128)(2,1)} %constant.130.clone.table_ref) | copy-start | bytes 4423684
  34.9 5.6 %copy-start.14 = (f32[8,256]{1,0:T(8,128)S(1)}, f32[8,256]{1,0:T(8,128)}, u32[]{:S(2)}) copy-start(f32[8,256]{1,0:T(8,128)} %copy-done.13) | copy-start | bytes 24580
  40.4 1.1 %copy-start.12 = (f32[3,256,256]{2,1,0:T(8,128)S(1)}, f32[3,256,256]{2,1,0:T(8,128)}, u32[]{:S(2)}) copy-start(f32[3,256,256]{2,1,0:T(8,128)} %get-tuple-element.15.main_ref) | copy-start | bytes 2359300

commit v8 on v7

--- a/solution.py
+++ b/solution.py
@@ -606,7 +606,7 @@
     core = lax.ppermute(tie(own, chip), "blk", exclusive("blk", 1))
     chip = tie(chip, far_ends, matrix, outer_rows)
     diagonal = lax.ppermute(chip, "blk", exclusive("blk", 1))
-    late_lower = lax.ppermute(tie(late_up, diagonal), "dep", ring("dep", 1))
+    late_lower = lax.ppermute(tie(late_up, chip), "dep", ring("dep", 1))
     info = jnp.stack([(block - (block ^ j)) % count for j in range(4)] + [block % 2]).astype(jnp.int32)
     main, outer = segment_call(rows_of_x, core, chip, diagonal, info, length)
     part, vertical = combine_call(main, outer, matrix, scalar, outer_rows, core, far_ends, info[4:])

time: 55.1 us -> 55.1 us (level)
  local copies, waits for them, and re-layouts: 8.42 us -> 6.39 us
  waiting for transfers between devices: 6.81 us -> 8.82 us
    unnamed x34 -> x30, local copies, waits for them, and re-layouts: 8.34 us -> 6.3 us
    ppermute x1, waiting for transfers between devices: 0.17 us -> 1.5 us  [per_device(): late_lower = lax.ppermute(tie(late_up, chip), 'dep', ring('dep', 1))]
    ppermute x1, waiting for transfers between devices: 0.01 us -> 0.69 us  [per_device(): late_upper = lax.ppermute(late_down, 'dep', ring('dep', -1))]
  transfers between devices with their start and end apart: 9 -> 9, of which waited for: 3 -> 4; matrix products, arithmetic and copies ran while one was open for 5% -> 5% of each run, Pallas kernels for 40% -> 40%
where the time goes in v8:
time: 55.1 us; the launch traced here: 54.8 us
  Pallas kernels  22.8 us (41%)
  starting transfers between devices  13.2 us (24%)
  waiting for transfers between devices  8.82 us (16%)
  local copies, waits for them, and re-layouts  6.39 us (12%)
  other arithmetic  2.68 us (5%)
  between operations  0.8 us (1%)
    pallas_call x1, Pallas kernels, combine_call(): pl.pallas_call(functools.partial(combine_kernel, cells // lanes), grid_sp...  9.49 us
    unnamed x30, local copies, waits for them, and re-layouts  6.3 us
    pallas_call x1, Pallas kernels, segment_call(): pl.pallas_call(functools.partial(segment_kernel, length), grid_spec=pltpu...  5.53 us
    ppermute x1, waiting for transfers between devices, per_device(): chip = lax.ppermute(rows_of_x, 'blk', exclusive('blk', 2))  4.56 us
    pallas_call x2, Pallas kernels, finish_call(): pl.pallas_call(functools.partial(finish_kernel, parts, aliased, aliased),...  3.47 us
    pallas_call x1, Pallas kernels, depart_call(): pl.pallas_call(depart_kernel, in_specs=[anywhere] * 3, out_specs=[anywher...  3.13 us
    ppermute x1, starting transfers between devices, per_device(): chip = lax.ppermute(rows_of_x, 'blk', exclusive('blk', 2))  3 us
    ppermute x1, starting transfers between devices, per_device(): upper = lax.ppermute(down, 'dep', ring('dep', -1))  2.86 us
  transfers between devices with their start and end apart: 9, of which 4 were waited for; matrix products, arithmetic and copies ran while one was open for 5% of the time, Pallas kernels for 40%

profile of v8, /device:TPU:0, one launch (start us, length us, event | category | flops | bytes accessed | tf_op | source)
XLA Modules:
  0.0 54.8 jit_solution(9656941617825023288)
XLA Ops:
  0.6 3.0 %collective-permute-start = (f32[3,256,256]{2,1,0:T(8,128)}, f32[3,256,256]{2,1,0:T(8,128)S(1)}, u32[]{:S(2)}, u32[]{:S(2)}) collective-permute-start(f32[3,256,256]{2,1,0:T(8,128)} %bitcast.16), channel_id=1, source_target_pairs={{0,8},{4,12},{8,0},{12,4},{1,9},{5,13},{9,1},{13,5},{2,10},{6,14},... | collective-permute-start | bytes 2359304 | tf_op jit(solution)/shard_map/ppermute | solution.py:596
  3.6 1.2 %slab.1.gate = f32[4,32,1792]{2,1,0:T(8,128)S(1)} custom-call(f32[8,32,2048]{2,1,0:T(8,128)} %right_ref.1), custom_call_target="tpu_custom_call" | custom-call | flops 1024 | bytes 1024 | tf_op jit(solution)/shard_map/slab/pallas_call | solution.py:427
  4.9 0.0 copy-start.5
  4.9 0.0 copy-start.13
  4.9 0.0 copy-start.14
  4.9 1.6 %collective-permute-start.7 = (f32[4,32,1792]{2,1,0:T(8,128)S(1)}, f32[4,32,1792]{2,1,0:T(8,128)}, u32[]{:S(2)}, u32[]{:S(2)}) collective-permute-start(f32[4,32,1792]{2,1,0:T(8,128)S(1)} %slab.1.gate), channel_id=1, source_target_pairs={{0,1},{1,2},{2,3},{3,0},{4,5},{5,6},{6,7},{7,4},{8,9},{9,10},{10,1... | collective-permute-start | bytes 2752520 | tf_op jit(solution)/shard_map/ppermute | solution.py:599
  6.5 0.0 copy-done.5
  6.5 3.1 %depart.1 = (f32[4,32,1792]{2,1,0:T(8,128)}, f32[4,32,256]{2,1,0:T(8,128)}, f32[4,32,256]{2,1,0:T(8,128)}, f32[8,8,2048]{2,1,0:T(8,128)}, f32[776,256]{1,0:T(8,128)}, /*index=5*/f32[8,256]{1,0:T(8,128)}) custom-call(f32[3,256,256]{2,1,0:T(8,128)} %bitcast.17, f32[8,32,2048]{2,1,0:T(8,128)} %right_ref.1, f32[4,32,1792]{2,1,0:T(8,128)} %copy-done.5), custom_call_target="tpu_custom_call" | custom-call | flops 1024 | bytes 1024 | tf_op jit(solution)/shard_map/depart/pallas_call | solution.py:487
  9.7 0.1 collective-permute-start.2
  9.8 1.6 %collective-permute-start.3 = (f32[8,8,2048]{2,1,0:T(8,128)}, f32[8,8,2048]{2,1,0:T(8,128)S(1)}, u32[]{:S(2)}, u32[]{:S(2)}) collective-permute-start(f32[8,8,2048]{2,1,0:T(8,128)} %get-tuple-element.14), channel_id=1, source_target_pairs={{0,16},{16,0},{1,17},{17,1},{2,18},{18,2},{3,19},{19,3},{4,20},{20... | collective-permute-start | bytes 1572872 | tf_op jit(solution)/shard_map/ppermute | solution.py:605
  11.3 2.9 %collective-permute-start.8 = (f32[4,32,1792]{2,1,0:T(8,128)}, f32[4,32,1792]{2,1,0:T(8,128)}, u32[]{:S(2)}, u32[]{:S(2)}) collective-permute-start(f32[4,32,1792]{2,1,0:T(8,128)} %get-tuple-element.21), channel_id=1, source_target_pairs={{0,3},{1,0},{2,1},{3,2},{4,7},{5,4},{6,5},{7,6},{8,11},{9,8},{10,9... | collective-permute-start | bytes 2752520 | tf_op jit(solution)/shard_map/ppermute | solution.py:601
  14.2 0.0 copy-done.13
  14.2 0.0 copy-done.14
  14.3 2.6 %select_select_fusion.refs_2_.matrix_ref = f32[256,2048]{1,0:T(8,128)} fusion(f32[2048]{0:T(1024)S(1)} %get-tuple-element.24, f32[2048]{0:T(1024)S(1)} %get-tuple-element.23, f32[2048]{0:T(1024)S(1)} %get-tuple-element.25, f32[2048]{0:T(1024)S(1)} %get-tuple-element.22, s32[2048]{0:T(1024)S(1)} %get-tuple-element.27, s32[2048]{0:T(1024)S(1)} %get-tuple-element.26, ...), kind=kLoop, calls=%fused_computation.10 | loop fusion | flops 8388608 | bytes 2154752 | tf_op jit(solution)/shard_map/jit(_where)/select_n | solution.py:194
  16.9 4.6 %collective-permute-done.refs_1_.refs_0_ = f32[3,256,256]{2,1,0:T(8,128)S(1)} collective-permute-done((f32[3,256,256]{2,1,0:T(8,128)}, f32[3,256,256]{2,1,0:T(8,128)S(1)}, u32[]{:S(2)}, u32[]{:S(2)}) %collective-permute-start) | collective-permute-done | bytes 786464 | tf_op jit(solution)/shard_map/ppermute | solution.py:596
  21.5 0.0 copy-start.3
  21.5 0.9 %copy-done.3 = f32[3,256,256]{2,1,0:T(8,128)} copy-done((f32[3,256,256]{2,1,0:T(8,128)}, f32[3,256,256]{2,1,0:T(8,128)S(1)}, u32[]{:S(2)}) %copy-start.3) | copy-done | bytes 786456
  22.4 0.0 collective-permute-done.2.refs_1_.far_ref
  22.4 2.1 %collective-permute-done.3.refs_3_.rows_ref = f32[8,8,2048]{2,1,0:T(8,128)S(1)} collective-permute-done((f32[8,8,2048]{2,1,0:T(8,128)}, f32[8,8,2048]{2,1,0:T(8,128)S(1)}, u32[]{:S(2)}, u32[]{:S(2)}) %collective-permute-start.3) | collective-permute-done | bytes 524320 | tf_op jit(solution)/shard_map/ppermute | solution.py:605
  24.4 0.0 copy-done.11
  24.4 0.8 %copy-done.7 = f32[8,8,2048]{2,1,0:T(8,128)} copy-done((f32[8,8,2048]{2,1,0:T(8,128)}, f32[8,8,2048]{2,1,0:T(8,128)S(1)}, u32[]{:S(2)}) %copy-start.7) | copy-done | bytes 524312
  25.2 0.0 collective-permute-start.4
  25.2 0.5 collective-permute-start.1
  25.7 2.9 %collective-permute-start.6 = (f32[4,32,256]{2,1,0:T(8,128)}, f32[4,32,256]{2,1,0:T(8,128)S(1)}, u32[]{:S(2)}, u32[]{:S(2)}) collective-permute-start(f32[4,32,256]{2,1,0:T(8,128)} %get-tuple-element.20), channel_id=1, source_target_pairs={{0,3},{1,0},{2,1},{3,2},{4,7},{5,4},{6,5},{7,6},{8,11},{9,8},{10,9... | collective-permute-start | bytes 393224 | tf_op jit(solution)/shard_map/ppermute | solution.py:602
  28.6 0.0 collective-permute-done.4.far_ref
  28.6 0.7 %collective-permute-start.5 = (f32[4,32,256]{2,1,0:T(8,128)}, f32[4,32,256]{2,1,0:T(8,128)S(1)}, u32[]{:S(2)}, u32[]{:S(2)}) collective-permute-start(f32[4,32,256]{2,1,0:T(8,128)} %tie.5), channel_id=1, source_target_pairs={{0,1},{1,2},{2,3},{3,0},{4,5},{5,6},{6,7},{7,4},{8,9},{9,10},{10,1... | collective-permute-start | bytes 393224 | tf_op jit(solution)/shard_map/ppermute | solution.py:609
  29.3 0.1 stack.20.info
  29.4 0.0 collective-permute-done.1.core_ref
  29.4 0.0 copy-done.6
  29.4 0.0 copy-start
  29.4 2.3 %copy-done = bf16[4,768,768]{2,1,0:T(8,128)(2,1)S(1)} copy-done((bf16[4,768,768]{2,1,0:T(8,128)(2,1)S(1)}, bf16[4,768,768]{2,1,0:T(8,128)(2,1)}, u32[]{:S(2)}) %copy-start) | copy-done | bytes 4718616
  31.7 1.1 %copy-done.4 = f32[3,256,256]{2,1,0:T(8,128)S(1)} copy-done((f32[3,256,256]{2,1,0:T(8,128)S(1)}, f32[3,256,256]{2,1,0:T(8,128)}, u32[]{:S(2)}) %copy-start.4) | copy-done | bytes 786456
  32.9 0.0 copy-start.12
  32.9 5.5 %segment.1 = (f32[3,256,256]{2,1,0:T(8,128)}, f32[3,256,128]{2,1,0:T(8,128)S(1)}) custom-call(s32[5]{0:T(128)S(1)} %stack.20.info, f32[3,256,256]{2,1,0:T(8,128)S(1)} %bitcast.18, f32[776,256]{1,0:T(8,128)S(1)} %collective-permute-done.1.core_ref, f32[3,256,256]{2,1,0:T(8,128)S(1)} %copy-done.4, f32[3,256,256]{2,1,0:T(8,128)S(1)} %collective-permute-done.4.far_ref, ...), custom_call_target="tpu_custom_call" | custom-call | flops 1024 | bytes 1024 | tf_op jit(solution)/shard_map/segment/pallas_call | solution.py:154
  38.4 0.0 copy-done.1
  38.4 0.0 copy-done.2
  38.4 0.0 copy-done.8
  38.4 0.0 copy-done.9
  38.4 0.0 copy-done.12
  38.4 0.0 copy-start.10
  38.4 1.1 %copy-done.10 = f32[3,256,256]{2,1,0:T(8,128)S(1)} copy-done((f32[3,256,256]{2,1,0:T(8,128)S(1)}, f32[3,256,256]{2,1,0:T(8,128)}, u32[]{:S(2)}) %copy-start.10) | copy-done | bytes 786456
  39.6 9.5 %combine.1 = (f32[256,2048]{1,0:T(8,128)S(1)}, f32[256,2048]{1,0:T(8,128)S(1)}) custom-call(s32[1]{0:T(128)} %bitcast.3.parity, f32[3,256,256]{2,1,0:T(8,128)S(1)} %copy-done.10, f32[3,256,128]{2,1,0:T(8,128)S(1)} %get-tuple-element.16.outer_ref, f32[256,2048]{1,0:T(8,128)S(1)} %copy-done.2, f32[8,32,2048]{2,1,0:T(8,128)S(1)} %copy-done.1, ...), custom_call_target="tpu_custom_call" | custom-call | flops 1024 | bytes 1024 | tf_op jit(solution)/shard_map/combine/pallas_call | solution.py:288
  49.1 0.0 collective-permute-done.7.refs_0_
  49.1 0.0 collective-permute-done.8.refs_1_
  49.1 2.7 %finish.2.refs_2_ = f32[8,32,2048]{2,1,0:T(8,128)} custom-call(f32[8,32,2048]{2,1,0:T(8,128)S(1)} %bitcast.12, f32[8,32,2048]{2,1,0:T(8,128)S(1)} %bitcast.14, f32[4,32,1792]{2,1,0:T(8,128)} %collective-permute-done.7.refs_0_, f32[4,32,1792]{2,1,0:T(8,128)} %collective-permute-done.8.refs_1_), custom_call_target="tpu_custom_call" | custom-call | flops 1024 | bytes 1024 | tf_op jit(solution)/shard_map/finish/pallas_call | solution.py:369
  51.8 0.7 %collective-permute-done.6.refs_1_ = f32[4,32,256]{2,1,0:T(8,128)S(1)} collective-permute-done((f32[4,32,256]{2,1,0:T(8,128)}, f32[4,32,256]{2,1,0:T(8,128)S(1)}, u32[]{:S(2)}, u32[]{:S(2)}) %collective-permute-start.6) | collective-permute-done | bytes 131104 | tf_op jit(solution)/shard_map/ppermute | solution.py:602
  52.5 1.5 %collective-permute-done.5.refs_0_ = f32[4,32,256]{2,1,0:T(8,128)S(1)} collective-permute-done((f32[4,32,256]{2,1,0:T(8,128)}, f32[4,32,256]{2,1,0:T(8,128)S(1)}, u32[]{:S(2)}, u32[]{:S(2)}) %collective-permute-start.5) | collective-permute-done | bytes 131104 | tf_op jit(solution)/shard_map/ppermute | solution.py:609
  54.0 0.8 %finish.3 = f32[8,32,2048]{2,1,0:T(8,128)} custom-call(f32[8,32,2048]{2,1,0:T(8,128)S(1)} %bitcast.13, f32[8,32,2048]{2,1,0:T(8,128)S(1)} %bitcast.15, f32[4,32,256]{2,1,0:T(8,128)S(1)} %collective-permute-done.5.refs_0_, f32[4,32,256]{2,1,0:T(8,128)S(1)} %collective-permute-done.6.refs_1_, f32[8,32,2048]{2,1,0:T(8,128)} %finish.2.refs_2_), custom_call_target="tpu_custom_call", output_to_operand_aliasing={{}: (4, {})} | custom-call | flops 1024 | bytes 1024 | tf_op jit(solution)/shard_map/finish/pallas_call | solution.py:369
  (15 shorter events, 0.1 us)
Async XLA Ops:
  0.6 20.8 %collective-permute-start = (f32[3,256,256]{2,1,0:T(8,128)}, f32[3,256,256]{2,1,0:T(8,128)S(1)}, u32[]{:S(2)}, u32[]{:S(2)}) collective-permute-start(f32[3,256,256]{2,1,0:T(8,128)} %bitcast.16), channel_id=1, source_target_pairs={{0,8},{4,12},{8,0},{12,4},{1,9},{5,13},{9,1},{13,5},{2,10},{6,14},... | collective-permute-start | bytes 2359304 | tf_op jit(solution)/shard_map/ppermute | solution.py:596
  4.9 1.7 %copy-start.5 = (f32[4,32,1792]{2,1,0:T(8,128)}, f32[4,32,1792]{2,1,0:T(8,128)S(1)}, u32[]{:S(2)}) copy-start(f32[4,32,1792]{2,1,0:T(8,128)S(1)} %slab.1.gate) | copy-start | bytes 2752516
  4.9 9.3 %copy-start.13 = (f32[2048]{0:T(1024)S(1)}, f32[2048]{0:T(1024)}, u32[]{:S(2)}) copy-start(f32[2048]{0:T(1024)} %param.9) | copy-start | bytes 24580
  4.9 9.3 %copy-start.14 = (s32[2048]{0:T(1024)S(1)}, s32[2048]{0:T(1024)}, u32[]{:S(2)}) copy-start(s32[2048]{0:T(1024)} %param.8) | copy-start | bytes 24580
  4.9 44.2 %collective-permute-start.7 = (f32[4,32,1792]{2,1,0:T(8,128)S(1)}, f32[4,32,1792]{2,1,0:T(8,128)}, u32[]{:S(2)}, u32[]{:S(2)}) collective-permute-start(f32[4,32,1792]{2,1,0:T(8,128)S(1)} %slab.1.gate), channel_id=1, source_target_pairs={{0,1},{1,2},{2,3},{3,0},{4,5},{5,6},{6,7},{7,4},{8,9},{9,10},{10,1... | collective-permute-start | bytes 2752520 | tf_op jit(solution)/shard_map/ppermute | solution.py:599
  9.7 12.7 %collective-permute-start.2 = (f32[8,256]{1,0:T(8,128)}, f32[8,256]{1,0:T(8,128)S(1)}, u32[]{:S(2)}, u32[]{:S(2)}) collective-permute-start(f32[8,256]{1,0:T(8,128)} %get-tuple-element.13), channel_id=1, source_target_pairs={{0,12},{4,8},{8,4},{12,0},{1,13},{5,9},{9,5},{13,1},{2,14},{6,10},... | collective-permute-start | bytes 24584 | tf_op jit(solution)/shard_map/ppermute | solution.py:603
  9.8 14.7 %collective-permute-start.3 = (f32[8,8,2048]{2,1,0:T(8,128)}, f32[8,8,2048]{2,1,0:T(8,128)S(1)}, u32[]{:S(2)}, u32[]{:S(2)}) collective-permute-start(f32[8,8,2048]{2,1,0:T(8,128)} %get-tuple-element.14), channel_id=1, source_target_pairs={{0,16},{16,0},{1,17},{17,1},{2,18},{18,2},{3,19},{19,3},{4,20},{20... | collective-permute-start | bytes 1572872 | tf_op jit(solution)/shard_map/ppermute | solution.py:605
  11.3 37.7 %collective-permute-start.8 = (f32[4,32,1792]{2,1,0:T(8,128)}, f32[4,32,1792]{2,1,0:T(8,128)}, u32[]{:S(2)}, u32[]{:S(2)}) collective-permute-start(f32[4,32,1792]{2,1,0:T(8,128)} %get-tuple-element.21), channel_id=1, source_target_pairs={{0,3},{1,0},{2,1},{3,2},{4,7},{5,4},{6,5},{7,6},{8,11},{9,8},{10,9... | collective-permute-start | bytes 2752520 | tf_op jit(solution)/shard_map/ppermute | solution.py:601
  21.5 0.9 %copy-start.3 = (f32[3,256,256]{2,1,0:T(8,128)}, f32[3,256,256]{2,1,0:T(8,128)S(1)}, u32[]{:S(2)}) copy-start(f32[3,256,256]{2,1,0:T(8,128)S(1)} %collective-permute-done.refs_1_.refs_0_) | copy-start | bytes 2359300
  22.4 7.0 %copy-start.6 = (f32[3,256,8,32]{1,3,2,0:T(8,128)S(1)}, f32[3,256,8,32]{1,3,2,0:T(8,128)}, u32[]{:S(2)}) copy-start(f32[3,256,8,32]{1,3,2,0:T(8,128)} %param.6) | copy-start | bytes 2359300
  22.4 2.1 %copy-start.11 = (f32[8,256]{1,0:T(8,128)}, f32[8,256]{1,0:T(8,128)S(1)}, u32[]{:S(2)}) copy-start(f32[8,256]{1,0:T(8,128)S(1)} %collective-permute-done.2.refs_1_.far_ref) | copy-start | bytes 24580
  24.4 0.8 %copy-start.7 = (f32[8,8,2048]{2,1,0:T(8,128)}, f32[8,8,2048]{2,1,0:T(8,128)S(1)}, u32[]{:S(2)}) copy-start(f32[8,8,2048]{2,1,0:T(8,128)S(1)} %collective-permute-done.3.refs_3_.rows_ref) | copy-start | bytes 1572868
  25.2 3.4 %collective-permute-start.4 = (f32[3,256,256]{2,1,0:T(8,128)}, f32[3,256,256]{2,1,0:T(8,128)S(1)}, u32[]{:S(2)}, u32[]{:S(2)}) collective-permute-start(f32[3,256,256]{2,1,0:T(8,128)} %tie.4.chip_ref.refs_1_), channel_id=1, source_target_pairs={{0,4},{4,0},{8,12},{12,8},{1,5},{5,1},{9,13},{13,9},{2,6},{6,2},{1... | collective-permute-start | bytes 2359304 | tf_op jit(solution)/shard_map/ppermute | solution.py:608
  25.2 4.2 %collective-permute-start.1 = (f32[776,256]{1,0:T(8,128)}, f32[776,256]{1,0:T(8,128)S(1)}, u32[]{:S(2)}, u32[]{:S(2)}) collective-permute-start(f32[776,256]{1,0:T(8,128)} %tie.3), channel_id=1, source_target_pairs={{0,4},{4,0},{8,12},{12,8},{1,5},{5,1},{9,13},{13,9},{2,6},{6,2},{1... | collective-permute-start | bytes 2383880 | tf_op jit(solution)/shard_map/ppermute | solution.py:606
  25.7 26.7 %collective-permute-start.6 = (f32[4,32,256]{2,1,0:T(8,128)}, f32[4,32,256]{2,1,0:T(8,128)S(1)}, u32[]{:S(2)}, u32[]{:S(2)}) collective-permute-start(f32[4,32,256]{2,1,0:T(8,128)} %get-tuple-element.20), channel_id=1, source_target_pairs={{0,3},{1,0},{2,1},{3,2},{4,7},{5,4},{6,5},{7,6},{8,11},{9,8},{10,9... | collective-permute-start | bytes 393224 | tf_op jit(solution)/shard_map/ppermute | solution.py:602
  28.6 25.4 %collective-permute-start.5 = (f32[4,32,256]{2,1,0:T(8,128)}, f32[4,32,256]{2,1,0:T(8,128)S(1)}, u32[]{:S(2)}, u32[]{:S(2)}) collective-permute-start(f32[4,32,256]{2,1,0:T(8,128)} %tie.5), channel_id=1, source_target_pairs={{0,1},{1,2},{2,3},{3,0},{4,5},{5,6},{6,7},{7,4},{8,9},{9,10},{10,1... | collective-permute-start | bytes 393224 | tf_op jit(solution)/shard_map/ppermute | solution.py:609
  29.4 2.3 %copy-start = (bf16[4,768,768]{2,1,0:T(8,128)(2,1)S(1)}, bf16[4,768,768]{2,1,0:T(8,128)(2,1)}, u32[]{:S(2)}) copy-start(bf16[4,768,768]{2,1,0:T(8,128)(2,1)} %constant.129.clone.refs_0_.refs_1_.refs_2_.refs_3_) | copy-start | bytes 14155780
  31.7 1.1 %copy-start.4 = (f32[3,256,256]{2,1,0:T(8,128)S(1)}, f32[3,256,256]{2,1,0:T(8,128)}, u32[]{:S(2)}) copy-start(f32[3,256,256]{2,1,0:T(8,128)} %tie.4.chip_ref.refs_1_) | copy-start | bytes 2359300
  32.9 5.5 %copy-start.1 = (f32[8,32,2048]{2,1,0:T(8,128)S(1)}, f32[8,32,2048]{2,1,0:T(8,128)}, u32[]{:S(2)}) copy-start(f32[8,32,2048]{2,1,0:T(8,128)} %right_ref.1) | copy-start | bytes 6291460
  32.9 5.5 %copy-start.2 = (f32[256,2048]{1,0:T(8,128)S(1)}, f32[256,2048]{1,0:T(8,128)}, u32[]{:S(2)}) copy-start(f32[256,2048]{1,0:T(8,128)} %select_select_fusion.refs_2_.matrix_ref) | copy-start | bytes 6291460
  32.9 5.5 %copy-start.8 = (f32[8,8,2048]{2,1,0:T(8,128)S(1)}, f32[8,8,2048]{2,1,0:T(8,128)}, u32[]{:S(2)}) copy-start(f32[8,8,2048]{2,1,0:T(8,128)} %copy-done.7) | copy-start | bytes 1572868
  32.9 5.6 %copy-start.9 = (bf16[768,960]{1,0:T(8,128)(2,1)S(1)}, bf16[768,960]{1,0:T(8,128)(2,1)}, u32[]{:S(2)}) copy-start(bf16[768,960]{1,0:T(8,128)(2,1)} %constant.130.clone.table_ref) | copy-start | bytes 4423684
  32.9 5.6 %copy-start.12 = (f32[8,256]{1,0:T(8,128)S(1)}, f32[8,256]{1,0:T(8,128)}, u32[]{:S(2)}) copy-start(f32[8,256]{1,0:T(8,128)} %copy-done.11) | copy-start | bytes 24580
  38.4 1.1 %copy-start.10 = (f32[3,256,256]{2,1,0:T(8,128)S(1)}, f32[3,256,256]{2,1,0:T(8,128)}, u32[]{:S(2)}) copy-start(f32[3,256,256]{2,1,0:T(8,128)} %get-tuple-element.15.main_ref) | copy-start | bytes 2359300
